TPU v7x, 32 devices: a whole 2x2x4 slice. The times are simulated.
32 devices in a mesh: wide: 16 (over z, y, core), narrow: 2 (over x).
Axes of the slice: x: 2, y: 2, z: 4, core: 2. Of those that a mesh axis runs over, the one named last changes fastest.
Arguments:
- child_pattern: bfloat16 [32, 2, 32, 16384], P('wide', None, None, 'narrow'), may hold values from -4 to 4
- child_parent: int32 [32], replicated, may hold values from -1 to 3, as said below
- child_octant: int32 [32], replicated, may hold values from 0 to 7, as said below
- parent_center: float32 [4, 3], replicated, may hold values from -16 to 16
- stencil_start: int32 [65536], replicated, may hold values from -3 to 16381, as said below
Outputs:
- parent_pattern: float32 [4, 2, 32, 2, 32768], P(None, None, None, 'narrow', 'wide')
- far_field: float32 [2, 32, 2, 32768], P(None, None, 'narrow', 'wide')
Inputs may be any that keep to these rules, and one draw needn't show every extreme that they name: `child_parent`: -1 marks an empty slot; every parent is named by one to eight slots, which lie in one aligned run of 8 slots, and slot 8 p of each run is live. `child_octant`: the live slots of one parent have distinct octants. stencil_start[j] is floor(j/4) - 2 or floor(j/4) - 3.
All inputs are finite; a program needn't handle non-finite values.
Results may differ from a plain program's by a relative error of at most 0.0029.
Values may be sent and summed in bfloat16 or wider, within the bound.
No kernel may reach another device: no remote copies, remote signals or barrier semaphores. Data moves between devices by JAX's collectives and lax.ppermute only.
A program may use at most 64 MiB of HBM per device.

v0:
```python
import math

import jax
import jax.numpy as jnp
from jax import lax
from jax.sharding import PartitionSpec as P

K2 = 65536


def with_halo(cells, sides, width):
    for axis, dim in sides:
        count = lax.axis_size(axis)
        head = lax.slice_in_dim(cells, 0, width, axis=dim)
        tail = lax.slice_in_dim(cells, cells.shape[dim] - width, cells.shape[dim], axis=dim)
        cells = jnp.concatenate(
            [
                lax.ppermute(tail, axis, [(i, (i + 1) % count) for i in range(count)]),
                cells,
                lax.ppermute(head, axis, [((i + 1) % count, i) for i in range(count)]),
            ],
            axis=dim,
        )
    return cells


def lagrange_taps(starts, first_out):
    sample_count = starts.shape[0]
    sample = first_out + jnp.arange(sample_count, dtype=jnp.int32)
    excess = sample // 4 - 2 - starts
    offset_u = (sample % 4).astype(jnp.float32) * 0.25 + 2.125 + excess.astype(jnp.float32)
    basis = []
    for node in range(6):
        value = jnp.ones_like(offset_u)
        for other in range(6):
            if other != node:
                value = value * (offset_u - other) / (node - other)
        basis.append(value)
    zeros = jnp.zeros_like(offset_u)
    stacked = []
    for offset in range(7):
        lower = basis[offset - 1] if offset >= 1 else zeros
        upper = basis[offset] if offset <= 5 else zeros
        stacked.append(jnp.where(excess == 0, lower, upper))
    return jnp.stack(stacked).reshape(7, sample_count // 4, 4)


def interpolate(window, tap_weights):
    block_len = tap_weights.shape[1]
    leading = window.shape[:-1]
    flat_rows = window.reshape((-1, window.shape[-1]))
    row_count = flat_rows.shape[0]
    if block_len % 64 == 0 and block_len > 64:
        group = 64
    else:
        group = block_len
    blocks = block_len // group
    taps = tap_weights.reshape(7, blocks, 4 * group)
    if blocks == 1:
        band_rows = flat_rows.shape[1]
        paired = flat_rows[:, None, :]
    else:
        band_rows = 2 * group
        extended = jnp.pad(flat_rows, ((0, 0), (0, (blocks + 1) * group - flat_rows.shape[1])))
        split_rows = extended.reshape(row_count, blocks + 1, group)
        paired = jnp.concatenate([split_rows[:, :-1], split_rows[:, 1:]], axis=2)
    column = jnp.arange(band_rows, dtype=jnp.int32)[None, :, None]
    target = (jnp.arange(4 * group, dtype=jnp.int32) // 4)[None, None, :]
    offsets = jnp.arange(7, dtype=jnp.int32)[:, None, None]
    onehot = (column == target + offsets).astype(jnp.float32)
    band = jnp.einsum("kcj,kbj->bcj", onehot, taps, precision=lax.Precision.HIGHEST)
    total = jnp.einsum(
        "rbc,bcj->rbj", paired.astype(jnp.float32), band, precision=lax.Precision.HIGHEST
    )
    return total.reshape(leading + (4 * block_len,)).astype(jnp.bfloat16)


def directions(first_out, sample_count):
    sample = first_out + jnp.arange(sample_count, dtype=jnp.int32)
    cycles = K2 // 256
    azimuth = 2.0 * math.pi * ((sample % 256).astype(jnp.float32) + 0.5) / 256.0
    polar = math.pi * ((sample // 256).astype(jnp.float32) + 0.5) / cycles
    return (jnp.sin(polar) * jnp.cos(azimuth), jnp.sin(polar) * jnp.sin(azimuth), jnp.cos(polar))


def child_phase(octant, dir_x, dir_y, dir_z):
    sign_x = (octant % 2 * 2 - 1).astype(jnp.float32)
    sign_y = (octant // 2 % 2 * 2 - 1).astype(jnp.float32)
    sign_z = (octant // 4 * 2 - 1).astype(jnp.float32)
    return (
        2.0
        * math.pi
        * 2.0
        * (sign_x[:, None] * dir_x + sign_y[:, None] * dir_y + sign_z[:, None] * dir_z)
    )


def shift_children(pattern, octant, dir_x, dir_y, dir_z):
    angle = child_phase(octant, dir_x, dir_y, dir_z)
    cosine = jnp.cos(angle)[:, None, :]
    sine_part = jnp.sin(angle)[:, None, :]
    real_part = pattern[:, 0].astype(jnp.float32)
    imag_part = pattern[:, 1].astype(jnp.float32)
    return jnp.stack(
        [cosine * real_part - sine_part * imag_part, sine_part * real_part + cosine * imag_part],
        axis=1,
    )


def per_device(child_pattern, child_parent, child_octant, parent_center, stencil_start):
    n_wide = lax.axis_size("wide")
    box_count, _, sources, block_one = child_pattern.shape
    block_two = 4 * block_one
    piece_len = block_one // n_wide
    narrow_at = lax.axis_index("narrow")
    wide_at = lax.axis_index("wide")
    out_first = narrow_at * block_two + wide_at * (4 * piece_len)
    parent_count = parent_center.shape[0]
    parent_ids = jnp.arange(parent_count, dtype=jnp.int32)
    dir_x, dir_y, dir_z = directions(out_first, 4 * piece_len)
    padded = with_halo(child_pattern, (("narrow", 3),), 3)
    shape_pieces = (box_count, 2, sources, n_wide, piece_len)
    left_rim = padded[..., 0:block_one].reshape(shape_pieces)[..., :3]
    middle = padded[..., 3 : 3 + block_one].reshape(shape_pieces)
    right_rim = padded[..., 6 : 6 + block_one].reshape(shape_pieces)[..., piece_len - 3 :]
    windows = jnp.concatenate([left_rim, middle, right_rim], axis=-1)
    starts = lax.dynamic_slice_in_dim(stencil_start, out_first, 4 * piece_len)
    tap_weights = lagrange_taps(starts, out_first)
    gathered = interpolate(
        lax.all_to_all(windows, "wide", split_axis=3, concat_axis=0, tiled=True)[:, :, :, 0, :],
        tap_weights,
    )
    shifted = shift_children(gathered, child_octant, dir_x, dir_y, dir_z)
    selector = (child_parent[:, None] == parent_ids[None, :]).astype(jnp.float32)
    parents_total = jnp.einsum("bp,bcrj->pcrj", selector, shifted, precision=lax.Precision.HIGHEST)
    center_angle = (
        2.0
        * math.pi
        * (
            parent_center[:, 0:1] * dir_x
            + parent_center[:, 1:2] * dir_y
            + parent_center[:, 2:3] * dir_z
        )
    )
    center_cos = jnp.cos(center_angle)
    center_sin = jnp.sin(center_angle)
    real_sum = jnp.einsum(
        "pj,prj->rj", center_cos, parents_total[:, 0], precision=lax.Precision.HIGHEST
    ) - jnp.einsum("pj,prj->rj", center_sin, parents_total[:, 1], precision=lax.Precision.HIGHEST)
    imag_sum = jnp.einsum(
        "pj,prj->rj", center_sin, parents_total[:, 0], precision=lax.Precision.HIGHEST
    ) + jnp.einsum("pj,prj->rj", center_cos, parents_total[:, 1], precision=lax.Precision.HIGHEST)
    far_field = jnp.stack([real_sum, imag_sum]) / math.sqrt(parent_count)
    parent_pattern = parents_total[:, :, :, None, :]
    return (parent_pattern, far_field[:, :, None, :])


def solution(mesh):
    in_specs = (P("wide", None, None, "narrow"), P(), P(), P(), P())
    out_specs = (P(None, None, None, "narrow", "wide"), P(None, None, "narrow", "wide"))
    return jax.shard_map(
        per_device, mesh=mesh, in_specs=in_specs, out_specs=out_specs, check_vma=False
    )
```

profile of v0, /device:TPU:13, one launch (start us, length us, event | category | flops | bytes accessed | tf_op | source)
XLA Modules:
  0.0 158.4 jit_solution(15369498526530554078)
XLA Ops:
  0.6 0.0 copy-start
  0.6 1.0 fusion.80
  1.6 1.2 collective-permute-start
  2.9 0.3 collective-permute-start.1
  3.1 1.8 %copy.69 = bf16[2,2,4,16,8,512]{5,4,2,1,0,3:T(8,128)(2,1)S(1)} copy(bf16[2,2,4,16,8,512]{5,4,3,2,1,0:T(8,128)(2,1)} %bitcast.66) | data formatting | bytes 4194304 | tf_op jit(solution)/shard_map/reshape | solution.py:124
  5.0 0.0 collective-permute-done
  5.0 1.2 collective-permute-done.1
  6.1 0.0 copy-done
  6.1 1.5 pad_maximum_fusion.2
  7.6 0.9 copy.58
  8.5 0.1 slice.64
  8.6 0.1 copy.48
  8.7 0.9 copy.59
  9.6 0.2 slice.65
  9.8 0.1 copy.49
  10.0 3.3 %pad_maximum_fusion = bf16[2,2,32,16,518]{4,2,1,0,3:T(8,128)(2,1)} fusion(bf16[2,2,32,16,3]{4,2,1,0,3:T(8,128)(2,1)S(1)} %copy.49, bf16[2,2,32,16,512]{4,2,1,0,3:T(8,128)(2,1)S(1)} %bitcast.69, bf16[2,2,32,16,3]{4,2,1,0,3:T(8,128)(2,1)S(1)} %copy.48), kind=kLoop, calls=%fused_computation.14 | loop fusion | flops 6365184 | bytes 4243456 | tf_op jit(solution)/shard_map/concatenate | solution.py:126
  13.3 7.6 %all-to-all-start = ((bf16[2,2,32,16,518]{4,2,1,0,3:T(8,128)(2,1)}), bf16[2,2,32,16,518]{4,2,1,0,3:T(8,128)(2,1)S(1)}, u32[]{:S(2)}, u32[]{:S(2)}) async-start(bf16[2,2,32,16,518]{4,2,1,0,3:T(8,128)(2,1)} %pad_maximum_fusion), calls=%async_computation | async-start | bytes 5242880 | tf_op jit(solution)/shard_map/all_to_all | solution.py:130
  20.9 0.8 broadcast_select_fusion
  21.9 1.3 copy.20
  23.2 0.1 iota_compare_fusion
  23.3 0.5 copy.21
  23.8 0.0 copy-done.3
  23.8 0.2 slice_reduce_fusion.2
  24.0 0.1 sine_multiply_fusion
  24.1 0.0 copy-done.5
  24.2 3.4 %fusion.81 = f32[256,8,128]{2,1,0:T(8,128)} fusion(f32[7,8,256]{1,0,2:T(8,128)} %copy.20, pred[7,128,256]{1,0,2:T(8,128)(4,1)S(1)} %copy.21), kind=kOutput, calls=%fused_computation.153 | convolution fusion | flops 22020096 | bytes 1335296 | tf_op jit(solution)/shard_map/kcj,kbj->bcj/dot_general | solution.py:71
  27.6 0.3 cosine_bitcast_fusion
  27.9 1.8 %fusion.12 = (f32[32,2048]{1,0:T(8,128)S(1)}, f32[32,2048]{1,0:T(8,128)}) fusion(f32[2048]{0:T(1024)S(1)} %get-tuple-element.43, f32[32]{0:T(128)S(1)} %get-tuple-element.40, f32[2048]{0:T(1024)S(1)} %get-tuple-element.41, f32[32]{0:T(128)S(1)} %get-tuple-element.39, f32[2048]{0:T(1024)S(1)} %get-tuple-element.42, f32[32]{0:T(128)S(1)} %get-tuple-element.38), kind=kLoop, calls=%fused_computation.32 | loop fusion | flops 393216 | bytes 549248 | tf_op jit(solution)/shard_map/cos | solution.py:100
  29.7 49.8 %all-to-all-done = bf16[2,2,32,16,518]{4,2,1,0,3:T(8,128)(2,1)S(1)} async-done(((bf16[2,2,32,16,518]{4,2,1,0,3:T(8,128)(2,1)}), bf16[2,2,32,16,518]{4,2,1,0,3:T(8,128)(2,1)S(1)}, u32[]{:S(2)}, u32[]{:S(2)}) %all-to-all-start) | async-done | bytes 2121760 | tf_op jit(solution)/shard_map/all_to_all | solution.py:130
  79.6 2.5 %copy.56 = bf16[2048,518]{0,1:T(8,128)(2,1)} copy(bf16[2048,518]{1,0:T(8,128)(2,1)S(1)} %bitcast.65) | data formatting | bytes 4243456
  82.1 1.9 %pad.4.clone = bf16[2048,576]{0,1:T(8,128)(2,1)S(1)} pad(bf16[2048,518]{0,1:T(8,128)(2,1)} %copy.56, bf16[]{:T(256)} %constant.191.clone.1), padding=0_0x0_58 | pad | bytes 4481026 | tf_op jit(solution)/shard_map/jit(_pad)/pad | solution.py:64
  84.0 1.8 %fusion.79 = (bf16[2048,8,64]{0,2,1:T(8,128)(2,1)}, bf16[2048,8,64]{0,2,1:T(8,128)(2,1)S(1)}) fusion(bf16[2048,9,64]{0,2,1:T(8,128)(2,1)S(1)} %bitcast.64), kind=kLoop, calls=%fused_computation.151 | loop fusion | bytes 8388608 | tf_op jit(solution)/shard_map/slice | solution.py:66
  85.8 4.8 %copy.50 = bf16[2048,8,64]{2,0,1:T(8,128)(2,1)} copy(bf16[2048,8,64]{0,2,1:T(8,128)(2,1)} %get-tuple-element.22) | data formatting | bytes 4194304
  90.6 3.2 %copy.51 = bf16[2048,8,64]{2,0,1:T(8,128)(2,1)} copy(bf16[2048,8,64]{0,2,1:T(8,128)(2,1)S(1)} %get-tuple-element.23) | data formatting | bytes 4194304
  93.8 0.0 copy-done.1
  93.8 15.2 %convert_bitcast_fusion = bf16[2048,8,256]{0,2,1:T(8,128)(2,1)} fusion(bf16[2048,8,64]{2,0,1:T(8,128)(2,1)} %copy.51, bf16[2048,8,64]{2,0,1:T(8,128)(2,1)} %copy.50, f32[256,8,128]{2,1,0:T(8,128)S(1)} %copy-done.1), kind=kOutput, calls=%fused_computation.10 | convolution fusion | flops 6455033856 | bytes 13631488 | tf_op jit(solution)/shard_map/rbc,bcj->rbj/dot_general | solution.py:72
  109.0 12.6 %copy.16 = bf16[2048,8,256]{2,1,0:T(8,128)(2,1)} copy(bf16[2048,8,256]{0,2,1:T(8,128)(2,1)} %convert_bitcast_fusion) | data formatting | bytes 16777216 | tf_op jit(solution)/shard_map/convert_element_type | solution.py:75
  121.7 13.5 %convert_element_type.71 = bf16[32,2,32,2048]{3,2,1,0:T(8,128)(2,1)} reshape(bf16[2048,8,256]{2,1,0:T(8,128)(2,1)} %copy.16) | data formatting | bytes 16777216 | tf_op jit(solution)/shard_map/convert_element_type | solution.py:75
  135.2 4.3 %fusion.78 = (bf16[32,1,32,2048]{3,2,1,0:T(8,128)(2,1)S(1)}, bf16[32,1,32,2048]{3,2,1,0:T(8,128)(2,1)S(1)}) fusion(bf16[32,2,32,2048]{3,2,1,0:T(8,128)(2,1)} %convert_element_type.71), kind=kLoop, calls=%fused_computation.150 | loop fusion | bytes 16777216 | tf_op jit(solution)/shard_map/slice | solution.py:102
  139.5 0.0 copy-done.2
  139.5 0.0 copy-start.4
  139.5 4.9 %fusion.4 = (f32[32,1,32,2048]{3,0,2,1:T(8,128)S(1)}, f32[32,1,32,2048]{3,0,2,1:T(8,128)S(1)}) fusion(f32[32,2048]{1,0:T(8,128)S(1)} %copy-done.2, f32[32,2048]{1,0:T(8,128)S(1)} %get-tuple-element.30, bf16[32,1,32,2048]{3,2,1,0:T(8,128)(2,1)S(1)} %get-tuple-element.21, bf16[32,1,32,2048]{3,2,1,0:T(8,128)(2,1)S(1)} %get-tuple-element.20), kind=kLoop, calls=%fused_computation.8 | loop fusion | flops 16777216 | bytes 25690112 | tf_op jit(solution)/shard_map/sub | solution.py:105
  144.5 6.0 %fusion = f32[4,2,32,2048]{3,0,2,1:T(4,128)S(1)} fusion(f32[32,1,32,2048]{3,0,2,1:T(8,128)S(1)} %get-tuple-element.19, f32[32,1,32,2048]{3,0,2,1:T(8,128)S(1)} %get-tuple-element.18, s32[32]{0:T(128)S(1)} %copy-done.4), kind=kOutput, calls=%fused_computation | convolution fusion | flops 205521024 | bytes 18874496 | tf_op jit(solution)/shard_map/bp,bcrj->pcrj/dot_general | solution.py:135
  150.5 2.6 %multiply_reduce_fusion.2 = (f32[2048,32]{0,1:T(8,128)S(1)}, f32[2048,32]{0,1:T(8,128)S(1)}, f32[2048,32]{0,1:T(8,128)S(1)}, f32[2048,32]{0,1:T(8,128)S(1)}) fusion(f32[4,2,32,2048]{3,0,2,1:T(4,128)S(1)} %fusion, f32[2048,4]{0,1:T(4,128)S(1)} %get-tuple-element.29, f32[2048,4]{0,1:T(4,128)S(1)} %get-tuple-element.28), kind=kLoop, calls=%fused_computation.23 | loop fusion | flops 1835008 | bytes 3211264 | tf_op jit(solution)/shard_map/pj,prj->rj/dot_general | solution.py:149
  153.2 0.2 stack.47
  153.4 0.2 stack.48
  153.6 3.5 %copy.19 = f32[4,2,32,1,2048]{4,3,2,1,0:T(1,128)} copy(f32[4,2,32,1,2048]{4,0,2,1,3:T(4,128)S(1)} %bitcast.63) | data formatting | bytes 4194304
  157.0 1.3 maximum_multiply_fusion
  (25 shorter events, 0.2 us)
Async XLA Ops:
  0.6 5.5 %copy-start = (bf16[2,2,32,8192]{3,2,1,0:T(8,128)(2,1)S(1)}, bf16[2,2,32,8192]{3,2,1,0:T(8,128)(2,1)}, u32[]{:S(2)}) copy-start(bf16[2,2,32,8192]{3,2,1,0:T(8,128)(2,1)} %param.5) | copy-start | bytes 6291460
  1.6 3.3 %collective-permute-start = (bf16[2,2,32,3]{3,2,1,0:T(8,128)(2,1)S(1)}, bf16[2,2,32,3]{3,2,1,0:T(8,128)(2,1)S(1)}, u32[]{:S(2)}, u32[]{:S(2)}) collective-permute-start(bf16[2,2,32,3]{3,2,1,0:T(8,128)(2,1)S(1)} %get-tuple-element.26), channel_id=1, source_target_pairs={{0,1},{1,0},{2,3},{3,2},{4,5},{5,4},{6,7},{7,6},{8,9},{9,8},{10,11... | collective-permute-start | bytes 2312 | tf_op jit(solution)/shard_map/ppermute | solution.py:18
  2.9 3.3 %collective-permute-start.1 = (bf16[2,2,32,3]{3,2,1,0:T(8,128)(2,1)S(1)}, bf16[2,2,32,3]{3,2,1,0:T(8,128)(2,1)S(1)}, u32[]{:S(2)}, u32[]{:S(2)}) collective-permute-start(bf16[2,2,32,3]{3,2,1,0:T(8,128)(2,1)S(1)} %get-tuple-element.27), channel_id=1, source_target_pairs={{1,0},{0,1},{3,2},{2,3},{5,4},{4,5},{7,6},{6,7},{9,8},{8,9},{11,10... | collective-permute-start | bytes 2312 | tf_op jit(solution)/shard_map/ppermute | solution.py:20
  13.3 10.6 %copy-start.3 = (f32[4,3]{1,0:T(4,128)S(1)}, f32[4,3]{1,0:T(4,128)}, u32[]{:S(2)}) copy-start(f32[4,3]{1,0:T(4,128)} %param.8) | copy-start | bytes 148
  13.3 10.8 %copy-start.5 = (s32[32]{0:T(128)S(1)}, s32[32]{0:T(128)}, u32[]{:S(2)}) copy-start(s32[32]{0:T(128)} %param.7) | copy-start | bytes 388
  13.3 66.3 %all-to-all-start = ((bf16[2,2,32,16,518]{4,2,1,0,3:T(8,128)(2,1)}), bf16[2,2,32,16,518]{4,2,1,0,3:T(8,128)(2,1)S(1)}, u32[]{:S(2)}, u32[]{:S(2)}) async-start(bf16[2,2,32,16,518]{4,2,1,0,3:T(8,128)(2,1)} %pad_maximum_fusion), calls=%async_computation | async-start | bytes 5242880 | tf_op jit(solution)/shard_map/all_to_all | solution.py:130
  90.6 3.2 %copy-start.1 = (f32[256,8,128]{2,1,0:T(8,128)S(1)}, f32[256,8,128]{2,1,0:T(8,128)}, u32[]{:S(2)}) copy-start(f32[256,8,128]{2,1,0:T(8,128)} %fusion.81) | copy-start | bytes 3145732
  135.2 4.3 %copy-start.2 = (f32[32,2048]{1,0:T(8,128)S(1)}, f32[32,2048]{1,0:T(8,128)}, u32[]{:S(2)}) copy-start(f32[32,2048]{1,0:T(8,128)} %get-tuple-element.31) | copy-start | bytes 786436
  139.5 5.0 %copy-start.4 = (s32[32]{0:T(128)S(1)}, s32[32]{0:T(128)}, u32[]{:S(2)}) copy-start(s32[32]{0:T(128)} %param.6) | copy-start | bytes 388
where the time goes:
time: 159 us; the launch traced here: 158 us
  local copies, waits for them, and re-layouts  55.8 us (35%)
  waiting for transfers between devices  51 us (32%)
  matrix products  24.7 us (16%)
  other arithmetic  16.9 us (11%)
  starting transfers between devices  9.11 us (6%)
    all_to_all x1, waiting for transfers between devices, per_device(): lax.all_to_all(windows, 'wide', split_axis=3, concat_axis=0, tiled=True)  49.8 us
    convert_element_type x2, local copies, waits for them, and re-layouts, interpolate(): return total.reshape(leading + (4 * block_len,)).astype(jnp.bfloat16)  26.1 us
    unnamed x26, local copies, waits for them, and re-layouts  16.1 us
    dot_general x1, matrix products, interpolate(): jnp.einsum('rbc,bcj->rbj', paired.astype(jnp.float32), band, precision=la...  15.2 us
    all_to_all x1, starting transfers between devices, per_device(): lax.all_to_all(windows, 'wide', split_axis=3, concat_axis=0, tiled=True)  7.62 us
    dot_general x1, matrix products, per_device(): jnp.einsum('bp,bcrj->pcrj', selector, shifted, precision=lax.Precision.HI...  6.03 us
    sub x1, other arithmetic, shift_children(): cosine * real_part - sine_part * imag_part  4.95 us
    slice x1, local copies, waits for them, and re-layouts, shift_children(): real_part = pattern[:, 0].astype(jnp.float32)  4.28 us
  transfers between devices with their start and end apart: 3, of which 2 were waited for; matrix products, arithmetic and copies ran while one was open for 7% of the time, Pallas kernels for 0%

commit v1 on v0

--- a/solution.py
+++ b/solution.py
@@ -1,8 +1,13 @@
+import functools
 import math
 
 import jax
 import jax.numpy as jnp
+import ml_dtypes
+import numpy as np
 from jax import lax
+from jax.experimental import pallas as pl
+from jax.experimental.pallas import tpu as pltpu
 from jax.sharding import PartitionSpec as P
 
 K2 = 65536
@@ -107,7 +112,7 @@
     )
 
 
-def per_device(child_pattern, child_parent, child_octant, parent_center, stencil_start):
+def exchanged(child_pattern, child_parent, child_octant, parent_center, stencil_start):
     n_wide = lax.axis_size("wide")
     box_count, _, sources, block_one = child_pattern.shape
     block_two = 4 * block_one
@@ -155,6 +160,302 @@
     return (parent_pattern, far_field[:, :, None, :])
 
 
+LANES = 128
+HALO = 3
+
+
+def pick_partner(index, step):
+    return index ^ step
+
+
+def stencil_tables(window, columns):
+    tables = np.zeros((2, window, columns), np.float32)
+    for excess in range(2):
+        for column in range(columns):
+            offset_u = np.float32((column % 4) * 0.25 + 2.125 + excess)
+            first = window // 4 + column // 4 - 2 - excess
+            for node in range(6):
+                value = np.float32(1.0)
+                for other in range(6):
+                    if other != node:
+                        value = np.float32(
+                            value * np.float32(np.float32(offset_u - np.float32(other)) / np.float32(node - other))
+                        )
+                tables[excess, first + node, column] = value
+    high = tables.astype(ml_dtypes.bfloat16)
+    low = (tables - high.astype(np.float32)).astype(ml_dtypes.bfloat16)
+    return np.concatenate([high, low], axis=1)
+
+
+def pack_kernel(groups, members, piece, cells, *outs):
+    boxes, parts, sources, block = cells.shape
+    rows = boxes * parts * sources
+    tiles = piece // LANES
+    wide_at = lax.axis_index("wide")
+    group_at, member_at = wide_at // members, wide_at % members
+    slot = lax.broadcasted_iota(jnp.int32, (16, LANES), 0)
+    lane = lax.broadcasted_iota(jnp.int32, (16, LANES), 1)
+    pick_left = jnp.where((slot < HALO) & (lane == LANES - HALO + slot), 1.0, 0.0).astype(jnp.bfloat16)
+    pick_right = jnp.where((slot >= HALO) & (slot < 2 * HALO) & (lane == slot - HALO), 1.0, 0.0).astype(jnp.bfloat16)
+    across = (((1,), (1,)), ((), ()))
+
+    def tile(at):
+        return cells[:, :, :, pl.ds(pl.multiple_of(at, LANES), LANES)].reshape(rows, LANES)
+
+    for step in range(groups):
+        for swap in range(members):
+            out = outs[step * members + swap]
+            first = (pick_partner(group_at, step) * members + pick_partner(member_at, swap)) * piece
+            for index in range(tiles):
+                out[index * rows : (index + 1) * rows, :] = tile(first + index * LANES)
+            before = tile(jnp.maximum(first - LANES, 0))
+            after = tile(jnp.minimum(first + piece, block - LANES))
+            rim = lax.dot_general(pick_left, before, across, preferred_element_type=jnp.float32)
+            rim = rim + lax.dot_general(pick_right, after, across, preferred_element_type=jnp.float32)
+            out[tiles * rows : tiles * rows + 16, :] = rim.astype(jnp.bfloat16)
+    edge = outs[groups * members]
+    rim = lax.dot_general(pick_left, tile(block - LANES), across, preferred_element_type=jnp.float32)
+    rim = rim + lax.dot_general(pick_right, tile(0), across, preferred_element_type=jnp.float32)
+    edge[...] = rim.astype(jnp.bfloat16)
+
+
+def prep_kernel(groups, members, boxes, piece, parent_of, octant_of, center, starts, cosines, sines, center_cos, center_sin, excess):
+    wide_at = lax.axis_index("wide")
+    narrow_at = lax.axis_index("narrow")
+    group_at, member_at = wide_at // members, wide_at % members
+    rows = 4 * piece // LANES
+    all_rows = starts.shape[0]
+    half_rows = all_rows // lax.axis_size("narrow")
+    sample_count = all_rows * LANES
+    cycles = sample_count // 256
+    row = lax.broadcasted_iota(jnp.int32, (rows, LANES), 0)
+    lane = lax.broadcasted_iota(jnp.int32, (rows, LANES), 1)
+
+    def place(group):
+        first_row = narrow_at * half_rows + (group * members + member_at) * rows
+        sample = (first_row + row) * LANES + lane
+        azimuth = 2.0 * math.pi * ((sample & 255).astype(jnp.float32) + 0.5) / 256.0
+        polar = math.pi * ((sample >> 8).astype(jnp.float32) + 0.5) / cycles
+        sin_polar = jnp.sin(polar)
+        return first_row, sample, sin_polar * jnp.cos(azimuth), sin_polar * jnp.sin(azimuth), jnp.cos(polar)
+
+    for step in range(groups):
+        first_row, sample, dir_x, dir_y, dir_z = place(pick_partner(group_at, step))
+        here = starts[pl.ds(pl.multiple_of(first_row, 8), rows), :]
+        excess[step] = ((sample >> 2) - 2 - here).astype(jnp.float32)
+        for swap in range(members):
+            for box in range(boxes):
+                slot = (group_at * members + pick_partner(member_at, swap)) * boxes + box
+                octant = octant_of[slot]
+                live = jnp.where(parent_of[slot] >= 0, 1.0, 0.0)
+                sign_x = ((octant & 1) * 2 - 1).astype(jnp.float32)
+                sign_y = (((octant >> 1) & 1) * 2 - 1).astype(jnp.float32)
+                sign_z = ((octant >> 2) * 2 - 1).astype(jnp.float32)
+                angle = 4.0 * math.pi * (sign_x * dir_x + sign_y * dir_y + sign_z * dir_z)
+                cosines[step, swap * boxes + box] = jnp.cos(angle) * live
+                sines[step, swap * boxes + box] = jnp.sin(angle) * live
+    _, _, dir_x, dir_y, dir_z = place(group_at)
+    for parent in range(center.shape[0]):
+        turns = center[parent, 0] * dir_x + center[parent, 1] * dir_y + center[parent, 2] * dir_z
+        angle = 2.0 * math.pi * turns
+        center_cos[parent] = jnp.cos(angle)
+        center_sin[parent] = jnp.sin(angle)
+
+
+def combine_kernel(step, groups, members, boxes, sources, piece, *refs):
+    pays, edges = refs[:members], refs[members : 2 * members]
+    cosines, sines, excess, band_zero, band_one, out, spread, total = refs[2 * members :]
+    rows = boxes * 2 * sources
+    tiles = piece // LANES
+    wide_at = lax.axis_index("wide")
+    last = lax.axis_size("wide") - 1
+    group_at, member_at = wide_at // members, wide_at % members
+    at = pick_partner(group_at, step) * members + member_at
+    slot = lax.broadcasted_iota(jnp.int32, (16, LANES), 0)
+    lane = lax.broadcasted_iota(jnp.int32, (16, LANES), 1)
+    place = jnp.where(
+        ((slot < HALO) & (lane == LANES - HALO + slot)) | ((slot >= HALO) & (slot < 2 * HALO) & (lane == slot - HALO)), 1.0, 0.0
+    ).astype(jnp.bfloat16)
+    outer = ((slot < HALO) & (at == 0)) | ((slot >= HALO) & (at == last))
+    rims = []
+    for swap in range(members):
+        rim = pays[swap][tiles * rows : tiles * rows + 16, :].astype(jnp.float32)
+        rims.append(jnp.where(outer, edges[swap][...].astype(jnp.float32), rim).astype(jnp.bfloat16))
+    rim = jnp.concatenate(rims, axis=1)
+    rim_tile = lax.dot_general(rim, place, (((0,), (0,)), ((), ())), preferred_element_type=jnp.float32).astype(jnp.bfloat16)
+
+    def tile(index):
+        if index < 0 or index >= tiles:
+            return rim_tile
+        return jnp.concatenate([pays[swap][index * rows : (index + 1) * rows, :] for swap in range(members)], axis=0)
+
+    for group in range(-1, tiles):
+        first = max(0, 4 * group + 2)
+        end = min(4 * tiles, 4 * group + 6)
+        left, right = tile(group), tile(group + 1)
+        window = jnp.concatenate([left, right, left, right], axis=1)
+        bands = []
+        for column in range(first, end):
+            at_column = (column + 2) % 4 * LANES
+            which = jnp.broadcast_to(excess[column : column + 1, :], (16, LANES)).astype(jnp.bfloat16)
+            which = jnp.concatenate([which] * (band_zero.shape[0] // 16), axis=0)
+            zero = band_zero[:, at_column : at_column + LANES]
+            one = band_one[:, at_column : at_column + LANES]
+            bands.append(zero * (1 - which) + one * which)
+        band = jnp.concatenate(bands, axis=1)
+        spread[:, : (end - first) * LANES] = jnp.dot(window, band, preferred_element_type=jnp.float32)
+        for column in range(first, end):
+            lanes = slice((column - first) * LANES, (column - first + 1) * LANES)
+            real_sum = jnp.zeros((sources, LANES), jnp.float32)
+            imag_sum = jnp.zeros((sources, LANES), jnp.float32)
+            for child in range(members * boxes):
+                start = child * 2 * sources
+                real = spread[start : start + sources, lanes].astype(jnp.bfloat16).astype(jnp.float32)
+                imag = spread[start + sources : start + 2 * sources, lanes].astype(jnp.bfloat16).astype(jnp.float32)
+                cosine = cosines[child, column : column + 1, :]
+                sine = sines[child, column : column + 1, :]
+                real_sum = real_sum + (cosine * real - sine * imag)
+                imag_sum = imag_sum + (sine * real + cosine * imag)
+            total[pl.ds(column, sources, stride=4 * tiles), :] = real_sum
+            total[pl.ds(sources * 4 * tiles + column, sources, stride=4 * tiles), :] = imag_sum
+    out[...] = total[...].astype(out.dtype)
+
+
+def finish_kernel(groups, members, boxes, sources, rows, parent_of, *refs):
+    arrived = refs[:groups]
+    center_cos, center_sin, parent_out, far_out = refs[groups:]
+    group_at = lax.axis_index("wide") // members
+    parents = center_cos.shape[0]
+    scale = 1.0 / math.sqrt(parents)
+    names = [parent_of[pick_partner(group_at, step) * members * boxes] for step in range(groups)]
+    turn_cos = [center_cos[name] * scale for name in names]
+    turn_sin = [center_sin[name] * scale for name in names]
+    for source in range(sources):
+        real_at = slice(source * rows, (source + 1) * rows)
+        imag_at = slice((sources + source) * rows, (sources + source + 1) * rows)
+        real_sum = jnp.zeros((rows, LANES), jnp.float32)
+        imag_sum = jnp.zeros((rows, LANES), jnp.float32)
+        for step in range(groups):
+            real = arrived[step][real_at, :].astype(jnp.float32)
+            imag = arrived[step][imag_at, :].astype(jnp.float32)
+            parent_out[names[step], real_at, :] = real
+            parent_out[names[step], imag_at, :] = imag
+            real_sum = real_sum + (turn_cos[step] * real - turn_sin[step] * imag)
+            imag_sum = imag_sum + (turn_sin[step] * real + turn_cos[step] * imag)
+        far_out[real_at, :] = real_sum
+        far_out[imag_at, :] = imag_sum
+
+
+def grouped(child_pattern, child_parent, child_octant, parent_center, stencil_start, members):
+    n_wide, n_narrow = lax.axis_size("wide"), lax.axis_size("narrow")
+    boxes, _, sources, block = child_pattern.shape
+    groups = n_wide // members
+    piece = block // n_wide
+    tiles = piece // LANES
+    rows = boxes * 2 * sources
+    out_rows = 4 * tiles
+    parents = parent_center.shape[0]
+    vmem = pl.BlockSpec(memory_space=pltpu.VMEM)
+    smem = pl.BlockSpec(memory_space=pltpu.SMEM)
+    limit = pltpu.CompilerParams(vmem_limit_bytes=32 * 1024 * 1024)
+    packed = pl.pallas_call(
+        functools.partial(pack_kernel, groups, members, piece),
+        out_shape=[jax.ShapeDtypeStruct((tiles * rows + 16, LANES), jnp.bfloat16)] * (groups * members)
+        + [jax.ShapeDtypeStruct((16, LANES), jnp.bfloat16)],
+        in_specs=[vmem],
+        out_specs=[vmem] * (groups * members + 1),
+        compiler_params=limit,
+        name="pack",
+    )(child_pattern)
+    edge = packed[-1]
+    order = list(range(groups - 1, -1, -1))
+
+    def swap_with(array, step):
+        return lax.ppermute(array, "wide", [(i, i ^ step) for i in range(n_wide)])
+
+    def edge_swap(step):
+        pairs = [(i * 2 + n, (i ^ step) * 2 + 1 - n) for i in range(n_wide) for n in range(2)]
+        return lax.ppermute(edge, ("wide", "narrow"), pairs)
+
+    edges = [edge_swap(swap) for swap in range(members)]
+    tables = pl.pallas_call(
+        functools.partial(prep_kernel, groups, members, boxes, piece),
+        out_shape=[
+            jax.ShapeDtypeStruct((groups, members * boxes, out_rows, LANES), jnp.float32),
+            jax.ShapeDtypeStruct((groups, members * boxes, out_rows, LANES), jnp.float32),
+            jax.ShapeDtypeStruct((parents, out_rows, LANES), jnp.float32),
+            jax.ShapeDtypeStruct((parents, out_rows, LANES), jnp.float32),
+            jax.ShapeDtypeStruct((groups, out_rows, LANES), jnp.float32),
+        ],
+        in_specs=[smem, smem, smem, vmem],
+        out_specs=[vmem] * 5,
+        compiler_params=limit,
+        name="prep",
+    )(child_parent, child_octant, parent_center, stencil_start.reshape(-1, LANES))
+    cosines, sines, center_cos, center_sin, excess = tables
+    bands = stencil_tables(2 * LANES, 4 * LANES)
+    arrived = [None] * groups
+    for step in order:
+        pays = [packed[step * members]]
+        pays += [swap_with(packed[step * members + swap], swap) for swap in range(1, members)]
+        total = pl.pallas_call(
+            functools.partial(combine_kernel, step, groups, members, boxes, sources, piece),
+            out_shape=jax.ShapeDtypeStruct((2 * sources * out_rows, LANES), jnp.bfloat16 if step else jnp.float32),
+            grid=(1,),
+            in_specs=[pl.BlockSpec(pay.shape, lambda i: (0, 0)) for pay in pays + edges]
+            + [pl.BlockSpec((None, members * boxes, out_rows, LANES), lambda i, step=step: (step, 0, 0, 0))] * 2
+            + [pl.BlockSpec((None, out_rows, LANES), lambda i, step=step: (step, 0, 0))]
+            + [pl.BlockSpec(bands.shape[1:], lambda i: (0, 0))] * 2,
+            out_specs=pl.BlockSpec((2 * sources * out_rows, LANES), lambda i: (0, 0)),
+            scratch_shapes=[
+                pltpu.VMEM((members * rows, 4 * LANES), jnp.float32),
+                pltpu.VMEM((2 * sources * out_rows, LANES), jnp.float32),
+            ],
+            compiler_params=limit,
+            name="combine",
+        )(*pays, *edges, cosines, sines, excess, bands[0], bands[1])
+        arrived[step] = swap_with(total, step * members) if step else total
+    parent_pattern, far_field = pl.pallas_call(
+        functools.partial(finish_kernel, groups, members, boxes, sources, out_rows),
+        out_shape=[
+            jax.ShapeDtypeStruct((parents, 2 * sources * out_rows, LANES), jnp.float32),
+            jax.ShapeDtypeStruct((2 * sources * out_rows, LANES), jnp.float32),
+        ],
+        in_specs=[smem] + [vmem] * (groups + 2),
+        out_specs=[vmem] * 2,
+        compiler_params=limit,
+        name="finish",
+    )(child_parent, *arrived, center_cos, center_sin)
+    return (
+        parent_pattern.reshape(parents, 2, sources, 1, 4 * piece),
+        far_field.reshape(2, sources, 1, 4 * piece),
+    )
+
+
+def power_of_two(number):
+    return number > 0 and number & (number - 1) == 0
+
+
+def per_device(child_pattern, child_parent, child_octant, parent_center, stencil_start):
+    n_wide, n_narrow = lax.axis_size("wide"), lax.axis_size("narrow")
+    boxes, _, sources, block = child_pattern.shape
+    run = child_parent.shape[0] // parent_center.shape[0]
+    if run % boxes == 0 and block % n_wide == 0:
+        members = run // boxes
+        fits = (
+            n_narrow == 2
+            and n_wide == members * parent_center.shape[0]
+            and power_of_two(members)
+            and power_of_two(n_wide)
+            and block // n_wide % LANES == 0
+            and sources % 16 == 0
+            and stencil_start.shape[0] == 4 * block * n_narrow
+        )
+        if fits:
+            return grouped(child_pattern, child_parent, child_octant, parent_center, stencil_start, members)
+    return exchanged(child_pattern, child_parent, child_octant, parent_center, stencil_start)
+
+
 def solution(mesh):
     in_specs = (P("wide", None, None, "narrow"), P(), P(), P(), P())
     out_specs = (P(None, None, None, "narrow", "wide"), P(None, None, "narrow", "wide"))

time: 159 us -> 61.5 us (0.39)
  the two profiles are of different devices: /device:TPU:13 before, /device:TPU:0 now
where the time goes in v1:
time: 61.5 us; the launch traced here: 61.4 us
  waiting for transfers between devices  24.5 us (40%)
  starting transfers between devices  20.8 us (34%)
  Pallas kernels  13.6 us (22%)
  local copies, waits for them, and re-layouts  1.7 us (3%)
  between operations  0.78 us (1%)
    ppermute x15, waiting for transfers between devices, swap_with(): return lax.ppermute(array, 'wide', [(i, i ^ step) for i in range(n_wide)])  16.2 us
    ppermute x15, starting transfers between devices, swap_with(): return lax.ppermute(array, 'wide', [(i, i ^ step) for i in range(n_wide)])  13.9 us
    ppermute x4, waiting for transfers between devices, edge_swap(): return lax.ppermute(edge, ('wide', 'narrow'), pairs)  8.21 us
    pallas_call x4, Pallas kernels, grouped(): pl.pallas_call(functools.partial(combine_kernel, step, groups, members, b...  8.02 us
    ppermute x4, starting transfers between devices, edge_swap(): return lax.ppermute(edge, ('wide', 'narrow'), pairs)  6.97 us
    pallas_call x1, Pallas kernels, grouped(): pl.pallas_call(functools.partial(finish_kernel, groups, members, boxes, s...  2.63 us
    pallas_call x1, Pallas kernels, grouped(): pl.pallas_call(functools.partial(prep_kernel, groups, members, boxes, pie...  1.96 us
    unnamed x14, local copies, waits for them, and re-layouts  1.7 us
  transfers between devices with their start and end apart: 19, of which 8 were waited for; matrix products, arithmetic and copies ran while one was open for 0% of the time, Pallas kernels for 16%

profile of v1, /device:TPU:0, one launch (start us, length us, event | category | flops | bytes accessed | tf_op | source)
XLA Modules:
  0.0 61.4 jit_solution(18128768022855011391)
XLA Ops:
  0.6 0.0 copy-start
  0.6 0.0 copy-start.1
  0.7 1.7 %copy-done.2 = bf16[2,2,32,8192]{3,2,1,0:T(8,128)(2,1)S(1)} copy-done((bf16[2,2,32,8192]{3,2,1,0:T(8,128)(2,1)S(1)}, bf16[2,2,32,8192]{3,2,1,0:T(8,128)(2,1)}, u32[]{:S(2)}) %copy-start.2) | copy-done | bytes 2097176
  2.3 1.0 %pack.1 = (bf16[528,128]{1,0:T(8,128)(2,1)S(1)}, bf16[528,128]{1,0:T(8,128)(2,1)S(1)}, bf16[528,128]{1,0:T(8,128)(2,1)S(1)}, bf16[528,128]{1,0:T(8,128)(2,1)S(1)...) custom-call(bf16[2,2,32,8192]{3,2,1,0:T(8,128)(2,1)S(1)} %copy-done.2), custom_call_target="tpu_custom_call" | custom-call | tf_op jit(solution)/shard_map/pack/pallas_call | solution.py:361
  3.3 0.5 collective-permute-start.11
  3.8 2.6 %collective-permute-start.12 = (bf16[528,128]{1,0:T(8,128)(2,1)S(1)}, bf16[528,128]{1,0:T(8,128)(2,1)S(1)}, u32[]{:S(2)}, u32[]{:S(2)}) collective-permute-start(bf16[528,128]{1,0:T(8,128)(2,1)S(1)} %get-tuple-element.40), channel_id=1, source_target_pairs={{0,4},{2,6},{4,0},{6,2},{8,12},{10,14},{12,8},{14,10},{16,20},{18,... | collective-permute-start | bytes 405512 | tf_op jit(solution)/shard_map/ppermute | solution.py:374
  6.4 0.2 collective-permute-start.15
  6.6 0.3 collective-permute-start.16
  6.9 2.4 %collective-permute-start.6 = (bf16[16,128]{1,0:T(8,128)(2,1)S(1)}, bf16[16,128]{1,0:T(8,128)(2,1)S(1)}, u32[]{:S(2)}, u32[]{:S(2)}) collective-permute-start(bf16[16,128]{1,0:T(8,128)(2,1)S(1)} %get-tuple-element.30), channel_id=1, source_target_pairs={{0,7},{1,6},{2,5},{3,4},{4,3},{5,2},{6,1},{7,0},{8,15},{9,14},{10,... | collective-permute-start | bytes 12296 | tf_op jit(solution)/shard_map/ppermute | solution.py:378
  9.2 1.7 %collective-permute-done.6.refs_7_ = bf16[16,128]{1,0:T(8,128)(2,1)S(1)} collective-permute-done((bf16[16,128]{1,0:T(8,128)(2,1)S(1)}, bf16[16,128]{1,0:T(8,128)(2,1)S(1)}, u32[]{:S(2)}, u32[]{:S(2)}) %collective-permute-start.6) | collective-permute-done | bytes 4128 | tf_op jit(solution)/shard_map/ppermute | solution.py:378
  10.9 2.7 %collective-permute-start.5 = (bf16[16,128]{1,0:T(8,128)(2,1)S(1)}, bf16[16,128]{1,0:T(8,128)(2,1)S(1)}, u32[]{:S(2)}, u32[]{:S(2)}) collective-permute-start(bf16[16,128]{1,0:T(8,128)(2,1)S(1)} %get-tuple-element.30), channel_id=1, source_target_pairs={{0,5},{1,4},{2,7},{3,6},{4,1},{5,0},{6,3},{7,2},{8,13},{9,12},{10,... | collective-permute-start | bytes 12296 | tf_op jit(solution)/shard_map/ppermute | solution.py:378
  13.6 1.8 %collective-permute-done.5.refs_6_ = bf16[16,128]{1,0:T(8,128)(2,1)S(1)} collective-permute-done((bf16[16,128]{1,0:T(8,128)(2,1)S(1)}, bf16[16,128]{1,0:T(8,128)(2,1)S(1)}, u32[]{:S(2)}, u32[]{:S(2)}) %collective-permute-start.5) | collective-permute-done | bytes 4128 | tf_op jit(solution)/shard_map/ppermute | solution.py:378
  15.4 0.2 collective-permute-start.4
  15.6 2.8 %collective-permute-done.4.refs_5_ = bf16[16,128]{1,0:T(8,128)(2,1)S(1)} collective-permute-done((bf16[16,128]{1,0:T(8,128)(2,1)S(1)}, bf16[16,128]{1,0:T(8,128)(2,1)S(1)}, u32[]{:S(2)}, u32[]{:S(2)}) %collective-permute-start.4) | collective-permute-done | bytes 4128 | tf_op jit(solution)/shard_map/ppermute | solution.py:378
  18.4 1.7 %collective-permute-start.3 = (bf16[16,128]{1,0:T(8,128)(2,1)S(1)}, bf16[16,128]{1,0:T(8,128)(2,1)S(1)}, u32[]{:S(2)}, u32[]{:S(2)}) collective-permute-start(bf16[16,128]{1,0:T(8,128)(2,1)S(1)} %get-tuple-element.30), channel_id=1, source_target_pairs={{0,1},{1,0},{2,3},{3,2},{4,5},{5,4},{6,7},{7,6},{8,9},{9,8},{10,11... | collective-permute-start | bytes 12296 | tf_op jit(solution)/shard_map/ppermute | solution.py:378
  20.2 1.9 %collective-permute-done.3.refs_4_ = bf16[16,128]{1,0:T(8,128)(2,1)S(1)} collective-permute-done((bf16[16,128]{1,0:T(8,128)(2,1)S(1)}, bf16[16,128]{1,0:T(8,128)(2,1)S(1)}, u32[]{:S(2)}, u32[]{:S(2)}) %collective-permute-start.3) | collective-permute-done | bytes 4128 | tf_op jit(solution)/shard_map/ppermute | solution.py:378
  22.0 0.3 collective-permute-start.17
  22.4 0.0 collective-permute-done.11.refs_1_
  22.4 1.4 %collective-permute-start.13 = (bf16[528,128]{1,0:T(8,128)(2,1)S(1)}, bf16[528,128]{1,0:T(8,128)(2,1)S(1)}, u32[]{:S(2)}, u32[]{:S(2)}) collective-permute-start(bf16[528,128]{1,0:T(8,128)(2,1)S(1)} %get-tuple-element.41), channel_id=1, source_target_pairs={{0,6},{2,4},{4,2},{6,0},{8,14},{10,12},{12,10},{14,8},{16,22},{18,... | collective-permute-start | bytes 405512 | tf_op jit(solution)/shard_map/ppermute | solution.py:374
  23.8 0.0 collective-permute-done.12.refs_2_
  23.8 0.2 collective-permute-start.7
  24.0 0.0 collective-permute-done.15.refs_1_
  24.0 1.6 %collective-permute-start.8 = (bf16[528,128]{1,0:T(8,128)(2,1)S(1)}, bf16[528,128]{1,0:T(8,128)(2,1)S(1)}, u32[]{:S(2)}, u32[]{:S(2)}) collective-permute-start(bf16[528,128]{1,0:T(8,128)(2,1)S(1)} %get-tuple-element.36), channel_id=1, source_target_pairs={{0,4},{2,6},{4,0},{6,2},{8,12},{10,14},{12,8},{14,10},{16,20},{18,... | collective-permute-start | bytes 405512 | tf_op jit(solution)/shard_map/ppermute | solution.py:374
  25.6 0.0 collective-permute-done.16.refs_2_
  25.7 0.1 collective-permute-start.9
  25.8 1.8 %collective-permute-done.17.refs_3_ = bf16[528,128]{1,0:T(8,128)(2,1)S(1)} collective-permute-done((bf16[528,128]{1,0:T(8,128)(2,1)S(1)}, bf16[528,128]{1,0:T(8,128)(2,1)S(1)}, u32[]{:S(2)}, u32[]{:S(2)}) %collective-permute-start.17) | collective-permute-done | bytes 135200 | tf_op jit(solution)/shard_map/ppermute | solution.py:374
  27.6 0.7 %collective-permute-start = (bf16[528,128]{1,0:T(8,128)(2,1)S(1)}, bf16[528,128]{1,0:T(8,128)(2,1)S(1)}, u32[]{:S(2)}, u32[]{:S(2)}) collective-permute-start(bf16[528,128]{1,0:T(8,128)(2,1)S(1)} %get-tuple-element.27), channel_id=1, source_target_pairs={{0,2},{2,0},{4,6},{6,4},{8,10},{10,8},{12,14},{14,12},{16,18},{18,... | collective-permute-start | bytes 405512 | tf_op jit(solution)/shard_map/ppermute | solution.py:374
  28.4 2.0 %prep.1 = (f32[4,8,16,128]{3,2,1,0:T(8,128)S(1)}, f32[4,8,16,128]{3,2,1,0:T(8,128)S(1)}, f32[4,16,128]{2,1,0:T(8,128)S(1)}, f32[4,16,128]{2,1,0:T(8,128)S(1)}, f32[4,16,128]{2,1,0:T(8,128)S(1)}) custom-call(s32[32]{0:T(128)S(1)} %copy-done.4, s32[32]{0:T(128)S(1)} %copy-done.6, f32[4,3]{1,0:T(4,128)S(1)} %copy-done.5, s32[512,128]{1,0:T(8,128)S(1)} %bitcast.3), custom_call_target="tpu_custom_call" | custom-call | tf_op jit(solution)/shard_map/prep/pallas_call | solution.py:381
  30.3 2.0 %combine.7 = bf16[1024,128]{1,0:T(8,128)(2,1)S(1)} custom-call(bf16[528,128]{1,0:T(8,128)(2,1)S(1)} %get-tuple-element.42.refs_0_, bf16[528,128]{1,0:T(8,128)(2,1)S(1)} %collective-permute-done.15.refs_1_, bf16[528,128]{1,0:T(8,128)(2,1)S(1)} %collective-permute-done.16.refs_2_, bf16[528,128]{1,0:T(8,128)(2,1)S(1)} %collective-permute-done.17.refs_3_, ...), custom_call_target="tpu_custom_call" | custom-call | tf_op jit(solution)/shard_map/combine/pallas_call | solution.py:401
  32.4 0.0 collective-permute-done.13.refs_3_
  32.4 3.7 %collective-permute-start.18 = (bf16[1024,128]{1,0:T(8,128)(2,1)S(1)}, bf16[1024,128]{1,0:T(8,128)(2,1)S(1)}, u32[]{:S(2)}, u32[]{:S(2)}) collective-permute-start(bf16[1024,128]{1,0:T(8,128)(2,1)S(1)} %combine.7), channel_id=1, source_target_pairs={{0,24},{2,26},{4,28},{6,30},{8,16},{10,18},{12,20},{14,22},{16,8},... | collective-permute-start | bytes 786440 | tf_op jit(solution)/shard_map/ppermute | solution.py:374
  36.0 2.0 %combine.6 = bf16[1024,128]{1,0:T(8,128)(2,1)S(1)} custom-call(bf16[528,128]{1,0:T(8,128)(2,1)S(1)} %get-tuple-element.38.refs_0_, bf16[528,128]{1,0:T(8,128)(2,1)S(1)} %collective-permute-done.11.refs_1_, bf16[528,128]{1,0:T(8,128)(2,1)S(1)} %collective-permute-done.12.refs_2_, bf16[528,128]{1,0:T(8,128)(2,1)S(1)} %collective-permute-done.13.refs_3_, ...), custom_call_target="tpu_custom_call" | custom-call | tf_op jit(solution)/shard_map/combine/pallas_call | solution.py:401
  38.1 0.0 collective-permute-done.7.refs_1_
  38.1 0.1 collective-permute-start.14
  38.1 0.0 collective-permute-done.8.refs_2_
  38.2 0.0 collective-permute-done.9.refs_3_
  38.2 2.0 %combine.5 = bf16[1024,128]{1,0:T(8,128)(2,1)S(1)} custom-call(bf16[528,128]{1,0:T(8,128)(2,1)S(1)} %get-tuple-element.34.refs_0_, bf16[528,128]{1,0:T(8,128)(2,1)S(1)} %collective-permute-done.7.refs_1_, bf16[528,128]{1,0:T(8,128)(2,1)S(1)} %collective-permute-done.8.refs_2_, bf16[528,128]{1,0:T(8,128)(2,1)S(1)} %collective-permute-done.9.refs_3_, ...), custom_call_target="tpu_custom_call" | custom-call | tf_op jit(solution)/shard_map/combine/pallas_call | solution.py:401
  40.2 0.8 %collective-permute-start.10 = (bf16[1024,128]{1,0:T(8,128)(2,1)S(1)}, bf16[1024,128]{1,0:T(8,128)(2,1)S(1)}, u32[]{:S(2)}, u32[]{:S(2)}) collective-permute-start(bf16[1024,128]{1,0:T(8,128)(2,1)S(1)} %combine.5), channel_id=1, source_target_pairs={{0,8},{2,10},{4,12},{6,14},{8,0},{10,2},{12,4},{14,6},{16,24},{18,... | collective-permute-start | bytes 786440 | tf_op jit(solution)/shard_map/ppermute | solution.py:374
  41.0 1.4 %collective-permute-start.1 = (bf16[528,128]{1,0:T(8,128)(2,1)S(1)}, bf16[528,128]{1,0:T(8,128)(2,1)S(1)}, u32[]{:S(2)}, u32[]{:S(2)}) collective-permute-start(bf16[528,128]{1,0:T(8,128)(2,1)S(1)} %get-tuple-element.28), channel_id=1, source_target_pairs={{0,4},{2,6},{4,0},{6,2},{8,12},{10,14},{12,8},{14,10},{16,20},{18,... | collective-permute-start | bytes 405512 | tf_op jit(solution)/shard_map/ppermute | solution.py:374
  42.4 0.0 collective-permute-done.refs_1_
  42.4 0.0 collective-permute-start.2
  42.4 4.3 %collective-permute-done.1.refs_2_ = bf16[528,128]{1,0:T(8,128)(2,1)S(1)} collective-permute-done((bf16[528,128]{1,0:T(8,128)(2,1)S(1)}, bf16[528,128]{1,0:T(8,128)(2,1)S(1)}, u32[]{:S(2)}, u32[]{:S(2)}) %collective-permute-start.1) | collective-permute-done | bytes 135200 | tf_op jit(solution)/shard_map/ppermute | solution.py:374
  46.7 1.5 %collective-permute-done.2.refs_3_ = bf16[528,128]{1,0:T(8,128)(2,1)S(1)} collective-permute-done((bf16[528,128]{1,0:T(8,128)(2,1)S(1)}, bf16[528,128]{1,0:T(8,128)(2,1)S(1)}, u32[]{:S(2)}, u32[]{:S(2)}) %collective-permute-start.2) | collective-permute-done | bytes 135200 | tf_op jit(solution)/shard_map/ppermute | solution.py:374
  48.2 2.0 %combine.4.refs_0_ = f32[1024,128]{1,0:T(8,128)S(1)} custom-call(bf16[528,128]{1,0:T(8,128)(2,1)S(1)} %get-tuple-element.26.refs_0_, bf16[528,128]{1,0:T(8,128)(2,1)S(1)} %collective-permute-done.refs_1_, bf16[528,128]{1,0:T(8,128)(2,1)S(1)} %collective-permute-done.1.refs_2_, bf16[528,128]{1,0:T(8,128)(2,1)S(1)} %collective-permute-done.2.refs_3_, ...), custom_call_target="tpu_custom_call" | custom-call | tf_op jit(solution)/shard_map/combine/pallas_call | solution.py:401
  50.2 0.0 collective-permute-done.18.refs_3_
  50.2 8.5 %collective-permute-done.14.refs_2_ = bf16[1024,128]{1,0:T(8,128)(2,1)S(1)} collective-permute-done((bf16[1024,128]{1,0:T(8,128)(2,1)S(1)}, bf16[1024,128]{1,0:T(8,128)(2,1)S(1)}, u32[]{:S(2)}, u32[]{:S(2)}) %collective-permute-start.14) | collective-permute-done | bytes 262176 | tf_op jit(solution)/shard_map/ppermute | solution.py:374
  58.8 0.0 collective-permute-done.10.refs_1_
  58.8 2.6 %finish.1 = (f32[4,1024,128]{2,1,0:T(8,128)}, f32[1024,128]{1,0:T(8,128)}) custom-call(s32[32]{0:T(128)S(1)} %copy-done.4, f32[1024,128]{1,0:T(8,128)S(1)} %combine.4.refs_0_, bf16[1024,128]{1,0:T(8,128)(2,1)S(1)} %collective-permute-done.10.refs_1_, bf16[1024,128]{1,0:T(8,128)(2,1)S(1)} %collective-permute-done.14.refs_2_, ...), custom_call_target="tpu_custom_call" | custom-call | tf_op jit(solution)/shard_map/finish/pallas_call | solution.py:418
  (11 shorter events, 0.0 us)
Async XLA Ops:
  0.6 29.7 %copy-start = (bf16[512,512]{1,0:T(8,128)(2,1)S(1)}, bf16[512,512]{1,0:T(8,128)(2,1)}, u32[]{:S(2)}) copy-start(bf16[512,512]{1,0:T(8,128)(2,1)} %constant.5.clone.refs_12_) | copy-start | bytes 1572868
  0.6 29.7 %copy-start.1 = (bf16[512,512]{1,0:T(8,128)(2,1)S(1)}, bf16[512,512]{1,0:T(8,128)(2,1)}, u32[]{:S(2)}) copy-start(bf16[512,512]{1,0:T(8,128)(2,1)} %constant.4.clone.refs_11_) | copy-start | bytes 1572868
  0.7 1.7 %copy-start.2 = (bf16[2,2,32,8192]{3,2,1,0:T(8,128)(2,1)S(1)}, bf16[2,2,32,8192]{3,2,1,0:T(8,128)(2,1)}, u32[]{:S(2)}) copy-start(bf16[2,2,32,8192]{3,2,1,0:T(8,128)(2,1)} %cells.1) | copy-start | bytes 6291460
  2.3 26.0 %copy-start.3 = (s32[65536]{0:T(1024)S(1)}, s32[65536]{0:T(1024)}, u32[]{:S(2)}) copy-start(s32[65536]{0:T(1024)} %param.17) | copy-start | bytes 786436
  2.3 26.0 %copy-start.4 = (s32[32]{0:T(128)S(1)}, s32[32]{0:T(128)}, u32[]{:S(2)}) copy-start(s32[32]{0:T(128)} %parent_of.3) | copy-start | bytes 388
  2.3 26.0 %copy-start.5 = (f32[4,3]{1,0:T(4,128)S(1)}, f32[4,3]{1,0:T(4,128)}, u32[]{:S(2)}) copy-start(f32[4,3]{1,0:T(4,128)} %center.1) | copy-start | bytes 148
  2.3 26.0 %copy-start.6 = (s32[32]{0:T(128)S(1)}, s32[32]{0:T(128)}, u32[]{:S(2)}) copy-start(s32[32]{0:T(128)} %octant_of.1) | copy-start | bytes 388
  3.3 19.0 %collective-permute-start.11 = (bf16[528,128]{1,0:T(8,128)(2,1)S(1)}, bf16[528,128]{1,0:T(8,128)(2,1)S(1)}, u32[]{:S(2)}, u32[]{:S(2)}) collective-permute-start(bf16[528,128]{1,0:T(8,128)(2,1)S(1)} %get-tuple-element.39), channel_id=1, source_target_pairs={{0,2},{2,0},{4,6},{6,4},{8,10},{10,8},{12,14},{14,12},{16,18},{18,... | collective-permute-start | bytes 405512 | tf_op jit(solution)/shard_map/ppermute | solution.py:374
  3.8 20.0 %collective-permute-start.12 = (bf16[528,128]{1,0:T(8,128)(2,1)S(1)}, bf16[528,128]{1,0:T(8,128)(2,1)S(1)}, u32[]{:S(2)}, u32[]{:S(2)}) collective-permute-start(bf16[528,128]{1,0:T(8,128)(2,1)S(1)} %get-tuple-element.40), channel_id=1, source_target_pairs={{0,4},{2,6},{4,0},{6,2},{8,12},{10,14},{12,8},{14,10},{16,20},{18,... | collective-permute-start | bytes 405512 | tf_op jit(solution)/shard_map/ppermute | solution.py:374
  6.4 17.6 %collective-permute-start.15 = (bf16[528,128]{1,0:T(8,128)(2,1)S(1)}, bf16[528,128]{1,0:T(8,128)(2,1)S(1)}, u32[]{:S(2)}, u32[]{:S(2)}) collective-permute-start(bf16[528,128]{1,0:T(8,128)(2,1)S(1)} %get-tuple-element.43), channel_id=1, source_target_pairs={{0,2},{2,0},{4,6},{6,4},{8,10},{10,8},{12,14},{14,12},{16,18},{18,... | collective-permute-start | bytes 405512 | tf_op jit(solution)/shard_map/ppermute | solution.py:374
  6.6 19.1 %collective-permute-start.16 = (bf16[528,128]{1,0:T(8,128)(2,1)S(1)}, bf16[528,128]{1,0:T(8,128)(2,1)S(1)}, u32[]{:S(2)}, u32[]{:S(2)}) collective-permute-start(bf16[528,128]{1,0:T(8,128)(2,1)S(1)} %get-tuple-element.44), channel_id=1, source_target_pairs={{0,4},{2,6},{4,0},{6,2},{8,12},{10,14},{12,8},{14,10},{16,20},{18,... | collective-permute-start | bytes 405512 | tf_op jit(solution)/shard_map/ppermute | solution.py:374
  6.9 4.0 %collective-permute-start.6 = (bf16[16,128]{1,0:T(8,128)(2,1)S(1)}, bf16[16,128]{1,0:T(8,128)(2,1)S(1)}, u32[]{:S(2)}, u32[]{:S(2)}) collective-permute-start(bf16[16,128]{1,0:T(8,128)(2,1)S(1)} %get-tuple-element.30), channel_id=1, source_target_pairs={{0,7},{1,6},{2,5},{3,4},{4,3},{5,2},{6,1},{7,0},{8,15},{9,14},{10,... | collective-permute-start | bytes 12296 | tf_op jit(solution)/shard_map/ppermute | solution.py:378
  10.9 4.5 %collective-permute-start.5 = (bf16[16,128]{1,0:T(8,128)(2,1)S(1)}, bf16[16,128]{1,0:T(8,128)(2,1)S(1)}, u32[]{:S(2)}, u32[]{:S(2)}) collective-permute-start(bf16[16,128]{1,0:T(8,128)(2,1)S(1)} %get-tuple-element.30), channel_id=1, source_target_pairs={{0,5},{1,4},{2,7},{3,6},{4,1},{5,0},{6,3},{7,2},{8,13},{9,12},{10,... | collective-permute-start | bytes 12296 | tf_op jit(solution)/shard_map/ppermute | solution.py:378
  15.4 3.0 %collective-permute-start.4 = (bf16[16,128]{1,0:T(8,128)(2,1)S(1)}, bf16[16,128]{1,0:T(8,128)(2,1)S(1)}, u32[]{:S(2)}, u32[]{:S(2)}) collective-permute-start(bf16[16,128]{1,0:T(8,128)(2,1)S(1)} %get-tuple-element.30), channel_id=1, source_target_pairs={{0,3},{1,2},{2,1},{3,0},{4,7},{5,6},{6,5},{7,4},{8,11},{9,10},{10,... | collective-permute-start | bytes 12296 | tf_op jit(solution)/shard_map/ppermute | solution.py:378
  18.4 3.6 %collective-permute-start.3 = (bf16[16,128]{1,0:T(8,128)(2,1)S(1)}, bf16[16,128]{1,0:T(8,128)(2,1)S(1)}, u32[]{:S(2)}, u32[]{:S(2)}) collective-permute-start(bf16[16,128]{1,0:T(8,128)(2,1)S(1)} %get-tuple-element.30), channel_id=1, source_target_pairs={{0,1},{1,0},{2,3},{3,2},{4,5},{5,4},{6,7},{7,6},{8,9},{9,8},{10,11... | collective-permute-start | bytes 12296 | tf_op jit(solution)/shard_map/ppermute | solution.py:378
  22.0 5.6 %collective-permute-start.17 = (bf16[528,128]{1,0:T(8,128)(2,1)S(1)}, bf16[528,128]{1,0:T(8,128)(2,1)S(1)}, u32[]{:S(2)}, u32[]{:S(2)}) collective-permute-start(bf16[528,128]{1,0:T(8,128)(2,1)S(1)} %get-tuple-element.45), channel_id=1, source_target_pairs={{0,6},{2,4},{4,2},{6,0},{8,14},{10,12},{12,10},{14,8},{16,22},{18,... | collective-permute-start | bytes 405512 | tf_op jit(solution)/shard_map/ppermute | solution.py:374
  22.4 10.0 %collective-permute-start.13 = (bf16[528,128]{1,0:T(8,128)(2,1)S(1)}, bf16[528,128]{1,0:T(8,128)(2,1)S(1)}, u32[]{:S(2)}, u32[]{:S(2)}) collective-permute-start(bf16[528,128]{1,0:T(8,128)(2,1)S(1)} %get-tuple-element.41), channel_id=1, source_target_pairs={{0,6},{2,4},{4,2},{6,0},{8,14},{10,12},{12,10},{14,8},{16,22},{18,... | collective-permute-start | bytes 405512 | tf_op jit(solution)/shard_map/ppermute | solution.py:374
  23.8 14.3 %collective-permute-start.7 = (bf16[528,128]{1,0:T(8,128)(2,1)S(1)}, bf16[528,128]{1,0:T(8,128)(2,1)S(1)}, u32[]{:S(2)}, u32[]{:S(2)}) collective-permute-start(bf16[528,128]{1,0:T(8,128)(2,1)S(1)} %get-tuple-element.35), channel_id=1, source_target_pairs={{0,2},{2,0},{4,6},{6,4},{8,10},{10,8},{12,14},{14,12},{16,18},{18,... | collective-permute-start | bytes 405512 | tf_op jit(solution)/shard_map/ppermute | solution.py:374
  24.0 14.1 %collective-permute-start.8 = (bf16[528,128]{1,0:T(8,128)(2,1)S(1)}, bf16[528,128]{1,0:T(8,128)(2,1)S(1)}, u32[]{:S(2)}, u32[]{:S(2)}) collective-permute-start(bf16[528,128]{1,0:T(8,128)(2,1)S(1)} %get-tuple-element.36), channel_id=1, source_target_pairs={{0,4},{2,6},{4,0},{6,2},{8,12},{10,14},{12,8},{14,10},{16,20},{18,... | collective-permute-start | bytes 405512 | tf_op jit(solution)/shard_map/ppermute | solution.py:374
  25.7 12.5 %collective-permute-start.9 = (bf16[528,128]{1,0:T(8,128)(2,1)S(1)}, bf16[528,128]{1,0:T(8,128)(2,1)S(1)}, u32[]{:S(2)}, u32[]{:S(2)}) collective-permute-start(bf16[528,128]{1,0:T(8,128)(2,1)S(1)} %get-tuple-element.37), channel_id=1, source_target_pairs={{0,6},{2,4},{4,2},{6,0},{8,14},{10,12},{12,10},{14,8},{16,22},{18,... | collective-permute-start | bytes 405512 | tf_op jit(solution)/shard_map/ppermute | solution.py:374
  27.6 14.7 %collective-permute-start = (bf16[528,128]{1,0:T(8,128)(2,1)S(1)}, bf16[528,128]{1,0:T(8,128)(2,1)S(1)}, u32[]{:S(2)}, u32[]{:S(2)}) collective-permute-start(bf16[528,128]{1,0:T(8,128)(2,1)S(1)} %get-tuple-element.27), channel_id=1, source_target_pairs={{0,2},{2,0},{4,6},{6,4},{8,10},{10,8},{12,14},{14,12},{16,18},{18,... | collective-permute-start | bytes 405512 | tf_op jit(solution)/shard_map/ppermute | solution.py:374
  32.4 17.8 %collective-permute-start.18 = (bf16[1024,128]{1,0:T(8,128)(2,1)S(1)}, bf16[1024,128]{1,0:T(8,128)(2,1)S(1)}, u32[]{:S(2)}, u32[]{:S(2)}) collective-permute-start(bf16[1024,128]{1,0:T(8,128)(2,1)S(1)} %combine.7), channel_id=1, source_target_pairs={{0,24},{2,26},{4,28},{6,30},{8,16},{10,18},{12,20},{14,22},{16,8},... | collective-permute-start | bytes 786440 | tf_op jit(solution)/shard_map/ppermute | solution.py:374
  38.1 20.7 %collective-permute-start.14 = (bf16[1024,128]{1,0:T(8,128)(2,1)S(1)}, bf16[1024,128]{1,0:T(8,128)(2,1)S(1)}, u32[]{:S(2)}, u32[]{:S(2)}) collective-permute-start(bf16[1024,128]{1,0:T(8,128)(2,1)S(1)} %combine.6), channel_id=1, source_target_pairs={{0,16},{2,18},{4,20},{6,22},{8,24},{10,26},{12,28},{14,30},{16,0},... | collective-permute-start | bytes 786440 | tf_op jit(solution)/shard_map/ppermute | solution.py:374
  40.2 18.6 %collective-permute-start.10 = (bf16[1024,128]{1,0:T(8,128)(2,1)S(1)}, bf16[1024,128]{1,0:T(8,128)(2,1)S(1)}, u32[]{:S(2)}, u32[]{:S(2)}) collective-permute-start(bf16[1024,128]{1,0:T(8,128)(2,1)S(1)} %combine.5), channel_id=1, source_target_pairs={{0,8},{2,10},{4,12},{6,14},{8,0},{10,2},{12,4},{14,6},{16,24},{18,... | collective-permute-start | bytes 786440 | tf_op jit(solution)/shard_map/ppermute | solution.py:374
  41.0 5.7 %collective-permute-start.1 = (bf16[528,128]{1,0:T(8,128)(2,1)S(1)}, bf16[528,128]{1,0:T(8,128)(2,1)S(1)}, u32[]{:S(2)}, u32[]{:S(2)}) collective-permute-start(bf16[528,128]{1,0:T(8,128)(2,1)S(1)} %get-tuple-element.28), channel_id=1, source_target_pairs={{0,4},{2,6},{4,0},{6,2},{8,12},{10,14},{12,8},{14,10},{16,20},{18,... | collective-permute-start | bytes 405512 | tf_op jit(solution)/shard_map/ppermute | solution.py:374
  42.4 5.8 %collective-permute-start.2 = (bf16[528,128]{1,0:T(8,128)(2,1)S(1)}, bf16[528,128]{1,0:T(8,128)(2,1)S(1)}, u32[]{:S(2)}, u32[]{:S(2)}) collective-permute-start(bf16[528,128]{1,0:T(8,128)(2,1)S(1)} %get-tuple-element.29), channel_id=1, source_target_pairs={{0,6},{2,4},{4,2},{6,0},{8,14},{10,12},{12,10},{14,8},{16,22},{18,... | collective-permute-start | bytes 405512 | tf_op jit(solution)/shard_map/ppermute | solution.py:374

commit v2 on v1

v2 whole, which is shorter than its diff:
```python
import functools
import math

import jax
import jax.numpy as jnp
import ml_dtypes
import numpy as np
from jax import lax
from jax.experimental import pallas as pl
from jax.experimental.pallas import tpu as pltpu
from jax.sharding import PartitionSpec as P

K2 = 65536


def with_halo(cells, sides, width):
    for axis, dim in sides:
        count = lax.axis_size(axis)
        head = lax.slice_in_dim(cells, 0, width, axis=dim)
        tail = lax.slice_in_dim(cells, cells.shape[dim] - width, cells.shape[dim], axis=dim)
        cells = jnp.concatenate(
            [
                lax.ppermute(tail, axis, [(i, (i + 1) % count) for i in range(count)]),
                cells,
                lax.ppermute(head, axis, [((i + 1) % count, i) for i in range(count)]),
            ],
            axis=dim,
        )
    return cells


def lagrange_taps(starts, first_out):
    sample_count = starts.shape[0]
    sample = first_out + jnp.arange(sample_count, dtype=jnp.int32)
    excess = sample // 4 - 2 - starts
    offset_u = (sample % 4).astype(jnp.float32) * 0.25 + 2.125 + excess.astype(jnp.float32)
    basis = []
    for node in range(6):
        value = jnp.ones_like(offset_u)
        for other in range(6):
            if other != node:
                value = value * (offset_u - other) / (node - other)
        basis.append(value)
    zeros = jnp.zeros_like(offset_u)
    stacked = []
    for offset in range(7):
        lower = basis[offset - 1] if offset >= 1 else zeros
        upper = basis[offset] if offset <= 5 else zeros
        stacked.append(jnp.where(excess == 0, lower, upper))
    return jnp.stack(stacked).reshape(7, sample_count // 4, 4)


def interpolate(window, tap_weights):
    block_len = tap_weights.shape[1]
    leading = window.shape[:-1]
    flat_rows = window.reshape((-1, window.shape[-1]))
    row_count = flat_rows.shape[0]
    if block_len % 64 == 0 and block_len > 64:
        group = 64
    else:
        group = block_len
    blocks = block_len // group
    taps = tap_weights.reshape(7, blocks, 4 * group)
    if blocks == 1:
        band_rows = flat_rows.shape[1]
        paired = flat_rows[:, None, :]
    else:
        band_rows = 2 * group
        extended = jnp.pad(flat_rows, ((0, 0), (0, (blocks + 1) * group - flat_rows.shape[1])))
        split_rows = extended.reshape(row_count, blocks + 1, group)
        paired = jnp.concatenate([split_rows[:, :-1], split_rows[:, 1:]], axis=2)
    column = jnp.arange(band_rows, dtype=jnp.int32)[None, :, None]
    target = (jnp.arange(4 * group, dtype=jnp.int32) // 4)[None, None, :]
    offsets = jnp.arange(7, dtype=jnp.int32)[:, None, None]
    onehot = (column == target + offsets).astype(jnp.float32)
    band = jnp.einsum("kcj,kbj->bcj", onehot, taps, precision=lax.Precision.HIGHEST)
    total = jnp.einsum(
        "rbc,bcj->rbj", paired.astype(jnp.float32), band, precision=lax.Precision.HIGHEST
    )
    return total.reshape(leading + (4 * block_len,)).astype(jnp.bfloat16)


def directions(first_out, sample_count):
    sample = first_out + jnp.arange(sample_count, dtype=jnp.int32)
    cycles = K2 // 256
    azimuth = 2.0 * math.pi * ((sample % 256).astype(jnp.float32) + 0.5) / 256.0
    polar = math.pi * ((sample // 256).astype(jnp.float32) + 0.5) / cycles
    return (jnp.sin(polar) * jnp.cos(azimuth), jnp.sin(polar) * jnp.sin(azimuth), jnp.cos(polar))


def child_phase(octant, dir_x, dir_y, dir_z):
    sign_x = (octant % 2 * 2 - 1).astype(jnp.float32)
    sign_y = (octant // 2 % 2 * 2 - 1).astype(jnp.float32)
    sign_z = (octant // 4 * 2 - 1).astype(jnp.float32)
    return (
        2.0
        * math.pi
        * 2.0
        * (sign_x[:, None] * dir_x + sign_y[:, None] * dir_y + sign_z[:, None] * dir_z)
    )


def shift_children(pattern, octant, dir_x, dir_y, dir_z):
    angle = child_phase(octant, dir_x, dir_y, dir_z)
    cosine = jnp.cos(angle)[:, None, :]
    sine_part = jnp.sin(angle)[:, None, :]
    real_part = pattern[:, 0].astype(jnp.float32)
    imag_part = pattern[:, 1].astype(jnp.float32)
    return jnp.stack(
        [cosine * real_part - sine_part * imag_part, sine_part * real_part + cosine * imag_part],
        axis=1,
    )


def exchanged(child_pattern, child_parent, child_octant, parent_center, stencil_start):
    n_wide = lax.axis_size("wide")
    box_count, _, sources, block_one = child_pattern.shape
    block_two = 4 * block_one
    piece_len = block_one // n_wide
    narrow_at = lax.axis_index("narrow")
    wide_at = lax.axis_index("wide")
    out_first = narrow_at * block_two + wide_at * (4 * piece_len)
    parent_count = parent_center.shape[0]
    parent_ids = jnp.arange(parent_count, dtype=jnp.int32)
    dir_x, dir_y, dir_z = directions(out_first, 4 * piece_len)
    padded = with_halo(child_pattern, (("narrow", 3),), 3)
    shape_pieces = (box_count, 2, sources, n_wide, piece_len)
    left_rim = padded[..., 0:block_one].reshape(shape_pieces)[..., :3]
    middle = padded[..., 3 : 3 + block_one].reshape(shape_pieces)
    right_rim = padded[..., 6 : 6 + block_one].reshape(shape_pieces)[..., piece_len - 3 :]
    windows = jnp.concatenate([left_rim, middle, right_rim], axis=-1)
    starts = lax.dynamic_slice_in_dim(stencil_start, out_first, 4 * piece_len)
    tap_weights = lagrange_taps(starts, out_first)
    gathered = interpolate(
        lax.all_to_all(windows, "wide", split_axis=3, concat_axis=0, tiled=True)[:, :, :, 0, :],
        tap_weights,
    )
    shifted = shift_children(gathered, child_octant, dir_x, dir_y, dir_z)
    selector = (child_parent[:, None] == parent_ids[None, :]).astype(jnp.float32)
    parents_total = jnp.einsum("bp,bcrj->pcrj", selector, shifted, precision=lax.Precision.HIGHEST)
    center_angle = (
        2.0
        * math.pi
        * (
            parent_center[:, 0:1] * dir_x
            + parent_center[:, 1:2] * dir_y
            + parent_center[:, 2:3] * dir_z
        )
    )
    center_cos = jnp.cos(center_angle)
    center_sin = jnp.sin(center_angle)
    real_sum = jnp.einsum(
        "pj,prj->rj", center_cos, parents_total[:, 0], precision=lax.Precision.HIGHEST
    ) - jnp.einsum("pj,prj->rj", center_sin, parents_total[:, 1], precision=lax.Precision.HIGHEST)
    imag_sum = jnp.einsum(
        "pj,prj->rj", center_sin, parents_total[:, 0], precision=lax.Precision.HIGHEST
    ) + jnp.einsum("pj,prj->rj", center_cos, parents_total[:, 1], precision=lax.Precision.HIGHEST)
    far_field = jnp.stack([real_sum, imag_sum]) / math.sqrt(parent_count)
    parent_pattern = parents_total[:, :, :, None, :]
    return (parent_pattern, far_field[:, :, None, :])


LANES = 128
HALO = 3
RIM = 16


def stencil_tables(window, columns):
    tables = np.zeros((2, window, columns), np.float32)
    for excess in range(2):
        for column in range(columns):
            offset_u = np.float32((column % 4) * 0.25 + 2.125 + excess)
            first = window // 4 + column // 4 - 2 - excess
            for node in range(6):
                value = np.float32(1.0)
                for other in range(6):
                    if other != node:
                        value = np.float32(
                            value * np.float32(np.float32(offset_u - np.float32(other)) / np.float32(node - other))
                        )
                tables[excess, first + node, column] = value
    high = tables.astype(ml_dtypes.bfloat16)
    low = (tables - high.astype(np.float32)).astype(ml_dtypes.bfloat16)
    return np.concatenate([high, low], axis=1)


def rim_masks():
    slot = lax.broadcasted_iota(jnp.int32, (RIM, LANES), 0)
    lane = lax.broadcasted_iota(jnp.int32, (RIM, LANES), 1)
    return slot, lane


def as_mask(condition):
    return jnp.where(condition, 1.0, 0.0).astype(jnp.bfloat16)


def rim_of(before, after, first_slot):
    slot, lane = rim_masks()
    slot = slot - first_slot
    pick_before = as_mask((slot >= 0) & (slot < HALO) & (lane == LANES - HALO + slot))
    pick_after = as_mask((slot >= HALO) & (slot < 2 * HALO) & (lane == slot - HALO))
    across = (((1,), (1,)), ((), ()))
    rim = lax.dot_general(pick_before, before, across, preferred_element_type=jnp.float32)
    return rim + lax.dot_general(pick_after, after, across, preferred_element_type=jnp.float32)


def first_pack_kernel(step, members, piece, cells, *refs):
    far = members - 2
    outs, edge, ends, sems = refs[:far], refs[far], refs[far + 1], refs[far + 2]
    block = cells.shape[3]
    wide_at = lax.axis_index("wide")
    group_at, member_at = wide_at // members, wide_at % members
    copies = []
    for swap in range(far):
        first = ((group_at ^ step) * members + (member_at ^ (swap + 2))) * piece
        at = pl.ds(pl.multiple_of(first, LANES), piece)
        copies.append(pltpu.make_async_copy(cells.at[:, :, :, at], outs[swap], sems.at[swap]))
    for index, at in enumerate((block - LANES, 0)):
        copies.append(
            pltpu.make_async_copy(cells.at[:, :, :, pl.ds(at, LANES)], ends.at[index], sems.at[far + index])
        )
    for copy in copies:
        copy.start()
    for copy in copies[far:]:
        copy.wait()
    rows = ends.shape[1] * ends.shape[2] * ends.shape[3]
    edge[...] = rim_of(ends[0].reshape(rows, LANES), ends[1].reshape(rows, LANES), 2 * HALO).astype(jnp.bfloat16)
    for copy in copies[:far]:
        copy.wait()


def rest_pack_kernel(groups, members, piece, cells, near, edge, near_edge, *outs):
    boxes, parts, sources, block = cells.shape
    rows = boxes * parts * sources
    tiles = piece // LANES
    wide_at = lax.axis_index("wide")
    group_at, member_at = wide_at // members, wide_at % members

    def tile(ref, at):
        return ref[:, :, :, pl.ds(pl.multiple_of(at, LANES), LANES)].reshape(rows, LANES)

    def rim_at(ref, first):
        return rim_of(tile(ref, jnp.maximum(first - LANES, 0)), tile(ref, jnp.minimum(first + piece, block - LANES)), 0)

    for part in range(1, groups):
        for swap in range(2, members, 2):
            out, base = outs[(part - 1) * (members // 2 - 1) + swap // 2 - 1], 0
            target = member_at ^ swap
            first = ((group_at ^ (groups - 1 - part)) * members + target) * piece
            for ref, rim_edge in ((cells, edge), (near, near_edge)):
                for index in range(tiles):
                    out[base : base + rows, :] = tile(ref, first + index * LANES)
                    base += rows
                out[base : base + RIM, :] = rim_at(ref, first).astype(jnp.bfloat16)
                base += RIM
                if part == 1:
                    rim = rim_at(ref, ((group_at ^ (groups - 1)) * members + target) * piece)
                    out[base : base + RIM, :] = (rim + rim_edge[...].astype(jnp.float32)).astype(jnp.bfloat16)
                    base += RIM


def prep_kernel(groups, members, boxes, piece, parent_of, octant_of, center, starts, cosines, sines, center_cos, center_sin, excess):
    wide_at = lax.axis_index("wide")
    narrow_at = lax.axis_index("narrow")
    group_at, member_at = wide_at // members, wide_at % members
    rows = 4 * piece // LANES
    all_rows = starts.shape[0]
    half_rows = all_rows // lax.axis_size("narrow")
    cycles = all_rows * LANES // 256
    row = lax.broadcasted_iota(jnp.int32, (rows, LANES), 0)
    lane = lax.broadcasted_iota(jnp.int32, (rows, LANES), 1)

    def place(group):
        first_row = narrow_at * half_rows + (group * members + member_at) * rows
        sample = (first_row + row) * LANES + lane
        azimuth = 2.0 * math.pi * ((sample & 255).astype(jnp.float32) + 0.5) / 256.0
        polar = math.pi * ((sample >> 8).astype(jnp.float32) + 0.5) / cycles
        sin_polar = jnp.sin(polar)
        return first_row, sample, sin_polar * jnp.cos(azimuth), sin_polar * jnp.sin(azimuth), jnp.cos(polar)

    for step in range(groups):
        first_row, sample, dir_x, dir_y, dir_z = place(group_at ^ step)
        here = starts[pl.ds(pl.multiple_of(first_row, 8), rows), :]
        excess[step] = ((sample >> 2) - 2 - here).astype(jnp.float32)
        for swap in range(members):
            for box in range(boxes):
                slot = (group_at * members + (member_at ^ swap)) * boxes + box
                octant = octant_of[slot]
                live = jnp.where(parent_of[slot] >= 0, 1.0, 0.0)
                sign_x = ((octant & 1) * 2 - 1).astype(jnp.float32)
                sign_y = (((octant >> 1) & 1) * 2 - 1).astype(jnp.float32)
                sign_z = ((octant >> 2) * 2 - 1).astype(jnp.float32)
                angle = 4.0 * math.pi * (sign_x * dir_x + sign_y * dir_y + sign_z * dir_z)
                cosines[step, swap * boxes + box] = jnp.cos(angle) * live
                sines[step, swap * boxes + box] = jnp.sin(angle) * live
    _, _, dir_x, dir_y, dir_z = place(group_at)
    scale = 1.0 / math.sqrt(center.shape[0])
    for parent in range(center.shape[0]):
        turns = center[parent, 0] * dir_x + center[parent, 1] * dir_y + center[parent, 2] * dir_z
        angle = 2.0 * math.pi * turns
        center_cos[parent] = jnp.cos(angle) * scale
        center_sin[parent] = jnp.sin(angle) * scale


def columns_of(windows, tiles):
    return [c for w in windows for c in range(max(0, 4 * w + 2), min(4 * tiles, 4 * w + 6))]


def combine_kernel(jobs, members, boxes, sources, tiles, count, *refs):
    data = refs[:count]
    cosines, sines, excess, band_zero, band_one = refs[count : count + 5]
    outs = refs[count + 5 : count + 5 + len(jobs)]
    spread, total = refs[count + 5 + len(jobs) :]
    for (step, *job), out in zip(jobs, outs):
        combine(
            step, *job, members, boxes, sources, tiles, data, cosines.at[step], sines.at[step], excess.at[step],
            band_zero, band_one, out, spread, total,
        )


def combine(
    step, windows, places, rims, members, boxes, sources, tiles, data, cosines, sines, excess, band_zero, band_one, out, spread, total
):
    rows = boxes * 2 * sources
    block = data[0].shape[3]
    wide_at = lax.axis_index("wide")
    last = lax.axis_size("wide") - 1
    at = ((wide_at // members) ^ step) * members + wide_at % members
    first = at * (tiles * LANES)

    def local(ref, lane):
        return ref[:, :, :, pl.ds(pl.multiple_of(lane, LANES), LANES)].reshape(rows, LANES)

    def tile(index):
        if index < 0 or index >= tiles:
            return rim_tile
        found = [local(data[member], first + index * LANES) for member in range(2)]
        for which, base in places:
            ref = data[which]
            if len(ref.shape) == 4:
                found.append(ref[:, :, :, index * LANES : (index + 1) * LANES].reshape(rows, LANES))
            else:
                found.append(ref[base + index * rows : base + (index + 1) * rows, :])
        return jnp.concatenate(found, axis=0)

    if rims is not None:
        slot, lane = rim_masks()
        from_other = slot >= 2 * HALO
        side = jnp.where(from_other, slot - 2 * HALO, slot)
        outer = ((side < HALO) & (at == 0)) | ((side >= HALO) & (at == last))
        keep = (outer == from_other) & (slot < 4 * HALO)
        place = as_mask(
            ((side < HALO) & (lane == LANES - HALO + side)) | ((side >= HALO) & (side < 2 * HALO) & (lane == side - HALO))
        )
        found = []
        for inner, (other, other_row) in rims:
            outside = data[other][other_row : other_row + RIM, :].astype(jnp.float32)
            if inner is None:
                inside = jnp.zeros((RIM, LANES), jnp.float32)
            else:
                inside = data[inner[0]][inner[1] : inner[1] + RIM, :].astype(jnp.float32)
            found.append(jnp.where(keep, jnp.where(from_other, outside, inside), 0.0).astype(jnp.bfloat16))
        rim = jnp.concatenate(found, axis=1)
        rim_tile = lax.dot_general(rim, place, (((0,), (0,)), ((), ())), preferred_element_type=jnp.float32)
        lane = lax.broadcasted_iota(jnp.int32, (rows, LANES), 1)
        from_before = (lane >= LANES - HALO) & (at != 0)
        from_after = (lane < HALO) & (at != last)
        near = []
        for member in range(2):
            before = local(data[member], jnp.maximum(first - LANES, 0)).astype(jnp.float32)
            after = local(data[member], jnp.minimum(first + tiles * LANES, block - LANES)).astype(jnp.float32)
            near.append(jnp.where(from_before, before, jnp.where(from_after, after, 0.0)))
        near = jnp.concatenate(near, axis=0)
        rim_tile = jnp.concatenate([rim_tile[: 2 * rows] + near, rim_tile[2 * rows :]], axis=0).astype(jnp.bfloat16)

    columns = columns_of(windows, tiles)
    width = len(columns)
    for turn, window in enumerate(windows):
        mine = columns_of([window], tiles)
        left, right = tile(window), tile(window + 1)
        cells = jnp.concatenate([left, right, left, right], axis=1)
        bands = []
        for column in mine:
            at_column = (column + 2) % 4 * LANES
            which = jnp.broadcast_to(excess[column : column + 1, :], (16, LANES)).astype(jnp.bfloat16)
            which = jnp.concatenate([which] * (band_zero.shape[0] // 16), axis=0)
            zero = band_zero[:, at_column : at_column + LANES]
            one = band_one[:, at_column : at_column + LANES]
            bands.append(zero * (1 - which) + one * which)
        band = jnp.concatenate(bands, axis=1)
        buffer = spread.at[turn % 2]
        buffer[:, : len(mine) * LANES] = jnp.dot(cells, band, preferred_element_type=jnp.float32)
        for number, column in enumerate(mine):
            lanes = slice(number * LANES, (number + 1) * LANES)
            real_sum = jnp.zeros((sources, LANES), jnp.float32)
            imag_sum = jnp.zeros((sources, LANES), jnp.float32)
            for child in range(members * boxes):
                start = child * 2 * sources
                real = buffer[start : start + sources, lanes].astype(jnp.bfloat16).astype(jnp.float32)
                imag = buffer[start + sources : start + 2 * sources, lanes].astype(jnp.bfloat16).astype(jnp.float32)
                cosine = cosines[child, column : column + 1, :]
                sine = sines[child, column : column + 1, :]
                real_sum = real_sum + (cosine * real - sine * imag)
                imag_sum = imag_sum + (sine * real + cosine * imag)
            at_row = columns.index(column)
            total[pl.ds(at_row, sources, stride=width), :] = real_sum
            total[pl.ds(sources * width + at_row, sources, stride=width), :] = imag_sum
    out[...] = total[: 2 * sources * width, :].astype(out.dtype)


def spans_of(columns):
    spans, begin = [], 0
    for i in range(1, len(columns) + 1):
        if i == len(columns) or columns[i] != columns[i - 1] + 1:
            spans.append((begin, columns[begin], i - begin))
            begin = i
    return spans


def finish_kernel(last, pieces, members, boxes, sources, rows, parent_of, *refs):
    arrived, refs = refs[: len(pieces)], refs[len(pieces) :]
    if last:
        center_cos, center_sin, far_in, _, parent_out, far_out, held, sems = refs
    else:
        center_cos, center_sin, parent_out, far_out = refs
    group_at = lax.axis_index("wide") // members
    names = [parent_of[(group_at ^ step) * members * boxes] for step, _ in pieces]
    turns = [(center_cos[name], center_sin[name]) for name in names]
    copies = []
    for source in range(sources):
        real_all, imag_all = (pl.ds((part * sources + source) * rows, rows) for part in range(2))
        if last:
            real_sum, imag_sum = far_in[real_all, :], far_in[imag_all, :]
        for piece, (step, columns) in enumerate(pieces):
            width = len(columns)
            for begin, column, length in spans_of(columns):
                real = arrived[piece][pl.ds(source * width + begin, length), :].astype(jnp.float32)
                imag = arrived[piece][pl.ds((sources + source) * width + begin, length), :].astype(jnp.float32)
                cosine, sine = (turn[column : column + length, :] for turn in turns[piece])
                real_at = pl.ds(source * rows + column, length)
                imag_at = pl.ds((sources + source) * rows + column, length)
                real_turned = cosine * real - sine * imag
                imag_turned = sine * real + cosine * imag
                if last:
                    held[piece, real_at, :] = real
                    held[piece, imag_at, :] = imag
                    real_sum = real_sum + real_turned
                    imag_sum = imag_sum + imag_turned
                else:
                    parent_out[names[piece], real_at, :] = real
                    parent_out[names[piece], imag_at, :] = imag
                    if piece == 0:
                        far_out[real_at, :] = real_turned
                        far_out[imag_at, :] = imag_turned
                    else:
                        far_out[real_at, :] += real_turned
                        far_out[imag_at, :] += imag_turned
        if last:
            far_out[real_all, :] = real_sum
            far_out[imag_all, :] = imag_sum
            if source % (sources // 2) == sources // 2 - 1:
                half = source // (sources // 2)
                size = sources // 2 * rows
                for piece in range(len(pieces)):
                    for part in range(2):
                        at = pl.ds(part * sources * rows + half * size, size)
                        copies.append(
                            pltpu.make_async_copy(
                                held.at[piece, at], parent_out.at[names[piece], at], sems.at[(half * len(pieces) + piece) * 2 + part]
                            )
                        )
                        copies[-1].start()
    for copy in copies:
        copy.wait()


def grouped(child_pattern, child_parent, child_octant, parent_center, stencil_start, members):
    n_wide = lax.axis_size("wide")
    boxes, _, sources, block = child_pattern.shape
    groups = n_wide // members
    piece = block // n_wide
    tiles = piece // LANES
    rows = boxes * 2 * sources
    out_rows = 4 * tiles
    parents = parent_center.shape[0]
    vmem = pl.BlockSpec(memory_space=pltpu.VMEM)
    smem = pl.BlockSpec(memory_space=pltpu.SMEM)
    hbm = pl.BlockSpec(memory_space=pltpu.HBM)
    limit = pltpu.CompilerParams(vmem_limit_bytes=16 * 1024 * 1024)

    def cost(micros):
        return pl.CostEstimate(flops=int(micros * 1e9), bytes_accessed=int(micros * 3.6e6) + 1, transcendentals=0)


    def bf16(*shape):
        return jax.ShapeDtypeStruct(shape, jnp.bfloat16)

    def f32(*shape):
        return jax.ShapeDtypeStruct(shape, jnp.float32)

    def swap_with(array, step):
        return lax.ppermute(array, "wide", [(i, i ^ step) for i in range(n_wide)])

    def tie(*arrays):
        return lax.optimization_barrier(arrays)

    far = members - 2
    *heads, edge = pl.pallas_call(
        functools.partial(first_pack_kernel, groups - 1, members, piece),
        out_shape=[bf16(boxes, 2, sources, piece)] * far + [bf16(RIM, LANES)],
        in_specs=[hbm],
        out_specs=[vmem] * (far + 1),
        scratch_shapes=[
            pltpu.VMEM((2, boxes, 2, sources, LANES), jnp.bfloat16),
            pltpu.SemaphoreType.DMA((members,)),
        ],
        compiler_params=pltpu.CompilerParams(vmem_limit_bytes=16 * 1024 * 1024),
        cost_estimate=cost(0),
        name="pack_first",
    )(child_pattern)
    near = swap_with(child_pattern, 1)
    heads = [swap_with(head, swap + 2) for swap, head in enumerate(heads)]

    def other_half(array, step):
        pairs = [(i * 2 + n, (i ^ step) * 2 + 1 - n) for i in range(n_wide) for n in range(2)]
        return lax.ppermute(array, ("wide", "narrow"), pairs)

    near_edge = other_half(edge, 1)
    edge = other_half(edge, 0)
    tables = pl.pallas_call(
        functools.partial(prep_kernel, groups, members, boxes, piece),
        out_shape=[
            f32(groups, members * boxes, out_rows, LANES),
            f32(groups, members * boxes, out_rows, LANES),
            f32(parents, out_rows, LANES),
            f32(parents, out_rows, LANES),
            f32(groups, out_rows, LANES),
        ],
        in_specs=[smem, smem, smem, vmem],
        out_specs=[vmem] * 5,
        compiler_params=limit,
            cost_estimate=cost(0),
        name="prep",
    )(child_parent, child_octant, parent_center, stencil_start.reshape(-1, LANES))
    cosines, sines, center_cos, center_sin, excess = tables
    edge, excess = tie(edge, excess)
    full = tiles * rows + RIM
    pairs = members // 2 - 1
    sends = list(pl.pallas_call(
        functools.partial(rest_pack_kernel, groups, members, piece),
        out_shape=[
            bf16(2 * (full + (RIM if part == 1 else 0)), LANES) for part in range(1, groups) for _ in range(pairs)
        ],
        in_specs=[vmem] * 4,
        out_specs=[vmem] * ((groups - 1) * pairs),
        compiler_params=limit,
        cost_estimate=cost(0),
        name="pack_rest",
    )(child_pattern, near, edge, near_edge))
    bands = stencil_tables(2 * LANES, 4 * LANES)

    def sums_of(jobs, data, dtype, micros):
        shapes = [jax.ShapeDtypeStruct((2 * sources * len(columns_of(job[1], tiles)), LANES), dtype) for job in jobs]
        inputs = [*data, cosines, sines, excess, bands[0], bands[1]]
        return pl.pallas_call(
            functools.partial(combine_kernel, jobs, members, boxes, sources, tiles, len(data)),
            out_shape=shapes,
            in_specs=[vmem] * len(inputs),
            out_specs=[vmem] * len(jobs),
            scratch_shapes=[
                pltpu.VMEM((2, members * rows, 4 * LANES), jnp.float32),
                pltpu.VMEM((2 * sources * out_rows, LANES), jnp.float32),
            ],
            compiler_params=limit,
            cost_estimate=cost(micros),
            name="combine",
        )(*inputs)

    top = groups - 1
    inner = list(range(tiles - 1))
    outer = [-1, tiles - 1]
    every = list(range(-1, tiles))
    locals_ = [child_pattern, near]
    first_data = locals_ + heads
    first_places = [(2 + member, 0) for member in range(far)]
    (total,) = sums_of([(top, inner, first_places, None)], first_data, jnp.bfloat16, 5)
    early_sends = sends[pairs : 2 * pairs]
    *early_sends, total = tie(*early_sends, total)
    sends[pairs : 2 * pairs] = early_sends
    done = [swap_with(total, top * members)]
    arrived = {}
    for part in range(1, groups):
        step = top - part
        sent = sends[(part - 1) * pairs : part * pairs]
        if part == 3:
            data[0], done[0] = tie(data[0], done[0])
        if part > 1:
            totals = sums_of(jobs, data, jnp.bfloat16, 30)
            if part < groups - 1:
                tied = tie(*sends[part * pairs : (part + 1) * pairs], *totals)
                sends[part * pairs : (part + 1) * pairs], totals = tied[:pairs], tied[pairs:]
            arrived[step + 1] = swap_with(totals[0], (step + 1) * members)
            if part == 2:
                done.append(swap_with(totals[1], top * members))
        got = [swap_with(array, 2 * pair + 2) for pair, array in enumerate(sent)]
        length = full + (RIM if part == 1 else 0)
        places = [(2 + member // 2, member % 2 * length) for member in range(far)]
        if part == 1:
            rest = got + [edge, near_edge]
            far_rims = [(which - 2, row + full) for which, row in places]
        shift = 2 + pairs if part > 1 else 2
        data = locals_ + (got if part > 1 else []) + rest
        rims = [(None, (shift + pairs + member, 0)) for member in range(2)]
        rims += [
            ((which, row + tiles * rows), (shift + other, other_row))
            for (which, row), (other, other_row) in zip(places, far_rims)
        ]
        jobs = [(step, every, places, rims)]
        if part == 1:
            outer_rims = [(None, (shift + pairs + member, 0)) for member in range(2)]
            outer_rims += [((shift + which, row),) * 2 for which, row in far_rims]
            outer_places = [(len(data) + member, 0) for member in range(far)]
            jobs.append((top, outer, outer_places, outer_rims))
            data = data + heads
    (arrived[0],) = sums_of(jobs, data, jnp.float32, 30)
    done = [(top, columns_of(inner, tiles), done[0]), (top, columns_of(outer, tiles), done[1])]
    held = arrived
    ahead = [(0, columns_of(every, tiles), held[0])] + done
    final = [(step, columns_of(every, tiles), held[step]) for step in sorted(held) if step]

    def finish(last, pieces, extra):
        shapes = [f32(parents, 2 * sources * out_rows, LANES), f32(2 * sources * out_rows, LANES)]
        return pl.pallas_call(
            functools.partial(
                finish_kernel, last, [(step, columns) for step, columns, _ in pieces], members, boxes, sources, out_rows
            ),
            out_shape=shapes,
            in_specs=[smem] + [vmem] * (len(pieces) + 2) + ([vmem, hbm] if last else []),
            out_specs=[hbm if last else vmem, vmem],
            input_output_aliases={len(pieces) + 4: 0} if last else {},
            scratch_shapes=[
                pltpu.VMEM((len(pieces),) + shapes[1].shape, jnp.float32),
                pltpu.SemaphoreType.DMA((4 * len(pieces),)),
            ]
            if last
            else [],
            compiler_params=limit,
            cost_estimate=cost(0 if last else 30),
            name="finish_last" if last else "finish_ahead",
        )(child_parent, *[array for _, _, array in pieces], center_cos, center_sin, *extra)

    parent_pattern, far_field = finish(False, ahead, [])
    parent_pattern, far_field = finish(True, final, [far_field, parent_pattern])
    return (
        parent_pattern.reshape(parents, 2, sources, 1, 4 * piece),
        far_field.reshape(2, sources, 1, 4 * piece),
    )


def power_of_two(number):
    return number > 0 and number & (number - 1) == 0


def per_device(child_pattern, child_parent, child_octant, parent_center, stencil_start):
    n_wide, n_narrow = lax.axis_size("wide"), lax.axis_size("narrow")
    boxes, _, sources, block = child_pattern.shape
    parents = parent_center.shape[0]
    run = child_parent.shape[0] // parents
    if run % boxes == 0 and block % n_wide == 0:
        members = run // boxes
        fits = (
            n_narrow == 2
            and n_wide == members * parents
            and power_of_two(members)
            and power_of_two(parents)
            and members >= 4
            and parents >= 4
            and block // n_wide % LANES == 0
            and block // n_wide // LANES >= 3
            and boxes * 2 * sources == LANES
            and sources % 16 == 0
            and stencil_start.shape[0] == 4 * block * n_narrow
        )
        if fits:
            return grouped(child_pattern, child_parent, child_octant, parent_center, stencil_start, members)
    return exchanged(child_pattern, child_parent, child_octant, parent_center, stencil_start)


def solution(mesh):
    in_specs = (P("wide", None, None, "narrow"), P(), P(), P(), P())
    out_specs = (P(None, None, None, "narrow", "wide"), P(None, None, "narrow", "wide"))
    return jax.shard_map(
        per_device, mesh=mesh, in_specs=in_specs, out_specs=out_specs, check_vma=False
    )
```

time: 61.5 us -> 49.2 us (0.80)
  waiting for transfers between devices: 24.5 us -> 11.5 us
  starting transfers between devices: 20.8 us -> 18.3 us
  Pallas kernels: 13.6 us -> 15.8 us
  local copies, waits for them, and re-layouts: 1.7 us -> 2.56 us
    ppermute x4 -> x2, waiting for transfers between devices: 8.21 us -> 0.06 us  [other_half(): return lax.ppermute(array, ('wide', 'narrow'), pairs)]
    ppermute x4 -> x2, starting transfers between devices: 6.97 us -> 1.64 us  [other_half(): return lax.ppermute(array, ('wide', 'narrow'), pairs)]
    ppermute x15 -> x10, waiting for transfers between devices: 16.2 us -> 11.5 us  [swap_with(): return lax.ppermute(array, 'wide', [(i, i ^ step) for i in range(n_wide)])]
    ppermute x15 -> x10, starting transfers between devices: 13.9 us -> 16.7 us  [swap_with(): return lax.ppermute(array, 'wide', [(i, i ^ step) for i in range(n_wide)])]
    pallas_call x6 -> x8, Pallas kernels: 11.6 us -> 13.9 us  [the longest x4 8.44 us: sums_of(): pl.pallas_call(functools.partial(combine_kernel, jobs, members, boxes, so...]
    unnamed x14 -> x16, local copies, waits for them, and re-layouts: 1.7 us -> 2.56 us
  transfers between devices with their start and end apart: 19 -> 12, of which waited for: 8 -> 5; matrix products, arithmetic and copies ran while one was open for 0% -> 0% of each run, Pallas kernels for 16% -> 27%
where the time goes in v2:
time: 49.2 us; the launch traced here: 49 us
  starting transfers between devices  18.3 us (37%)
  Pallas kernels  15.8 us (32%)
  waiting for transfers between devices  11.5 us (23%)
  local copies, waits for them, and re-layouts  2.56 us (5%)
  between operations  0.75 us (2%)
    ppermute x10, starting transfers between devices, swap_with(): return lax.ppermute(array, 'wide', [(i, i ^ step) for i in range(n_wide)])  16.7 us
    ppermute x10, waiting for transfers between devices, swap_with(): return lax.ppermute(array, 'wide', [(i, i ^ step) for i in range(n_wide)])  11.5 us
    pallas_call x4, Pallas kernels, sums_of(): pl.pallas_call(functools.partial(combine_kernel, jobs, members, boxes, so...  8.44 us
    pallas_call x2, Pallas kernels, finish(): pl.pallas_call(functools.partial(finish_kernel, last, [(step, columns) fo...  4.67 us
    unnamed x16, local copies, waits for them, and re-layouts  2.56 us
    pallas_call x1, Pallas kernels, grouped(): pl.pallas_call(functools.partial(prep_kernel, groups, members, boxes, pie...  1.96 us
    ppermute x2, starting transfers between devices, other_half(): return lax.ppermute(array, ('wide', 'narrow'), pairs)  1.64 us
  transfers between devices with their start and end apart: 12, of which 5 were waited for; matrix products, arithmetic and copies ran while one was open for 0% of the time, Pallas kernels for 27%

profile of v2, /device:TPU:0, one launch (start us, length us, event | category | flops | bytes accessed | tf_op | source)
XLA Modules:
  0.0 49.0 jit_solution(5685078398145844206)
XLA Ops:
  0.6 0.5 %collective-permute-start = (bf16[2,2,32,8192]{3,2,1,0:T(8,128)(2,1)}, bf16[2,2,32,8192]{3,2,1,0:T(8,128)(2,1)S(1)}, u32[]{:S(2)}, u32[]{:S(2)}) collective-permute-start(bf16[2,2,32,8192]{3,2,1,0:T(8,128)(2,1)} %refs_0_.6), channel_id=1, source_target_pairs={{0,2},{2,0},{4,6},{6,4},{8,10},{10,8},{12,14},{14,12},{16,18},{18,... | collective-permute-start | bytes 6291464 | tf_op jit(solution)/shard_map/ppermute | solution.py:502
  1.1 0.0 copy-start
  1.2 1.6 %copy-done = bf16[2,2,32,8192]{3,2,1,0:T(8,128)(2,1)S(1)} copy-done((bf16[2,2,32,8192]{3,2,1,0:T(8,128)(2,1)S(1)}, bf16[2,2,32,8192]{3,2,1,0:T(8,128)(2,1)}, u32[]{:S(2)}) %copy-start) | copy-done | bytes 2097176
  2.7 0.0 copy-start.3
  2.7 0.0 copy-start.4
  2.7 0.0 copy-start.5
  2.8 0.3 pack_first.1
  3.0 2.6 %collective-permute-start.3 = (bf16[2,2,32,512]{3,2,1,0:T(8,128)(2,1)S(1)}, bf16[2,2,32,512]{3,2,1,0:T(8,128)(2,1)S(1)}, u32[]{:S(2)}, u32[]{:S(2)}) collective-permute-start(bf16[2,2,32,512]{3,2,1,0:T(8,128)(2,1)S(1)} %get-tuple-element.32), channel_id=1, source_target_pairs={{0,4},{2,6},{4,0},{6,2},{8,12},{10,14},{12,8},{14,10},{16,20},{18,... | collective-permute-start | bytes 393224 | tf_op jit(solution)/shard_map/ppermute | solution.py:502
  5.6 0.2 collective-permute-start.4
  5.8 1.6 %collective-permute-start.1 = (bf16[16,128]{1,0:T(8,128)(2,1)S(1)}, bf16[16,128]{1,0:T(8,128)(2,1)S(1)}, u32[]{:S(2)}, u32[]{:S(2)}) collective-permute-start(bf16[16,128]{1,0:T(8,128)(2,1)S(1)} %get-tuple-element.28), channel_id=1, source_target_pairs={{0,1},{1,0},{2,3},{3,2},{4,5},{5,4},{6,7},{7,6},{8,9},{9,8},{10,11... | collective-permute-start | bytes 12296 | tf_op jit(solution)/shard_map/ppermute | solution.py:526
  7.4 0.0 collective-permute-start.2
  7.4 0.0 copy-done.3
  7.4 0.0 copy-done.4
  7.5 0.0 copy-done.5
  7.5 0.0 copy-start.2
  7.5 0.9 %copy-done.2 = s32[65536]{0:T(1024)S(1)} copy-done((s32[65536]{0:T(1024)S(1)}, s32[65536]{0:T(1024)}, u32[]{:S(2)}) %copy-start.2) | copy-done | bytes 262168
  8.4 2.0 %prep.1 = (f32[4,8,16,128]{3,2,1,0:T(8,128)S(1)}, f32[4,8,16,128]{3,2,1,0:T(8,128)S(1)}, f32[4,16,128]{2,1,0:T(8,128)S(1)}, f32[4,16,128]{2,1,0:T(8,128)S(1)}, f32[4,16,128]{2,1,0:T(8,128)S(1)}) custom-call(s32[32]{0:T(128)S(1)} %copy-done.4, s32[32]{0:T(128)S(1)} %copy-done.5, f32[4,3]{1,0:T(4,128)S(1)} %copy-done.3, s32[512,128]{1,0:T(8,128)S(1)} %bitcast.3), custom_call_target="tpu_custom_call" | custom-call | bytes 1 | tf_op jit(solution)/shard_map/prep/pallas_call | solution.py:530
  10.4 0.0 collective-permute-done.1.edge.refs_4_.refs_3_
  10.4 0.0 copy-start.6
  10.4 0.0 copy-start.7
  10.4 0.1 collective-permute-done.2.near_edge.refs_5_.refs_4_
  10.5 0.0 collective-permute-done.near.refs_1_
  10.5 0.0 copy-done.1
  10.5 0.5 %pack_rest.1 = (bf16[1088,128]{1,0:T(8,128)(2,1)S(1)}, bf16[1056,128]{1,0:T(8,128)(2,1)S(1)}, bf16[1056,128]{1,0:T(8,128)(2,1)S(1)}) custom-call(bf16[2,2,32,8192]{3,2,1,0:T(8,128)(2,1)S(1)} %copy-done.1, bf16[2,2,32,8192]{3,2,1,0:T(8,128)(2,1)S(1)} %collective-permute-done.near.refs_1_, bf16[16,128]{1,0:T(8,128)(2,1)S(1)} %collective-permute-done.1.edge.refs_4_.refs_3_, ...), custom_call_target="tpu_custom_call" | custom-call | bytes 1 | tf_op jit(solution)/shard_map/pack_rest/pallas_call | solution.py:549
  11.0 1.7 %collective-permute-start.7 = (bf16[1088,128]{1,0:T(8,128)(2,1)S(1)}, bf16[1088,128]{1,0:T(8,128)(2,1)S(1)}, u32[]{:S(2)}, u32[]{:S(2)}) collective-permute-start(bf16[1088,128]{1,0:T(8,128)(2,1)S(1)} %get-tuple-element.40), channel_id=1, source_target_pairs={{0,4},{2,6},{4,0},{6,2},{8,12},{10,14},{12,8},{14,10},{16,20},{18,... | collective-permute-start | bytes 835592 | tf_op jit(solution)/shard_map/ppermute | solution.py:502
  12.6 0.0 collective-permute-done.3.refs_2_.refs_5_
  12.6 0.0 collective-permute-done.4.refs_3_.refs_6_
  12.7 0.0 copy-done.6
  12.7 0.0 copy-done.7
  12.7 1.5 %combine.4 = bf16[768,128]{1,0:T(8,128)(2,1)S(1)} custom-call(bf16[2,2,32,8192]{3,2,1,0:T(8,128)(2,1)S(1)} %copy-done.1, bf16[2,2,32,8192]{3,2,1,0:T(8,128)(2,1)S(1)} %collective-permute-done.near.refs_1_, bf16[2,2,32,512]{3,2,1,0:T(8,128)(2,1)S(1)} %collective-permute-done.3.refs_2_.refs_5_, ...), custom_call_target="tpu_custom_call" | custom-call | flops 5000000000 | bytes 18000000 | tf_op jit(solution)/shard_map/combine/pallas_call | solution.py:565
  14.2 3.7 %collective-permute-start.5 = (bf16[768,128]{1,0:T(8,128)(2,1)S(1)}, bf16[768,128]{1,0:T(8,128)(2,1)S(1)}, u32[]{:S(2)}, u32[]{:S(2)}) collective-permute-start(bf16[768,128]{1,0:T(8,128)(2,1)S(1)} %combine.4), channel_id=1, source_target_pairs={{0,24},{2,26},{4,28},{6,30},{8,16},{10,18},{12,20},{14,22},{16,8},... | collective-permute-start | bytes 589832 | tf_op jit(solution)/shard_map/ppermute | solution.py:502
  17.9 1.3 %collective-permute-start.6 = (bf16[1056,128]{1,0:T(8,128)(2,1)S(1)}, bf16[1056,128]{1,0:T(8,128)(2,1)S(1)}, u32[]{:S(2)}, u32[]{:S(2)}) collective-permute-start(bf16[1056,128]{1,0:T(8,128)(2,1)S(1)} %get-tuple-element.39), channel_id=1, source_target_pairs={{0,4},{2,6},{4,0},{6,2},{8,12},{10,14},{12,8},{14,10},{16,20},{18,... | collective-permute-start | bytes 811016 | tf_op jit(solution)/shard_map/ppermute | solution.py:502
  19.1 4.1 %collective-permute-done.5.refs_1_ = bf16[768,128]{1,0:T(8,128)(2,1)S(1)} collective-permute-done((bf16[768,128]{1,0:T(8,128)(2,1)S(1)}, bf16[768,128]{1,0:T(8,128)(2,1)S(1)}, u32[]{:S(2)}, u32[]{:S(2)}) %collective-permute-start.5) | collective-permute-done | bytes 196640 | tf_op jit(solution)/shard_map/ppermute | solution.py:502
  23.3 0.0 collective-permute-done.7.refs_3_.refs_2_
  23.3 2.8 %combine.6 = (bf16[1024,128]{1,0:T(8,128)(2,1)S(1)}, bf16[256,128]{1,0:T(8,128)(2,1)S(1)}) custom-call(bf16[2,2,32,8192]{3,2,1,0:T(8,128)(2,1)S(1)} %copy-done.1, bf16[2,2,32,8192]{3,2,1,0:T(8,128)(2,1)S(1)} %collective-permute-done.near.refs_1_, bf16[1088,128]{1,0:T(8,128)(2,1)S(1)} %collective-permute-done.7.refs_3_.refs_2_, ...), custom_call_target="tpu_custom_call" | custom-call | flops 30000001024 | bytes 108000000 | tf_op jit(solution)/shard_map/combine/pallas_call | solution.py:565
  26.0 3.6 %collective-permute-start.11 = (bf16[256,128]{1,0:T(8,128)(2,1)S(1)}, bf16[256,128]{1,0:T(8,128)(2,1)S(1)}, u32[]{:S(2)}, u32[]{:S(2)}) collective-permute-start(bf16[256,128]{1,0:T(8,128)(2,1)S(1)} %get-tuple-element.49), channel_id=1, source_target_pairs={{0,24},{2,26},{4,28},{6,30},{8,16},{10,18},{12,20},{14,22},{16,8},... | collective-permute-start | bytes 196616 | tf_op jit(solution)/shard_map/ppermute | solution.py:502
  29.6 1.7 %collective-permute-start.9 = (bf16[1024,128]{1,0:T(8,128)(2,1)S(1)}, bf16[1024,128]{1,0:T(8,128)(2,1)S(1)}, u32[]{:S(2)}, u32[]{:S(2)}) collective-permute-start(bf16[1024,128]{1,0:T(8,128)(2,1)S(1)} %get-tuple-element.44), channel_id=1, source_target_pairs={{0,16},{2,18},{4,20},{6,22},{8,24},{10,26},{12,28},{14,30},{16,0},... | collective-permute-start | bytes 786440 | tf_op jit(solution)/shard_map/ppermute | solution.py:502
  31.4 1.3 %collective-permute-start.10 = (bf16[1056,128]{1,0:T(8,128)(2,1)S(1)}, bf16[1056,128]{1,0:T(8,128)(2,1)S(1)}, u32[]{:S(2)}, u32[]{:S(2)}) collective-permute-start(bf16[1056,128]{1,0:T(8,128)(2,1)S(1)} %get-tuple-element.47), channel_id=1, source_target_pairs={{0,4},{2,6},{4,0},{6,2},{8,12},{10,14},{12,8},{14,10},{16,20},{18,... | collective-permute-start | bytes 811016 | tf_op jit(solution)/shard_map/ppermute | solution.py:502
  32.7 0.0 collective-permute-done.6.refs_2_
  32.7 2.1 %combine.5 = bf16[1024,128]{1,0:T(8,128)(2,1)S(1)} custom-call(bf16[2,2,32,8192]{3,2,1,0:T(8,128)(2,1)S(1)} %copy-done.1, bf16[2,2,32,8192]{3,2,1,0:T(8,128)(2,1)S(1)} %collective-permute-done.near.refs_1_, bf16[1056,128]{1,0:T(8,128)(2,1)S(1)} %collective-permute-done.6.refs_2_, bf16[1088,128]{1,0:T(8,128)(2,1)S(1)} %collective-permute-done.7.refs_3_.refs_2_, ...), custom_call_target="tpu_custom_call" | custom-call | flops 30000001024 | bytes 108000000 | tf_op jit(solution)/shard_map/combine/pallas_call | solution.py:565
  34.7 0.2 collective-permute-start.8
  34.9 3.7 %collective-permute-done.10.refs_2_ = bf16[1056,128]{1,0:T(8,128)(2,1)S(1)} collective-permute-done((bf16[1056,128]{1,0:T(8,128)(2,1)S(1)}, bf16[1056,128]{1,0:T(8,128)(2,1)S(1)}, u32[]{:S(2)}, u32[]{:S(2)}) %collective-permute-start.10) | collective-permute-done | bytes 270368 | tf_op jit(solution)/shard_map/ppermute | solution.py:502
  38.6 2.1 %combine.7.refs_0_ = f32[1024,128]{1,0:T(8,128)S(1)} custom-call(bf16[2,2,32,8192]{3,2,1,0:T(8,128)(2,1)S(1)} %copy-done.1, bf16[2,2,32,8192]{3,2,1,0:T(8,128)(2,1)S(1)} %collective-permute-done.near.refs_1_, bf16[1056,128]{1,0:T(8,128)(2,1)S(1)} %collective-permute-done.10.refs_2_, bf16[1088,128]{1,0:T(8,128)(2,1)S(1)} %collective-permute-done.7.refs_3_.refs_2_, ...), custom_call_target="tpu_custom_call" | custom-call | flops 30000001024 | bytes 108000000 | tf_op jit(solution)/shard_map/combine/pallas_call | solution.py:565
  40.7 0.0 collective-permute-done.11.refs_2_
  40.7 2.2 %finish_ahead.1 = (f32[4,1024,128]{2,1,0:T(8,128)}, f32[1024,128]{1,0:T(8,128)S(1)}) custom-call(s32[32]{0:T(128)S(1)} %copy-done.4, f32[1024,128]{1,0:T(8,128)S(1)} %combine.7.refs_0_, bf16[768,128]{1,0:T(8,128)(2,1)S(1)} %collective-permute-done.5.refs_1_, bf16[256,128]{1,0:T(8,128)(2,1)S(1)} %collective-permute-done.11.refs_2_, ...), custom_call_target="tpu_custom_call" | custom-call | flops 30000001024 | bytes 108000000 | tf_op jit(solution)/shard_map/finish_ahead/pallas_call | solution.py:633
  42.9 1.9 %collective-permute-done.9.refs_1_ = bf16[1024,128]{1,0:T(8,128)(2,1)S(1)} collective-permute-done((bf16[1024,128]{1,0:T(8,128)(2,1)S(1)}, bf16[1024,128]{1,0:T(8,128)(2,1)S(1)}, u32[]{:S(2)}, u32[]{:S(2)}) %collective-permute-start.9) | collective-permute-done | bytes 262176 | tf_op jit(solution)/shard_map/ppermute | solution.py:502
  44.8 1.8 %collective-permute-done.8.refs_0_ = bf16[1024,128]{1,0:T(8,128)(2,1)S(1)} collective-permute-done((bf16[1024,128]{1,0:T(8,128)(2,1)S(1)}, bf16[1024,128]{1,0:T(8,128)(2,1)S(1)}, u32[]{:S(2)}, u32[]{:S(2)}) %collective-permute-start.8) | collective-permute-done | bytes 262176 | tf_op jit(solution)/shard_map/ppermute | solution.py:502
  46.6 2.4 %finish_last.1 = (f32[4,1024,128]{2,1,0:T(8,128)}, f32[1024,128]{1,0:T(8,128)}) custom-call(s32[32]{0:T(128)S(1)} %copy-done.4, bf16[1024,128]{1,0:T(8,128)(2,1)S(1)} %collective-permute-done.8.refs_0_, bf16[1024,128]{1,0:T(8,128)(2,1)S(1)} %collective-permute-done.9.refs_1_, ...), custom_call_target="tpu_custom_call", output_to_operand_aliasing={{0}: (6, {})} | custom-call | bytes 1 | tf_op jit(solution)/shard_map/finish_last/pallas_call | solution.py:633
  (1 shorter events, 0.0 us)
Async XLA Ops:
  0.6 9.8 %collective-permute-start = (bf16[2,2,32,8192]{3,2,1,0:T(8,128)(2,1)}, bf16[2,2,32,8192]{3,2,1,0:T(8,128)(2,1)S(1)}, u32[]{:S(2)}, u32[]{:S(2)}) collective-permute-start(bf16[2,2,32,8192]{3,2,1,0:T(8,128)(2,1)} %refs_0_.6), channel_id=1, source_target_pairs={{0,2},{2,0},{4,6},{6,4},{8,10},{10,8},{12,14},{14,12},{16,18},{18,... | collective-permute-start | bytes 6291464 | tf_op jit(solution)/shard_map/ppermute | solution.py:502
  1.1 1.6 %copy-start = (bf16[2,2,32,8192]{3,2,1,0:T(8,128)(2,1)S(1)}, bf16[2,2,32,8192]{3,2,1,0:T(8,128)(2,1)}, u32[]{:S(2)}) copy-start(bf16[2,2,32,8192]{3,2,1,0:T(8,128)(2,1)} %refs_0_.6) | copy-start | bytes 6291460
  2.7 4.7 %copy-start.3 = (f32[4,3]{1,0:T(4,128)S(1)}, f32[4,3]{1,0:T(4,128)}, u32[]{:S(2)}) copy-start(f32[4,3]{1,0:T(4,128)} %center.1) | copy-start | bytes 148
  2.7 4.7 %copy-start.4 = (s32[32]{0:T(128)S(1)}, s32[32]{0:T(128)}, u32[]{:S(2)}) copy-start(s32[32]{0:T(128)} %parent_of.5) | copy-start | bytes 388
  2.7 4.7 %copy-start.5 = (s32[32]{0:T(128)S(1)}, s32[32]{0:T(128)}, u32[]{:S(2)}) copy-start(s32[32]{0:T(128)} %octant_of.1) | copy-start | bytes 388
  2.7 7.7 %copy-start.1 = (bf16[2,2,32,8192]{3,2,1,0:T(8,128)(2,1)S(1)}, bf16[2,2,32,8192]{3,2,1,0:T(8,128)(2,1)}, u32[]{:S(2)}) copy-start(bf16[2,2,32,8192]{3,2,1,0:T(8,128)(2,1)} %refs_0_.6) | copy-start | bytes 6291460
  3.0 9.6 %collective-permute-start.3 = (bf16[2,2,32,512]{3,2,1,0:T(8,128)(2,1)S(1)}, bf16[2,2,32,512]{3,2,1,0:T(8,128)(2,1)S(1)}, u32[]{:S(2)}, u32[]{:S(2)}) collective-permute-start(bf16[2,2,32,512]{3,2,1,0:T(8,128)(2,1)S(1)} %get-tuple-element.32), channel_id=1, source_target_pairs={{0,4},{2,6},{4,0},{6,2},{8,12},{10,14},{12,8},{14,10},{16,20},{18,... | collective-permute-start | bytes 393224 | tf_op jit(solution)/shard_map/ppermute | solution.py:502
  5.6 7.0 %collective-permute-start.4 = (bf16[2,2,32,512]{3,2,1,0:T(8,128)(2,1)S(1)}, bf16[2,2,32,512]{3,2,1,0:T(8,128)(2,1)S(1)}, u32[]{:S(2)}, u32[]{:S(2)}) collective-permute-start(bf16[2,2,32,512]{3,2,1,0:T(8,128)(2,1)S(1)} %get-tuple-element.33), channel_id=1, source_target_pairs={{0,6},{2,4},{4,2},{6,0},{8,14},{10,12},{12,10},{14,8},{16,22},{18,... | collective-permute-start | bytes 393224 | tf_op jit(solution)/shard_map/ppermute | solution.py:502
  5.8 4.6 %collective-permute-start.1 = (bf16[16,128]{1,0:T(8,128)(2,1)S(1)}, bf16[16,128]{1,0:T(8,128)(2,1)S(1)}, u32[]{:S(2)}, u32[]{:S(2)}) collective-permute-start(bf16[16,128]{1,0:T(8,128)(2,1)S(1)} %get-tuple-element.28), channel_id=1, source_target_pairs={{0,1},{1,0},{2,3},{3,2},{4,5},{5,4},{6,7},{7,6},{8,9},{9,8},{10,11... | collective-permute-start | bytes 12296 | tf_op jit(solution)/shard_map/ppermute | solution.py:526
  7.4 3.0 %collective-permute-start.2 = (bf16[16,128]{1,0:T(8,128)(2,1)S(1)}, bf16[16,128]{1,0:T(8,128)(2,1)S(1)}, u32[]{:S(2)}, u32[]{:S(2)}) collective-permute-start(bf16[16,128]{1,0:T(8,128)(2,1)S(1)} %get-tuple-element.28), channel_id=1, source_target_pairs={{0,3},{1,2},{2,1},{3,0},{4,7},{5,6},{6,5},{7,4},{8,11},{9,10},{10,... | collective-permute-start | bytes 12296 | tf_op jit(solution)/shard_map/ppermute | solution.py:526
  7.5 1.0 %copy-start.2 = (s32[65536]{0:T(1024)S(1)}, s32[65536]{0:T(1024)}, u32[]{:S(2)}) copy-start(s32[65536]{0:T(1024)} %param.17) | copy-start | bytes 786436
  10.4 2.3 %copy-start.6 = (bf16[512,512]{1,0:T(8,128)(2,1)S(1)}, bf16[512,512]{1,0:T(8,128)(2,1)}, u32[]{:S(2)}) copy-start(bf16[512,512]{1,0:T(8,128)(2,1)} %constant.5.clone.refs_8_.refs_10_.refs_11_) | copy-start | bytes 1572868
  10.4 2.3 %copy-start.7 = (bf16[512,512]{1,0:T(8,128)(2,1)S(1)}, bf16[512,512]{1,0:T(8,128)(2,1)}, u32[]{:S(2)}) copy-start(bf16[512,512]{1,0:T(8,128)(2,1)} %constant.4.clone.refs_7_.refs_9_.refs_10_) | copy-start | bytes 1572868
  11.0 12.3 %collective-permute-start.7 = (bf16[1088,128]{1,0:T(8,128)(2,1)S(1)}, bf16[1088,128]{1,0:T(8,128)(2,1)S(1)}, u32[]{:S(2)}, u32[]{:S(2)}) collective-permute-start(bf16[1088,128]{1,0:T(8,128)(2,1)S(1)} %get-tuple-element.40), channel_id=1, source_target_pairs={{0,4},{2,6},{4,0},{6,2},{8,12},{10,14},{12,8},{14,10},{16,20},{18,... | collective-permute-start | bytes 835592 | tf_op jit(solution)/shard_map/ppermute | solution.py:502
  14.2 9.1 %collective-permute-start.5 = (bf16[768,128]{1,0:T(8,128)(2,1)S(1)}, bf16[768,128]{1,0:T(8,128)(2,1)S(1)}, u32[]{:S(2)}, u32[]{:S(2)}) collective-permute-start(bf16[768,128]{1,0:T(8,128)(2,1)S(1)} %combine.4), channel_id=1, source_target_pairs={{0,24},{2,26},{4,28},{6,30},{8,16},{10,18},{12,20},{14,22},{16,8},... | collective-permute-start | bytes 589832 | tf_op jit(solution)/shard_map/ppermute | solution.py:502
  17.9 14.8 %collective-permute-start.6 = (bf16[1056,128]{1,0:T(8,128)(2,1)S(1)}, bf16[1056,128]{1,0:T(8,128)(2,1)S(1)}, u32[]{:S(2)}, u32[]{:S(2)}) collective-permute-start(bf16[1056,128]{1,0:T(8,128)(2,1)S(1)} %get-tuple-element.39), channel_id=1, source_target_pairs={{0,4},{2,6},{4,0},{6,2},{8,12},{10,14},{12,8},{14,10},{16,20},{18,... | collective-permute-start | bytes 811016 | tf_op jit(solution)/shard_map/ppermute | solution.py:502
  26.0 14.6 %collective-permute-start.11 = (bf16[256,128]{1,0:T(8,128)(2,1)S(1)}, bf16[256,128]{1,0:T(8,128)(2,1)S(1)}, u32[]{:S(2)}, u32[]{:S(2)}) collective-permute-start(bf16[256,128]{1,0:T(8,128)(2,1)S(1)} %get-tuple-element.49), channel_id=1, source_target_pairs={{0,24},{2,26},{4,28},{6,30},{8,16},{10,18},{12,20},{14,22},{16,8},... | collective-permute-start | bytes 196616 | tf_op jit(solution)/shard_map/ppermute | solution.py:502
  29.6 15.1 %collective-permute-start.9 = (bf16[1024,128]{1,0:T(8,128)(2,1)S(1)}, bf16[1024,128]{1,0:T(8,128)(2,1)S(1)}, u32[]{:S(2)}, u32[]{:S(2)}) collective-permute-start(bf16[1024,128]{1,0:T(8,128)(2,1)S(1)} %get-tuple-element.44), channel_id=1, source_target_pairs={{0,16},{2,18},{4,20},{6,22},{8,24},{10,26},{12,28},{14,30},{16,0},... | collective-permute-start | bytes 786440 | tf_op jit(solution)/shard_map/ppermute | solution.py:502
  31.4 7.2 %collective-permute-start.10 = (bf16[1056,128]{1,0:T(8,128)(2,1)S(1)}, bf16[1056,128]{1,0:T(8,128)(2,1)S(1)}, u32[]{:S(2)}, u32[]{:S(2)}) collective-permute-start(bf16[1056,128]{1,0:T(8,128)(2,1)S(1)} %get-tuple-element.47), channel_id=1, source_target_pairs={{0,4},{2,6},{4,0},{6,2},{8,12},{10,14},{12,8},{14,10},{16,20},{18,... | collective-permute-start | bytes 811016 | tf_op jit(solution)/shard_map/ppermute | solution.py:502
  34.7 11.9 %collective-permute-start.8 = (bf16[1024,128]{1,0:T(8,128)(2,1)S(1)}, bf16[1024,128]{1,0:T(8,128)(2,1)S(1)}, u32[]{:S(2)}, u32[]{:S(2)}) collective-permute-start(bf16[1024,128]{1,0:T(8,128)(2,1)S(1)} %combine.5), channel_id=1, source_target_pairs={{0,8},{2,10},{4,12},{6,14},{8,0},{10,2},{12,4},{14,6},{16,24},{18,... | collective-permute-start | bytes 786440 | tf_op jit(solution)/shard_map/ppermute | solution.py:502

commit v3 on v2

--- a/solution.py
+++ b/solution.py
@@ -204,32 +204,7 @@
     return rim + lax.dot_general(pick_after, after, across, preferred_element_type=jnp.float32)
 
 
-def first_pack_kernel(step, members, piece, cells, *refs):
-    far = members - 2
-    outs, edge, ends, sems = refs[:far], refs[far], refs[far + 1], refs[far + 2]
-    block = cells.shape[3]
-    wide_at = lax.axis_index("wide")
-    group_at, member_at = wide_at // members, wide_at % members
-    copies = []
-    for swap in range(far):
-        first = ((group_at ^ step) * members + (member_at ^ (swap + 2))) * piece
-        at = pl.ds(pl.multiple_of(first, LANES), piece)
-        copies.append(pltpu.make_async_copy(cells.at[:, :, :, at], outs[swap], sems.at[swap]))
-    for index, at in enumerate((block - LANES, 0)):
-        copies.append(
-            pltpu.make_async_copy(cells.at[:, :, :, pl.ds(at, LANES)], ends.at[index], sems.at[far + index])
-        )
-    for copy in copies:
-        copy.start()
-    for copy in copies[far:]:
-        copy.wait()
-    rows = ends.shape[1] * ends.shape[2] * ends.shape[3]
-    edge[...] = rim_of(ends[0].reshape(rows, LANES), ends[1].reshape(rows, LANES), 2 * HALO).astype(jnp.bfloat16)
-    for copy in copies[:far]:
-        copy.wait()
-
-
-def rest_pack_kernel(groups, members, piece, cells, near, edge, near_edge, *outs):
+def rest_pack_kernel(groups, members, piece, cells, near, *outs):
     boxes, parts, sources, block = cells.shape
     rows = boxes * parts * sources
     tiles = piece // LANES
@@ -242,12 +217,16 @@
     def rim_at(ref, first):
         return rim_of(tile(ref, jnp.maximum(first - LANES, 0)), tile(ref, jnp.minimum(first + piece, block - LANES)), 0)
 
+    edges = outs[-1]
+    for half, ref in enumerate((cells, near)):
+        rim = rim_of(tile(ref, block - LANES), tile(ref, 0), 2 * HALO)
+        edges[half * RIM : (half + 1) * RIM, :] = rim.astype(jnp.bfloat16)
     for part in range(1, groups):
         for swap in range(2, members, 2):
             out, base = outs[(part - 1) * (members // 2 - 1) + swap // 2 - 1], 0
             target = member_at ^ swap
             first = ((group_at ^ (groups - 1 - part)) * members + target) * piece
-            for ref, rim_edge in ((cells, edge), (near, near_edge)):
+            for ref in (cells, near):
                 for index in range(tiles):
                     out[base : base + rows, :] = tile(ref, first + index * LANES)
                     base += rows
@@ -255,33 +234,68 @@
                 base += RIM
                 if part == 1:
                     rim = rim_at(ref, ((group_at ^ (groups - 1)) * members + target) * piece)
-                    out[base : base + RIM, :] = (rim + rim_edge[...].astype(jnp.float32)).astype(jnp.bfloat16)
+                    out[base : base + RIM, :] = rim.astype(jnp.bfloat16)
                     base += RIM
 
 
-def prep_kernel(groups, members, boxes, piece, parent_of, octant_of, center, starts, cosines, sines, center_cos, center_sin, excess):
+def turned(cycles):
+    half = math.pi * (cycles - jnp.floor(cycles + 0.5))
+    square = half * half
+    sine, cosine = jnp.zeros_like(half), jnp.zeros_like(half)
+    for order in range(13, 0, -2):
+        sine = sine * square + (-1) ** (order // 2) / math.factorial(order)
+        cosine = cosine * square + (-1) ** (order // 2) / math.factorial(order - 1)
+    sine = sine * half
+    return 1.0 - 2.0 * sine * sine, 2.0 * sine * cosine
+
+
+def axes_kernel(groups, members, piece, sample_count, cosines, sines, center_dirs):
     wide_at = lax.axis_index("wide")
-    narrow_at = lax.axis_index("narrow")
     group_at, member_at = wide_at // members, wide_at % members
     rows = 4 * piece // LANES
-    all_rows = starts.shape[0]
-    half_rows = all_rows // lax.axis_size("narrow")
-    cycles = all_rows * LANES // 256
+    half_rows = sample_count // LANES // lax.axis_size("narrow")
     row = lax.broadcasted_iota(jnp.int32, (rows, LANES), 0)
     lane = lax.broadcasted_iota(jnp.int32, (rows, LANES), 1)
-
-    def place(group):
-        first_row = narrow_at * half_rows + (group * members + member_at) * rows
-        sample = (first_row + row) * LANES + lane
-        azimuth = 2.0 * math.pi * ((sample & 255).astype(jnp.float32) + 0.5) / 256.0
-        polar = math.pi * ((sample >> 8).astype(jnp.float32) + 0.5) / cycles
-        sin_polar = jnp.sin(polar)
-        return first_row, sample, sin_polar * jnp.cos(azimuth), sin_polar * jnp.sin(azimuth), jnp.cos(polar)
-
+    cos_azimuth, sin_azimuth = turned((((row * LANES + lane) & 255).astype(jnp.float32) + 0.5) / 256.0)
     for step in range(groups):
-        first_row, sample, dir_x, dir_y, dir_z = place(group_at ^ step)
-        here = starts[pl.ds(pl.multiple_of(first_row, 8), rows), :]
-        excess[step] = ((sample >> 2) - 2 - here).astype(jnp.float32)
+        first_row = lax.axis_index("narrow") * half_rows + ((group_at ^ step) * members + member_at) * rows
+        ring = ((first_row + row) * LANES + lane) >> 8
+        dir_z, sin_polar = turned((ring.astype(jnp.float32) + 0.5) / (2 * (sample_count // 256)))
+        for axis, direction in enumerate((sin_polar * cos_azimuth, sin_polar * sin_azimuth, dir_z)):
+            cosines[step, axis], sines[step, axis] = turned(2.0 * direction)
+            if step == 0:
+                center_dirs[axis] = direction
+
+
+def prep_kernel(
+    groups, members, boxes, piece, parent_of, octant_of, center, starts, axis_cos, axis_sin, center_dirs,
+    cosines, sines, center_cos, center_sin, excess, held, sems,
+):
+    wide_at = lax.axis_index("wide")
+    group_at, member_at = wide_at // members, wide_at % members
+    rows = 4 * piece // LANES
+    half_rows = starts.shape[0] // lax.axis_size("narrow")
+    row = lax.broadcasted_iota(jnp.int32, (rows, LANES), 0)
+    lane = lax.broadcasted_iota(jnp.int32, (rows, LANES), 1)
+    first_rows = [
+        pl.multiple_of(lax.axis_index("narrow") * half_rows + ((group_at ^ step) * members + member_at) * rows, 8)
+        for step in range(groups)
+    ]
+    copies = [
+        pltpu.make_async_copy(starts.at[pl.ds(first_rows[step], rows)], held.at[step], sems.at[step]) for step in range(groups)
+    ]
+    for copy in copies:
+        copy.start()
+    scale = 1.0 / math.sqrt(center.shape[0])
+    for step in range(groups):
+        parent = parent_of[(group_at ^ step) * members * boxes]
+        turns = sum(center[parent, axis] * center_dirs[axis] for axis in range(3))
+        turn_cos, turn_sin = turned(turns)
+        center_cos[step] = turn_cos * scale
+        center_sin[step] = turn_sin * scale
+    for step in range(groups):
+        (cos_x, cos_y, cos_z), (sin_x, sin_y, sin_z) = ([table[step, axis] for axis in range(3)] for table in (axis_cos, axis_sin))
+        both_cos, both_sin, sin_cos, cos_sin = cos_x * cos_y, sin_x * sin_y, sin_x * cos_y, cos_x * sin_y
         for swap in range(members):
             for box in range(boxes):
                 slot = (group_at * members + (member_at ^ swap)) * boxes + box
@@ -290,27 +304,25 @@
                 sign_x = ((octant & 1) * 2 - 1).astype(jnp.float32)
                 sign_y = (((octant >> 1) & 1) * 2 - 1).astype(jnp.float32)
                 sign_z = ((octant >> 2) * 2 - 1).astype(jnp.float32)
-                angle = 4.0 * math.pi * (sign_x * dir_x + sign_y * dir_y + sign_z * dir_z)
-                cosines[step, swap * boxes + box] = jnp.cos(angle) * live
-                sines[step, swap * boxes + box] = jnp.sin(angle) * live
-    _, _, dir_x, dir_y, dir_z = place(group_at)
-    scale = 1.0 / math.sqrt(center.shape[0])
-    for parent in range(center.shape[0]):
-        turns = center[parent, 0] * dir_x + center[parent, 1] * dir_y + center[parent, 2] * dir_z
-        angle = 2.0 * math.pi * turns
-        center_cos[parent] = jnp.cos(angle) * scale
-        center_sin[parent] = jnp.sin(angle) * scale
-
-
-def columns_of(windows, tiles):
-    return [c for w in windows for c in range(max(0, 4 * w + 2), min(4 * tiles, 4 * w + 6))]
+                real = both_cos - (sign_x * sign_y) * both_sin
+                imag = sign_x * sin_cos + sign_y * cos_sin
+                turn_cos, turn_sin = live * cos_z, (live * sign_z) * sin_z
+                cosines[step, swap * boxes + box] = real * turn_cos - imag * turn_sin
+                sines[step, swap * boxes + box] = real * turn_sin + imag * turn_cos
+    for step in range(groups):
+        copies[step].wait()
+        child = ((first_rows[step] + row) * LANES + lane) >> 2
+        excess[step] = (child - 2 - held[step]).astype(jnp.float32)
+
+
+def columns_of(windows):
+    return [2 * window + half for window in windows for half in range(2)]
 
 
 def combine_kernel(jobs, members, boxes, sources, tiles, count, *refs):
     data = refs[:count]
     cosines, sines, excess, band_zero, band_one = refs[count : count + 5]
-    outs = refs[count + 5 : count + 5 + len(jobs)]
-    spread, total = refs[count + 5 + len(jobs) :]
+    *outs, spread, total = refs[count + 5 :]
     for (step, *job), out in zip(jobs, outs):
         combine(
             step, *job, members, boxes, sources, tiles, data, cosines.at[step], sines.at[step], excess.at[step],
@@ -373,39 +385,52 @@
         near = jnp.concatenate(near, axis=0)
         rim_tile = jnp.concatenate([rim_tile[: 2 * rows] + near, rim_tile[2 * rows :]], axis=0).astype(jnp.bfloat16)
 
-    columns = columns_of(windows, tiles)
+    def window_of(window):
+        cut = 32 if window % 2 else 96
+        left, right = tile((window - 1 + window % 2) // 2), tile((window + 1) // 2)
+        cells = jnp.concatenate([left[:, cut:], right[:, :cut]], axis=1)
+        return jnp.concatenate([cells, cells], axis=1)
+
+    columns = columns_of(windows)
     width = len(columns)
-    for turn, window in enumerate(windows):
-        mine = columns_of([window], tiles)
-        left, right = tile(window), tile(window + 1)
-        cells = jnp.concatenate([left, right, left, right], axis=1)
+
+    def spread_window(turn):
         bands = []
-        for column in mine:
-            at_column = (column + 2) % 4 * LANES
+        for half, column in enumerate(columns[2 * turn : 2 * turn + 2]):
             which = jnp.broadcast_to(excess[column : column + 1, :], (16, LANES)).astype(jnp.bfloat16)
             which = jnp.concatenate([which] * (band_zero.shape[0] // 16), axis=0)
-            zero = band_zero[:, at_column : at_column + LANES]
-            one = band_one[:, at_column : at_column + LANES]
-            bands.append(zero * (1 - which) + one * which)
-        band = jnp.concatenate(bands, axis=1)
-        buffer = spread.at[turn % 2]
-        buffer[:, : len(mine) * LANES] = jnp.dot(cells, band, preferred_element_type=jnp.float32)
-        for number, column in enumerate(mine):
-            lanes = slice(number * LANES, (number + 1) * LANES)
+            lanes = slice(half * LANES, (half + 1) * LANES)
+            bands.append(band_zero[:, lanes] * (1 - which) + band_one[:, lanes] * which)
+        spread[turn % 2] = jnp.dot(
+            window_of(windows[turn]), jnp.concatenate(bands, axis=1), preferred_element_type=jnp.float32
+        )
+
+    def sum_window(turn):
+        for half, column in enumerate(columns[2 * turn : 2 * turn + 2]):
+            lanes = slice(half * LANES, (half + 1) * LANES)
             real_sum = jnp.zeros((sources, LANES), jnp.float32)
             imag_sum = jnp.zeros((sources, LANES), jnp.float32)
             for child in range(members * boxes):
                 start = child * 2 * sources
-                real = buffer[start : start + sources, lanes].astype(jnp.bfloat16).astype(jnp.float32)
-                imag = buffer[start + sources : start + 2 * sources, lanes].astype(jnp.bfloat16).astype(jnp.float32)
+                real = spread[turn % 2, start : start + sources, lanes].astype(jnp.bfloat16).astype(jnp.float32)
+                imag = spread[turn % 2, start + sources : start + 2 * sources, lanes]
+                imag = imag.astype(jnp.bfloat16).astype(jnp.float32)
                 cosine = cosines[child, column : column + 1, :]
                 sine = sines[child, column : column + 1, :]
                 real_sum = real_sum + (cosine * real - sine * imag)
                 imag_sum = imag_sum + (sine * real + cosine * imag)
-            at_row = columns.index(column)
+            at_row = 2 * turn + half
             total[pl.ds(at_row, sources, stride=width), :] = real_sum
             total[pl.ds(sources * width + at_row, sources, stride=width), :] = imag_sum
-    out[...] = total[: 2 * sources * width, :].astype(out.dtype)
+
+    for turn in range(len(windows) + 1):
+        if turn < len(windows):
+            spread_window(turn)
+        if turn:
+            sum_window(turn - 1)
+    out[: 2 * sources * width, :] = total[: 2 * sources * width, :].astype(out.dtype)
+    if out.shape[0] > 2 * sources * width:
+        out[2 * sources * width :, :] = jnp.zeros((out.shape[0] - 2 * sources * width, LANES), out.dtype)
 
 
 def spans_of(columns):
@@ -417,59 +442,69 @@
     return spans
 
 
-def finish_kernel(last, pieces, members, boxes, sources, rows, parent_of, *refs):
-    arrived, refs = refs[: len(pieces)], refs[len(pieces) :]
-    if last:
-        center_cos, center_sin, far_in, _, parent_out, far_out, held, sems = refs
-    else:
-        center_cos, center_sin, parent_out, far_out = refs
+def finish_ahead_kernel(own_step, early_step, columns, members, boxes, sources, rows, parent_of, own, early, center_cos, center_sin, parent_out, far_out, early_out):
+    name = parent_of[((lax.axis_index("wide") // members) ^ own_step) * members * boxes]
+    width = len(columns)
+    for source in range(sources):
+        real_at, imag_at = (pl.ds((half * sources + source) * rows, rows) for half in range(2))
+        real, imag = own[real_at, :], own[imag_at, :]
+        cosine, sine = center_cos[own_step], center_sin[own_step]
+        parent_out[name, real_at, :] = real
+        parent_out[name, imag_at, :] = imag
+        far_out[real_at, :] = cosine * real - sine * imag
+        far_out[imag_at, :] = sine * real + cosine * imag
+        for begin, column, length in spans_of(columns):
+            real, imag = (early[pl.ds((half * sources + source) * width + begin, length), :].astype(jnp.float32) for half in range(2))
+            cosine, sine = (table[early_step, column : column + length, :] for table in (center_cos, center_sin))
+            real_at, imag_at = (pl.ds((half * sources + source) * rows + column, length) for half in range(2))
+            early_out[real_at, :] = real
+            early_out[imag_at, :] = imag
+            far_out[real_at, :] += cosine * real - sine * imag
+            far_out[imag_at, :] += sine * real + cosine * imag
+
+
+def finish_kernel(steps, early_step, columns, members, boxes, sources, rows, parts, parent_of, *refs):
+    whole, refs = refs[: len(steps)], refs[len(steps) :]
+    late, early, center_cos, center_sin, far_in, _, parent_out, far_out, names, held, far_held, name_sem, sems = refs
+    name_copy = pltpu.make_async_copy(parent_of, names, name_sem)
+    name_copy.start()
+    width = len(columns)
     group_at = lax.axis_index("wide") // members
-    names = [parent_of[(group_at ^ step) * members * boxes] for step, _ in pieces]
-    turns = [(center_cos[name], center_sin[name]) for name in names]
     copies = []
-    for source in range(sources):
-        real_all, imag_all = (pl.ds((part * sources + source) * rows, rows) for part in range(2))
-        if last:
-            real_sum, imag_sum = far_in[real_all, :], far_in[imag_all, :]
-        for piece, (step, columns) in enumerate(pieces):
-            width = len(columns)
+    each = sources // parts
+    for part in range(parts):
+        for source in range(part * each, (part + 1) * each):
+            real_at, imag_at = (pl.ds((half * sources + source) * rows, rows) for half in range(2))
+            far_real, far_imag = far_in[real_at, :], far_in[imag_at, :]
+            for index, step in enumerate(steps):
+                real, imag = whole[index][real_at, :].astype(jnp.float32), whole[index][imag_at, :].astype(jnp.float32)
+                cosine, sine = center_cos[step], center_sin[step]
+                held[index, real_at, :] = real
+                held[index, imag_at, :] = imag
+                far_real = far_real + (cosine * real - sine * imag)
+                far_imag = far_imag + (sine * real + cosine * imag)
+            far_held[real_at, :] = far_real
+            far_held[imag_at, :] = far_imag
+            index = len(steps)
+            held[index, real_at, :] = early[real_at, :]
+            held[index, imag_at, :] = early[imag_at, :]
             for begin, column, length in spans_of(columns):
-                real = arrived[piece][pl.ds(source * width + begin, length), :].astype(jnp.float32)
-                imag = arrived[piece][pl.ds((sources + source) * width + begin, length), :].astype(jnp.float32)
-                cosine, sine = (turn[column : column + length, :] for turn in turns[piece])
-                real_at = pl.ds(source * rows + column, length)
-                imag_at = pl.ds((sources + source) * rows + column, length)
-                real_turned = cosine * real - sine * imag
-                imag_turned = sine * real + cosine * imag
-                if last:
-                    held[piece, real_at, :] = real
-                    held[piece, imag_at, :] = imag
-                    real_sum = real_sum + real_turned
-                    imag_sum = imag_sum + imag_turned
-                else:
-                    parent_out[names[piece], real_at, :] = real
-                    parent_out[names[piece], imag_at, :] = imag
-                    if piece == 0:
-                        far_out[real_at, :] = real_turned
-                        far_out[imag_at, :] = imag_turned
-                    else:
-                        far_out[real_at, :] += real_turned
-                        far_out[imag_at, :] += imag_turned
-        if last:
-            far_out[real_all, :] = real_sum
-            far_out[imag_all, :] = imag_sum
-            if source % (sources // 2) == sources // 2 - 1:
-                half = source // (sources // 2)
-                size = sources // 2 * rows
-                for piece in range(len(pieces)):
-                    for part in range(2):
-                        at = pl.ds(part * sources * rows + half * size, size)
-                        copies.append(
-                            pltpu.make_async_copy(
-                                held.at[piece, at], parent_out.at[names[piece], at], sems.at[(half * len(pieces) + piece) * 2 + part]
-                            )
-                        )
-                        copies[-1].start()
+                real, imag = (late[pl.ds((half * sources + source) * width + begin, length), :].astype(jnp.float32) for half in range(2))
+                cosine, sine = (table[early_step, column : column + length, :] for table in (center_cos, center_sin))
+                real_at, imag_at = (pl.ds((half * sources + source) * rows + column, length) for half in range(2))
+                held[index, real_at, :] = real
+                held[index, imag_at, :] = imag
+                far_held[real_at, :] += cosine * real - sine * imag
+                far_held[imag_at, :] += sine * real + cosine * imag
+        if part == 0:
+            name_copy.wait()
+            places = [names[(group_at ^ step) * members * boxes] for step in (*steps, early_step)]
+        for half in range(2):
+            at = pl.ds((half * sources + part * each) * rows, each * rows)
+            moves = [(held.at[index, at], parent_out.at[place, at]) for index, place in enumerate(places)]
+            for source, target in moves + [(far_held.at[at], far_out.at[at])]:
+                copies.append(pltpu.make_async_copy(source, target, sems.at[len(copies)]))
+                copies[-1].start()
     for copy in copies:
         copy.wait()
 
@@ -505,19 +540,11 @@
         return lax.optimization_barrier(arrays)
 
     far = members - 2
-    *heads, edge = pl.pallas_call(
-        functools.partial(first_pack_kernel, groups - 1, members, piece),
-        out_shape=[bf16(boxes, 2, sources, piece)] * far + [bf16(RIM, LANES)],
-        in_specs=[hbm],
-        out_specs=[vmem] * (far + 1),
-        scratch_shapes=[
-            pltpu.VMEM((2, boxes, 2, sources, LANES), jnp.bfloat16),
-            pltpu.SemaphoreType.DMA((members,)),
-        ],
-        compiler_params=pltpu.CompilerParams(vmem_limit_bytes=16 * 1024 * 1024),
-        cost_estimate=cost(0),
-        name="pack_first",
-    )(child_pattern)
+    wide_at = lax.axis_index("wide")
+    heads = []
+    for swap in range(2, members):
+        first = (((wide_at // members) ^ (groups - 1)) * members + ((wide_at % members) ^ swap)) * piece
+        heads.append(lax.dynamic_slice_in_dim(child_pattern, first, piece, 3))
     near = swap_with(child_pattern, 1)
     heads = [swap_with(head, swap + 2) for swap, head in enumerate(heads)]
 
@@ -525,8 +552,14 @@
         pairs = [(i * 2 + n, (i ^ step) * 2 + 1 - n) for i in range(n_wide) for n in range(2)]
         return lax.ppermute(array, ("wide", "narrow"), pairs)
 
-    near_edge = other_half(edge, 1)
-    edge = other_half(edge, 0)
+    axes = pl.pallas_call(
+        functools.partial(axes_kernel, groups, members, piece, stencil_start.shape[0]),
+        out_shape=[f32(groups, 3, out_rows, LANES)] * 2 + [f32(3, out_rows, LANES)],
+        out_specs=[vmem] * 3,
+        compiler_params=limit,
+        cost_estimate=cost(1),
+        name="axes",
+    )()
     tables = pl.pallas_call(
         functools.partial(prep_kernel, groups, members, boxes, piece),
         out_shape=[
@@ -536,39 +569,46 @@
             f32(parents, out_rows, LANES),
             f32(groups, out_rows, LANES),
         ],
-        in_specs=[smem, smem, smem, vmem],
+        in_specs=[smem, smem, smem, hbm] + [vmem] * 3,
         out_specs=[vmem] * 5,
+        scratch_shapes=[pltpu.VMEM((groups, out_rows, LANES), jnp.int32), pltpu.SemaphoreType.DMA((groups,))],
         compiler_params=limit,
-            cost_estimate=cost(0),
+            cost_estimate=cost(1),
         name="prep",
-    )(child_parent, child_octant, parent_center, stencil_start.reshape(-1, LANES))
+    )(child_parent, child_octant, parent_center, stencil_start.reshape(-1, LANES), *axes)
     cosines, sines, center_cos, center_sin, excess = tables
-    edge, excess = tie(edge, excess)
     full = tiles * rows + RIM
     pairs = members // 2 - 1
-    sends = list(pl.pallas_call(
+    *sends, edges = pl.pallas_call(
         functools.partial(rest_pack_kernel, groups, members, piece),
         out_shape=[
             bf16(2 * (full + (RIM if part == 1 else 0)), LANES) for part in range(1, groups) for _ in range(pairs)
-        ],
-        in_specs=[vmem] * 4,
-        out_specs=[vmem] * ((groups - 1) * pairs),
+        ]
+        + [bf16(2 * RIM, LANES)],
+        in_specs=[vmem] * 2,
+        out_specs=[vmem] * ((groups - 1) * pairs + 1),
         compiler_params=limit,
-        cost_estimate=cost(0),
-        name="pack_rest",
-    )(child_pattern, near, edge, near_edge))
-    bands = stencil_tables(2 * LANES, 4 * LANES)
+        cost_estimate=cost(1),
+        name="pack",
+    )(child_pattern, near)
+    common = [other_half(edges, 2 * pair) for pair in range(pairs + 1)]
+    bands = stencil_tables(LANES, 2 * LANES)
+
+    top = groups - 1
 
     def sums_of(jobs, data, dtype, micros):
-        shapes = [jax.ShapeDtypeStruct((2 * sources * len(columns_of(job[1], tiles)), LANES), dtype) for job in jobs]
+        shapes = [
+            jax.ShapeDtypeStruct((2 * sources * len(columns_of(job[1])) + (RIM if job[0] == top - 1 else 0), LANES), dtype)
+            for job in jobs
+        ]
         inputs = [*data, cosines, sines, excess, bands[0], bands[1]]
         return pl.pallas_call(
             functools.partial(combine_kernel, jobs, members, boxes, sources, tiles, len(data)),
             out_shape=shapes,
             in_specs=[vmem] * len(inputs),
-            out_specs=[vmem] * len(jobs),
+            out_specs=[vmem] * len(shapes),
             scratch_shapes=[
-                pltpu.VMEM((2, members * rows, 4 * LANES), jnp.float32),
+                pltpu.VMEM((2, members * rows, 2 * LANES), jnp.float32),
                 pltpu.VMEM((2 * sources * out_rows, LANES), jnp.float32),
             ],
             compiler_params=limit,
@@ -576,10 +616,9 @@
             name="combine",
         )(*inputs)
 
-    top = groups - 1
-    inner = list(range(tiles - 1))
-    outer = [-1, tiles - 1]
-    every = list(range(-1, tiles))
+    inner = list(range(1, 2 * tiles - 1))
+    outer = [0, 2 * tiles - 1]
+    every = list(range(2 * tiles))
     locals_ = [child_pattern, near]
     first_data = locals_ + heads
     first_places = [(2 + member, 0) for member in range(far)]
@@ -592,65 +631,61 @@
     for part in range(1, groups):
         step = top - part
         sent = sends[(part - 1) * pairs : part * pairs]
-        if part == 3:
-            data[0], done[0] = tie(data[0], done[0])
         if part > 1:
-            totals = sums_of(jobs, data, jnp.bfloat16, 30)
+            totals = list(sums_of(jobs, data, jnp.bfloat16, 30 if part == 2 else 2))
             if part < groups - 1:
                 tied = tie(*sends[part * pairs : (part + 1) * pairs], *totals)
-                sends[part * pairs : (part + 1) * pairs], totals = tied[:pairs], tied[pairs:]
+                sends[part * pairs : (part + 1) * pairs], totals = tied[:pairs], list(tied[pairs:])
             arrived[step + 1] = swap_with(totals[0], (step + 1) * members)
             if part == 2:
                 done.append(swap_with(totals[1], top * members))
         got = [swap_with(array, 2 * pair + 2) for pair, array in enumerate(sent)]
         length = full + (RIM if part == 1 else 0)
         places = [(2 + member // 2, member % 2 * length) for member in range(far)]
+        data = locals_ + got + common
+        shift = 2 + pairs
+        edge_at = [(shift + member // 2, member % 2 * RIM) for member in range(members)]
+        rims = [None, None] + [(which, row + tiles * rows) for which, row in places]
+        jobs = [(step, every, places, list(zip(rims, edge_at)))]
         if part == 1:
-            rest = got + [edge, near_edge]
-            far_rims = [(which - 2, row + full) for which, row in places]
-        shift = 2 + pairs if part > 1 else 2
-        data = locals_ + (got if part > 1 else []) + rest
-        rims = [(None, (shift + pairs + member, 0)) for member in range(2)]
-        rims += [
-            ((which, row + tiles * rows), (shift + other, other_row))
-            for (which, row), (other, other_row) in zip(places, far_rims)
-        ]
-        jobs = [(step, every, places, rims)]
-        if part == 1:
-            outer_rims = [(None, (shift + pairs + member, 0)) for member in range(2)]
-            outer_rims += [((shift + which, row),) * 2 for which, row in far_rims]
+            rims = [None, None] + [(which, row + full) for which, row in places]
             outer_places = [(len(data) + member, 0) for member in range(far)]
-            jobs.append((top, outer, outer_places, outer_rims))
+            jobs.append((top, outer, outer_places, list(zip(rims, edge_at))))
             data = data + heads
-    (arrived[0],) = sums_of(jobs, data, jnp.float32, 30)
-    done = [(top, columns_of(inner, tiles), done[0]), (top, columns_of(outer, tiles), done[1])]
+    data[0], done[0] = tie(data[0], done[0])
+    (arrived[0],) = sums_of(jobs, data, jnp.float32, 1)
+    done = [(top, columns_of(inner), done[0]), (top, columns_of(outer), done[1])]
     held = arrived
-    ahead = [(0, columns_of(every, tiles), held[0])] + done
-    final = [(step, columns_of(every, tiles), held[step]) for step in sorted(held) if step]
-
-    def finish(last, pieces, extra):
-        shapes = [f32(parents, 2 * sources * out_rows, LANES), f32(2 * sources * out_rows, LANES)]
-        return pl.pallas_call(
-            functools.partial(
-                finish_kernel, last, [(step, columns) for step, columns, _ in pieces], members, boxes, sources, out_rows
-            ),
-            out_shape=shapes,
-            in_specs=[smem] + [vmem] * (len(pieces) + 2) + ([vmem, hbm] if last else []),
-            out_specs=[hbm if last else vmem, vmem],
-            input_output_aliases={len(pieces) + 4: 0} if last else {},
-            scratch_shapes=[
-                pltpu.VMEM((len(pieces),) + shapes[1].shape, jnp.float32),
-                pltpu.SemaphoreType.DMA((4 * len(pieces),)),
-            ]
-            if last
-            else [],
-            compiler_params=limit,
-            cost_estimate=cost(0 if last else 30),
-            name="finish_last" if last else "finish_ahead",
-        )(child_parent, *[array for _, _, array in pieces], center_cos, center_sin, *extra)
-
-    parent_pattern, far_field = finish(False, ahead, [])
-    parent_pattern, far_field = finish(True, final, [far_field, parent_pattern])
+    whole = f32(2 * sources * out_rows, LANES)
+    (_, early_columns, early_array), (_, late_columns, late_array) = done
+    parent_pattern, far_field, early_pattern = pl.pallas_call(
+        functools.partial(finish_ahead_kernel, 0, top, early_columns, members, boxes, sources, out_rows),
+        out_shape=[f32(parents, *whole.shape), whole, whole],
+        in_specs=[smem] + [vmem] * 4,
+        out_specs=[vmem] * 3,
+        compiler_params=limit,
+        cost_estimate=cost(0),
+        name="finish_ahead",
+    )(child_parent, held[0], early_array, center_cos, center_sin)
+    steps = sorted((step for step in held if step), reverse=True)
+    parts = 4
+    parent_pattern, far_field = pl.pallas_call(
+        functools.partial(finish_kernel, steps, top, late_columns, members, boxes, sources, out_rows, parts),
+        out_shape=[f32(parents, *whole.shape), whole],
+        in_specs=[hbm] + [vmem] * (len(steps) + 5) + [hbm],
+        out_specs=[hbm, hbm],
+        input_output_aliases={len(steps) + 6: 0},
+        scratch_shapes=[
+            pltpu.SMEM(child_parent.shape, jnp.int32),
+            pltpu.VMEM((len(steps) + 1, *whole.shape), jnp.float32),
+            pltpu.VMEM(whole.shape, jnp.float32),
+            pltpu.SemaphoreType.DMA,
+            pltpu.SemaphoreType.DMA((2 * parts * (len(steps) + 2),)),
+        ],
+        compiler_params=limit,
+        cost_estimate=cost(30),
+        name="finish_last",
+    )(child_parent, *[held[step] for step in steps], late_array, early_pattern, center_cos, center_sin, far_field, parent_pattern)
     return (
         parent_pattern.reshape(parents, 2, sources, 1, 4 * piece),
         far_field.reshape(2, sources, 1, 4 * piece),

time: 49.2 us -> 41.9 us (0.85)
  waiting for transfers between devices: 11.5 us -> 4.89 us
  starting transfers between devices: 18.3 us -> 21.8 us
  Pallas kernels: 15.8 us -> 12.8 us
  local copies, waits for them, and re-layouts: 2.56 us -> 1.6 us
    ppermute x10, waiting for transfers between devices: 11.5 us -> 4.88 us  [swap_with(): return lax.ppermute(array, 'wide', [(i, i ^ step) for i in range(n_wide)])]
    unnamed x16 -> x14, local copies, waits for them, and re-layouts: 2.56 us -> 0.57 us
    ppermute x2, starting transfers between devices: 1.64 us -> 3.46 us  [other_half(): return lax.ppermute(array, ('wide', 'narrow'), pairs)]
    ppermute x10, starting transfers between devices: 16.7 us -> 18.3 us  [swap_with(): return lax.ppermute(array, 'wide', [(i, i ^ step) for i in range(n_wide)])]
    pallas_call x4, Pallas kernels: 8.44 us -> 6.96 us  [sums_of(): pl.pallas_call(functools.partial(combine_kernel, jobs, members, boxes, so...]
    dynamic_slice x0 -> x1, local copies, waits for them, and re-layouts: none -> 1.04 us  [grouped(): heads.append(lax.dynamic_slice_in_dim(child_pattern, first, piece, 3))]
    pallas_call x1, Pallas kernels: 1.96 us -> 0.96 us  [grouped(): pl.pallas_call(functools.partial(prep_kernel, groups, members, boxes, pie...]
    pallas_call x3, Pallas kernels: 4.95 us -> 4.34 us  [the longest x1 2.12 us: grouped(): pl.pallas_call(functools.partial(finish_kernel, steps, top, late_columns,...]
  transfers between devices with their start and end apart: 12 -> 12, of which waited for: 5 -> 3; matrix products, arithmetic and copies ran while one was open for 0% -> 2% of each run, Pallas kernels for 27% -> 25%
where the time goes in v3:
time: 41.9 us; the launch traced here: 41.8 us
  starting transfers between devices  21.8 us (52%)
  Pallas kernels  12.8 us (31%)
  waiting for transfers between devices  4.89 us (12%)
  local copies, waits for them, and re-layouts  1.6 us (4%)
  between operations  0.76 us (2%)
    ppermute x10, starting transfers between devices, swap_with(): return lax.ppermute(array, 'wide', [(i, i ^ step) for i in range(n_wide)])  18.3 us
    pallas_call x4, Pallas kernels, sums_of(): pl.pallas_call(functools.partial(combine_kernel, jobs, members, boxes, so...  6.96 us
    ppermute x10, waiting for transfers between devices, swap_with(): return lax.ppermute(array, 'wide', [(i, i ^ step) for i in range(n_wide)])  4.88 us
    ppermute x2, starting transfers between devices, other_half(): return lax.ppermute(array, ('wide', 'narrow'), pairs)  3.46 us
    pallas_call x1, Pallas kernels, grouped(): pl.pallas_call(functools.partial(finish_kernel, steps, top, late_columns,...  2.12 us
    pallas_call x1, Pallas kernels, grouped(): pl.pallas_call(functools.partial(finish_ahead_kernel, 0, top, early_colum...  2.01 us
    dynamic_slice x1, local copies, waits for them, and re-layouts, grouped(): heads.append(lax.dynamic_slice_in_dim(child_pattern, first, piece, 3))  1.04 us
    pallas_call x1, Pallas kernels, grouped(): pl.pallas_call(functools.partial(prep_kernel, groups, members, boxes, pie...  0.96 us
  transfers between devices with their start and end apart: 12, of which 3 were waited for; matrix products, arithmetic and copies ran while one was open for 2% of the time, Pallas kernels for 25%

profile of v3, /device:TPU:0, one launch (start us, length us, event | category | flops | bytes accessed | tf_op | source)
XLA Modules:
  0.0 41.8 jit_solution(7729876965779479949)
XLA Ops:
  0.6 0.5 %collective-permute-start = (bf16[2,2,32,8192]{3,2,1,0:T(8,128)(2,1)}, bf16[2,2,32,8192]{3,2,1,0:T(8,128)(2,1)S(1)}, u32[]{:S(2)}, u32[]{:S(2)}) collective-permute-start(bf16[2,2,32,8192]{3,2,1,0:T(8,128)(2,1)} %refs_0_.6), channel_id=1, source_target_pairs={{0,2},{2,0},{4,6},{6,4},{8,10},{10,8},{12,14},{14,12},{16,18},{18,... | collective-permute-start | bytes 6291464 | tf_op jit(solution)/shard_map/ppermute | solution.py:537
  1.1 0.0 copy-start.3
  1.2 0.0 copy-start.4
  1.2 0.0 copy-start.5
  1.2 0.0 copy-start.6
  1.2 1.0 %constant_dynamic-slice_fusion = (bf16[2,2,32,512]{3,2,1,0:T(8,128)(2,1)S(1)}, bf16[2,2,32,512]{3,2,1,0:T(8,128)(2,1)S(1)}) fusion(bf16[2,2,32,8192]{3,2,1,0:T(8,128)(2,1)} %refs_0_.6, s32[]{:T(128)S(6)} %select_n.23, s32[]{:T(128)S(6)} %select_n.22), kind=kLoop, calls=%fused_computation | loop fusion | bytes 524296 | tf_op jit(solution)/shard_map/dynamic_slice | solution.py:547
  2.2 2.7 %collective-permute-start.5 = (bf16[2,2,32,512]{3,2,1,0:T(8,128)(2,1)S(1)}, bf16[2,2,32,512]{3,2,1,0:T(8,128)(2,1)S(1)}, u32[]{:S(2)}, u32[]{:S(2)}) collective-permute-start(bf16[2,2,32,512]{3,2,1,0:T(8,128)(2,1)S(1)} %get-tuple-element.56), channel_id=1, source_target_pairs={{0,6},{2,4},{4,2},{6,0},{8,14},{10,12},{12,10},{14,8},{16,22},{18,... | collective-permute-start | bytes 393224 | tf_op jit(solution)/shard_map/ppermute | solution.py:537
  4.9 0.1 collective-permute-start.4
  4.9 0.2 axes.1
  5.2 0.0 copy-start
  5.2 0.0 copy-done.3
  5.2 0.0 copy-done.4
  5.2 0.0 copy-done.5
  5.2 0.0 copy-done.6
  5.2 1.0 %prep.1 = (f32[4,8,16,128]{3,2,1,0:T(8,128)S(1)}, f32[4,8,16,128]{3,2,1,0:T(8,128)S(1)}, f32[4,16,128]{2,1,0:T(8,128)S(1)}, f32[4,16,128]{2,1,0:T(8,128)S(1)}, f32[4,16,128]{2,1,0:T(8,128)S(1)}) custom-call(s32[32]{0:T(128)S(1)} %copy-done.3, s32[32]{0:T(128)S(1)} %copy-done.6, f32[4,3]{1,0:T(4,128)S(1)} %copy-done.5, s32[512,128]{1,0:T(8,128)S(1)} %bitcast.3, ...), custom_call_target="tpu_custom_call" | custom-call | flops 1000000000 | bytes 3600001 | tf_op jit(solution)/shard_map/prep/pallas_call | solution.py:563
  6.2 0.0 copy-start.1
  6.2 0.0 copy-start.2
  6.2 0.0 collective-permute-done.near.refs_1_
  6.2 0.5 %copy-done = bf16[2,2,32,8192]{3,2,1,0:T(8,128)(2,1)S(1)} copy-done((bf16[2,2,32,8192]{3,2,1,0:T(8,128)(2,1)S(1)}, bf16[2,2,32,8192]{3,2,1,0:T(8,128)(2,1)}, u32[]{:S(2)}) %copy-start) | copy-done | bytes 2097176
  6.7 0.5 %pack.1 = (bf16[1088,128]{1,0:T(8,128)(2,1)S(1)}, bf16[1056,128]{1,0:T(8,128)(2,1)S(1)}, bf16[1056,128]{1,0:T(8,128)(2,1)S(1)}, bf16[32,128]{1,0:T(8,128)(2,1)S(1)}) custom-call(bf16[2,2,32,8192]{3,2,1,0:T(8,128)(2,1)S(1)} %copy-done, bf16[2,2,32,8192]{3,2,1,0:T(8,128)(2,1)S(1)} %collective-permute-done.near.refs_1_), custom_call_target="tpu_custom_call" | custom-call | flops 1000000000 | bytes 3600001 | tf_op jit(solution)/shard_map/pack/pallas_call | solution.py:582
  7.3 2.9 %collective-permute-start.3 = (bf16[32,128]{1,0:T(8,128)(2,1)S(1)}, bf16[32,128]{1,0:T(8,128)(2,1)S(1)}, u32[]{:S(2)}, u32[]{:S(2)}) collective-permute-start(bf16[32,128]{1,0:T(8,128)(2,1)S(1)} %get-tuple-element.30), channel_id=1, source_target_pairs={{0,5},{1,4},{2,7},{3,6},{4,1},{5,0},{6,3},{7,2},{8,13},{9,12},{10,... | collective-permute-start | bytes 24584 | tf_op jit(solution)/shard_map/ppermute | solution.py:553
  10.2 0.5 %collective-permute-start.2 = (bf16[32,128]{1,0:T(8,128)(2,1)S(1)}, bf16[32,128]{1,0:T(8,128)(2,1)S(1)}, u32[]{:S(2)}, u32[]{:S(2)}) collective-permute-start(bf16[32,128]{1,0:T(8,128)(2,1)S(1)} %get-tuple-element.30), channel_id=1, source_target_pairs={{0,1},{1,0},{2,3},{3,2},{4,5},{5,4},{6,7},{7,6},{8,9},{9,8},{10,11... | collective-permute-start | bytes 24584 | tf_op jit(solution)/shard_map/ppermute | solution.py:553
  10.7 0.1 collective-permute-start.1
  10.8 0.0 collective-permute-done.5.refs_6_.refs_3_
  10.8 1.1 %collective-permute-done.4.refs_5_.refs_2_ = bf16[2,2,32,512]{3,2,1,0:T(8,128)(2,1)S(1)} collective-permute-done((bf16[2,2,32,512]{3,2,1,0:T(8,128)(2,1)S(1)}, bf16[2,2,32,512]{3,2,1,0:T(8,128)(2,1)S(1)}, u32[]{:S(2)}, u32[]{:S(2)}) %collective-permute-start.4) | collective-permute-done | bytes 131104 | tf_op jit(solution)/shard_map/ppermute | solution.py:537
  11.9 0.0 copy-done.1
  11.9 0.0 copy-done.2
  11.9 1.1 %combine.5 = bf16[768,128]{1,0:T(8,128)(2,1)S(1)} custom-call(bf16[2,2,32,8192]{3,2,1,0:T(8,128)(2,1)S(1)} %copy-done, bf16[2,2,32,8192]{3,2,1,0:T(8,128)(2,1)S(1)} %collective-permute-done.near.refs_1_, bf16[2,2,32,512]{3,2,1,0:T(8,128)(2,1)S(1)} %collective-permute-done.4.refs_5_.refs_2_, ...), custom_call_target="tpu_custom_call" | custom-call | flops 5000000000 | bytes 18000000 | tf_op jit(solution)/shard_map/combine/pallas_call | solution.py:605
  13.0 3.8 %collective-permute-start.10 = (bf16[768,128]{1,0:T(8,128)(2,1)S(1)}, bf16[768,128]{1,0:T(8,128)(2,1)S(1)}, u32[]{:S(2)}, u32[]{:S(2)}) collective-permute-start(bf16[768,128]{1,0:T(8,128)(2,1)S(1)} %combine.5), channel_id=1, source_target_pairs={{0,24},{2,26},{4,28},{6,30},{8,16},{10,18},{12,20},{14,22},{16,8},... | collective-permute-start | bytes 589832 | tf_op jit(solution)/shard_map/ppermute | solution.py:537
  16.8 2.0 %collective-permute-start.7 = (bf16[1056,128]{1,0:T(8,128)(2,1)S(1)}, bf16[1056,128]{1,0:T(8,128)(2,1)S(1)}, u32[]{:S(2)}, u32[]{:S(2)}) collective-permute-start(bf16[1056,128]{1,0:T(8,128)(2,1)S(1)} %get-tuple-element.41), channel_id=1, source_target_pairs={{0,4},{2,6},{4,0},{6,2},{8,12},{10,14},{12,8},{14,10},{16,20},{18,... | collective-permute-start | bytes 811016 | tf_op jit(solution)/shard_map/ppermute | solution.py:537
  18.8 0.0 collective-permute-done.3.refs_4_
  18.8 0.0 collective-permute-done.2.refs_3_
  18.8 0.0 collective-permute-done.1.refs_2_
  18.8 2.2 %combine.4 = (bf16[1040,128]{1,0:T(8,128)(2,1)S(1)}, bf16[256,128]{1,0:T(8,128)(2,1)S(1)}) custom-call(bf16[2,2,32,8192]{3,2,1,0:T(8,128)(2,1)S(1)} %copy-done, bf16[2,2,32,8192]{3,2,1,0:T(8,128)(2,1)S(1)} %collective-permute-done.near.refs_1_, bf16[1088,128]{1,0:T(8,128)(2,1)S(1)} %collective-permute-done.1.refs_2_, ...), custom_call_target="tpu_custom_call" | custom-call | flops 30000001024 | bytes 108000000 | tf_op jit(solution)/shard_map/combine/pallas_call | solution.py:605
  21.1 4.1 %collective-permute-start.6 = (bf16[1040,128]{1,0:T(8,128)(2,1)S(1)}, bf16[1040,128]{1,0:T(8,128)(2,1)S(1)}, u32[]{:S(2)}, u32[]{:S(2)}) collective-permute-start(bf16[1040,128]{1,0:T(8,128)(2,1)S(1)} %get-tuple-element.39), channel_id=1, source_target_pairs={{0,16},{2,18},{4,20},{6,22},{8,24},{10,26},{12,28},{14,30},{16,0},... | collective-permute-start | bytes 798728 | tf_op jit(solution)/shard_map/ppermute | solution.py:537
  25.2 0.5 %collective-permute-start.11 = (bf16[1056,128]{1,0:T(8,128)(2,1)S(1)}, bf16[1056,128]{1,0:T(8,128)(2,1)S(1)}, u32[]{:S(2)}, u32[]{:S(2)}) collective-permute-start(bf16[1056,128]{1,0:T(8,128)(2,1)S(1)} %get-tuple-element.45), channel_id=1, source_target_pairs={{0,4},{2,6},{4,0},{6,2},{8,12},{10,14},{12,8},{14,10},{16,20},{18,... | collective-permute-start | bytes 811016 | tf_op jit(solution)/shard_map/ppermute | solution.py:537
  25.7 0.0 collective-permute-done.7.refs_2_
  25.7 1.8 %combine.6 = bf16[1024,128]{1,0:T(8,128)(2,1)S(1)} custom-call(bf16[2,2,32,8192]{3,2,1,0:T(8,128)(2,1)S(1)} %copy-done, bf16[2,2,32,8192]{3,2,1,0:T(8,128)(2,1)S(1)} %collective-permute-done.near.refs_1_, bf16[1056,128]{1,0:T(8,128)(2,1)S(1)} %collective-permute-done.7.refs_2_, bf16[32,128]{1,0:T(8,128)(2,1)S(1)} %collective-permute-done.2.refs_3_, ...), custom_call_target="tpu_custom_call" | custom-call | flops 2000000000 | bytes 7200001 | tf_op jit(solution)/shard_map/combine/pallas_call | solution.py:605
  27.5 1.6 %collective-permute-start.8 = (bf16[1024,128]{1,0:T(8,128)(2,1)S(1)}, bf16[1024,128]{1,0:T(8,128)(2,1)S(1)}, u32[]{:S(2)}, u32[]{:S(2)}) collective-permute-start(bf16[1024,128]{1,0:T(8,128)(2,1)S(1)} %combine.6), channel_id=1, source_target_pairs={{0,8},{2,10},{4,12},{6,14},{8,0},{10,2},{12,4},{14,6},{16,24},{18,... | collective-permute-start | bytes 786440 | tf_op jit(solution)/shard_map/ppermute | solution.py:537
  29.2 0.0 collective-permute-done.10.early
  29.2 2.9 %collective-permute-start.9 = (bf16[256,128]{1,0:T(8,128)(2,1)S(1)}, bf16[256,128]{1,0:T(8,128)(2,1)S(1)}, u32[]{:S(2)}, u32[]{:S(2)}) collective-permute-start(bf16[256,128]{1,0:T(8,128)(2,1)S(1)} %get-tuple-element.42), channel_id=1, source_target_pairs={{0,24},{2,26},{4,28},{6,30},{8,16},{10,18},{12,20},{14,22},{16,8},... | collective-permute-start | bytes 196616 | tf_op jit(solution)/shard_map/ppermute | solution.py:537
  32.1 0.0 collective-permute-done.11.refs_2_
  32.1 1.8 %combine.7.own = f32[1024,128]{1,0:T(8,128)S(1)} custom-call(bf16[2,2,32,8192]{3,2,1,0:T(8,128)(2,1)S(1)} %copy-done, bf16[2,2,32,8192]{3,2,1,0:T(8,128)(2,1)S(1)} %collective-permute-done.near.refs_1_, bf16[1056,128]{1,0:T(8,128)(2,1)S(1)} %collective-permute-done.11.refs_2_, bf16[32,128]{1,0:T(8,128)(2,1)S(1)} %collective-permute-done.2.refs_3_, ...), custom_call_target="tpu_custom_call" | custom-call | flops 1000000000 | bytes 3600001 | tf_op jit(solution)/shard_map/combine/pallas_call | solution.py:605
  33.9 2.0 %finish_ahead.1 = (f32[4,1024,128]{2,1,0:T(8,128)}, f32[1024,128]{1,0:T(8,128)S(1)}, f32[1024,128]{1,0:T(8,128)S(1)}) custom-call(s32[32]{0:T(128)S(1)} %copy-done.3, f32[1024,128]{1,0:T(8,128)S(1)} %combine.7.own, bf16[768,128]{1,0:T(8,128)(2,1)S(1)} %collective-permute-done.10.early, f32[4,16,128]{2,1,0:T(8,128)S(1)} %get-tuple-element.47.center_cos.refs_4_, ...), custom_call_target="tpu_custom_call" | custom-call | bytes 1 | tf_op jit(solution)/shard_map/finish_ahead/pallas_call | solution.py:661
  35.9 2.2 %collective-permute-done.9.refs_2_ = bf16[256,128]{1,0:T(8,128)(2,1)S(1)} collective-permute-done((bf16[256,128]{1,0:T(8,128)(2,1)S(1)}, bf16[256,128]{1,0:T(8,128)(2,1)S(1)}, u32[]{:S(2)}, u32[]{:S(2)}) %collective-permute-start.9) | collective-permute-done | bytes 65568 | tf_op jit(solution)/shard_map/ppermute | solution.py:537
  38.1 1.5 %collective-permute-done.8.refs_1_ = bf16[1024,128]{1,0:T(8,128)(2,1)S(1)} collective-permute-done((bf16[1024,128]{1,0:T(8,128)(2,1)S(1)}, bf16[1024,128]{1,0:T(8,128)(2,1)S(1)}, u32[]{:S(2)}, u32[]{:S(2)}) %collective-permute-start.8) | collective-permute-done | bytes 262176 | tf_op jit(solution)/shard_map/ppermute | solution.py:537
  39.6 0.0 collective-permute-done.6.refs_0_
  39.7 2.1 %finish_last.1 = (f32[4,1024,128]{2,1,0:T(8,128)}, f32[1024,128]{1,0:T(8,128)}) custom-call(s32[32]{0:T(128)S(1)} %copy-done.3, bf16[1040,128]{1,0:T(8,128)(2,1)S(1)} %collective-permute-done.6.refs_0_, bf16[1024,128]{1,0:T(8,128)(2,1)S(1)} %collective-permute-done.8.refs_1_, ...), custom_call_target="tpu_custom_call", output_to_operand_aliasing={{0}: (8, {})} | custom-call | flops 30000001024 | bytes 108000000 | tf_op jit(solution)/shard_map/finish_last/pallas_call | solution.py:672
Async XLA Ops:
  0.6 5.6 %collective-permute-start = (bf16[2,2,32,8192]{3,2,1,0:T(8,128)(2,1)}, bf16[2,2,32,8192]{3,2,1,0:T(8,128)(2,1)S(1)}, u32[]{:S(2)}, u32[]{:S(2)}) collective-permute-start(bf16[2,2,32,8192]{3,2,1,0:T(8,128)(2,1)} %refs_0_.6), channel_id=1, source_target_pairs={{0,2},{2,0},{4,6},{6,4},{8,10},{10,8},{12,14},{14,12},{16,18},{18,... | collective-permute-start | bytes 6291464 | tf_op jit(solution)/shard_map/ppermute | solution.py:537
  1.1 4.0 %copy-start.3 = (s32[32]{0:T(128)S(1)}, s32[32]{0:T(128)}, u32[]{:S(2)}) copy-start(s32[32]{0:T(128)} %parent_of.5) | copy-start | bytes 388
  1.2 4.0 %copy-start.4 = (s32[65536]{0:T(1024)S(1)}, s32[65536]{0:T(1024)}, u32[]{:S(2)}) copy-start(s32[65536]{0:T(1024)} %param.17) | copy-start | bytes 786436
  1.2 4.0 %copy-start.5 = (f32[4,3]{1,0:T(4,128)S(1)}, f32[4,3]{1,0:T(4,128)}, u32[]{:S(2)}) copy-start(f32[4,3]{1,0:T(4,128)} %center.1) | copy-start | bytes 148
  1.2 4.0 %copy-start.6 = (s32[32]{0:T(128)S(1)}, s32[32]{0:T(128)}, u32[]{:S(2)}) copy-start(s32[32]{0:T(128)} %octant_of.1) | copy-start | bytes 388
  2.2 8.6 %collective-permute-start.5 = (bf16[2,2,32,512]{3,2,1,0:T(8,128)(2,1)S(1)}, bf16[2,2,32,512]{3,2,1,0:T(8,128)(2,1)S(1)}, u32[]{:S(2)}, u32[]{:S(2)}) collective-permute-start(bf16[2,2,32,512]{3,2,1,0:T(8,128)(2,1)S(1)} %get-tuple-element.56), channel_id=1, source_target_pairs={{0,6},{2,4},{4,2},{6,0},{8,14},{10,12},{12,10},{14,8},{16,22},{18,... | collective-permute-start | bytes 393224 | tf_op jit(solution)/shard_map/ppermute | solution.py:537
  4.9 7.0 %collective-permute-start.4 = (bf16[2,2,32,512]{3,2,1,0:T(8,128)(2,1)S(1)}, bf16[2,2,32,512]{3,2,1,0:T(8,128)(2,1)S(1)}, u32[]{:S(2)}, u32[]{:S(2)}) collective-permute-start(bf16[2,2,32,512]{3,2,1,0:T(8,128)(2,1)S(1)} %get-tuple-element.57), channel_id=1, source_target_pairs={{0,4},{2,6},{4,0},{6,2},{8,12},{10,14},{12,8},{14,10},{16,20},{18,... | collective-permute-start | bytes 393224 | tf_op jit(solution)/shard_map/ppermute | solution.py:537
  5.2 1.6 %copy-start = (bf16[2,2,32,8192]{3,2,1,0:T(8,128)(2,1)S(1)}, bf16[2,2,32,8192]{3,2,1,0:T(8,128)(2,1)}, u32[]{:S(2)}) copy-start(bf16[2,2,32,8192]{3,2,1,0:T(8,128)(2,1)} %refs_0_.6) | copy-start | bytes 6291460
  6.2 5.8 %copy-start.1 = (bf16[256,256]{1,0:T(8,128)(2,1)S(1)}, bf16[256,256]{1,0:T(8,128)(2,1)}, u32[]{:S(2)}) copy-start(bf16[256,256]{1,0:T(8,128)(2,1)} %constant.48.clone.refs_11_.refs_8_.refs_9_) | copy-start | bytes 393220
  6.2 5.7 %copy-start.2 = (bf16[256,256]{1,0:T(8,128)(2,1)S(1)}, bf16[256,256]{1,0:T(8,128)(2,1)}, u32[]{:S(2)}) copy-start(bf16[256,256]{1,0:T(8,128)(2,1)} %constant.47.clone.refs_10_.refs_7_.refs_8_) | copy-start | bytes 393220
  7.3 11.6 %collective-permute-start.3 = (bf16[32,128]{1,0:T(8,128)(2,1)S(1)}, bf16[32,128]{1,0:T(8,128)(2,1)S(1)}, u32[]{:S(2)}, u32[]{:S(2)}) collective-permute-start(bf16[32,128]{1,0:T(8,128)(2,1)S(1)} %get-tuple-element.30), channel_id=1, source_target_pairs={{0,5},{1,4},{2,7},{3,6},{4,1},{5,0},{6,3},{7,2},{8,13},{9,12},{10,... | collective-permute-start | bytes 24584 | tf_op jit(solution)/shard_map/ppermute | solution.py:553
  10.2 8.6 %collective-permute-start.2 = (bf16[32,128]{1,0:T(8,128)(2,1)S(1)}, bf16[32,128]{1,0:T(8,128)(2,1)S(1)}, u32[]{:S(2)}, u32[]{:S(2)}) collective-permute-start(bf16[32,128]{1,0:T(8,128)(2,1)S(1)} %get-tuple-element.30), channel_id=1, source_target_pairs={{0,1},{1,0},{2,3},{3,2},{4,5},{5,4},{6,7},{7,6},{8,9},{9,8},{10,11... | collective-permute-start | bytes 24584 | tf_op jit(solution)/shard_map/ppermute | solution.py:553
  10.7 8.1 %collective-permute-start.1 = (bf16[1088,128]{1,0:T(8,128)(2,1)S(1)}, bf16[1088,128]{1,0:T(8,128)(2,1)S(1)}, u32[]{:S(2)}, u32[]{:S(2)}) collective-permute-start(bf16[1088,128]{1,0:T(8,128)(2,1)S(1)} %get-tuple-element.29), channel_id=1, source_target_pairs={{0,4},{2,6},{4,0},{6,2},{8,12},{10,14},{12,8},{14,10},{16,20},{18,... | collective-permute-start | bytes 835592 | tf_op jit(solution)/shard_map/ppermute | solution.py:537
  13.0 16.2 %collective-permute-start.10 = (bf16[768,128]{1,0:T(8,128)(2,1)S(1)}, bf16[768,128]{1,0:T(8,128)(2,1)S(1)}, u32[]{:S(2)}, u32[]{:S(2)}) collective-permute-start(bf16[768,128]{1,0:T(8,128)(2,1)S(1)} %combine.5), channel_id=1, source_target_pairs={{0,24},{2,26},{4,28},{6,30},{8,16},{10,18},{12,20},{14,22},{16,8},... | collective-permute-start | bytes 589832 | tf_op jit(solution)/shard_map/ppermute | solution.py:537
  16.8 8.9 %collective-permute-start.7 = (bf16[1056,128]{1,0:T(8,128)(2,1)S(1)}, bf16[1056,128]{1,0:T(8,128)(2,1)S(1)}, u32[]{:S(2)}, u32[]{:S(2)}) collective-permute-start(bf16[1056,128]{1,0:T(8,128)(2,1)S(1)} %get-tuple-element.41), channel_id=1, source_target_pairs={{0,4},{2,6},{4,0},{6,2},{8,12},{10,14},{12,8},{14,10},{16,20},{18,... | collective-permute-start | bytes 811016 | tf_op jit(solution)/shard_map/ppermute | solution.py:537
  21.1 18.6 %collective-permute-start.6 = (bf16[1040,128]{1,0:T(8,128)(2,1)S(1)}, bf16[1040,128]{1,0:T(8,128)(2,1)S(1)}, u32[]{:S(2)}, u32[]{:S(2)}) collective-permute-start(bf16[1040,128]{1,0:T(8,128)(2,1)S(1)} %get-tuple-element.39), channel_id=1, source_target_pairs={{0,16},{2,18},{4,20},{6,22},{8,24},{10,26},{12,28},{14,30},{16,0},... | collective-permute-start | bytes 798728 | tf_op jit(solution)/shard_map/ppermute | solution.py:537
  25.2 6.9 %collective-permute-start.11 = (bf16[1056,128]{1,0:T(8,128)(2,1)S(1)}, bf16[1056,128]{1,0:T(8,128)(2,1)S(1)}, u32[]{:S(2)}, u32[]{:S(2)}) collective-permute-start(bf16[1056,128]{1,0:T(8,128)(2,1)S(1)} %get-tuple-element.45), channel_id=1, source_target_pairs={{0,4},{2,6},{4,0},{6,2},{8,12},{10,14},{12,8},{14,10},{16,20},{18,... | collective-permute-start | bytes 811016 | tf_op jit(solution)/shard_map/ppermute | solution.py:537
  27.5 12.1 %collective-permute-start.8 = (bf16[1024,128]{1,0:T(8,128)(2,1)S(1)}, bf16[1024,128]{1,0:T(8,128)(2,1)S(1)}, u32[]{:S(2)}, u32[]{:S(2)}) collective-permute-start(bf16[1024,128]{1,0:T(8,128)(2,1)S(1)} %combine.6), channel_id=1, source_target_pairs={{0,8},{2,10},{4,12},{6,14},{8,0},{10,2},{12,4},{14,6},{16,24},{18,... | collective-permute-start | bytes 786440 | tf_op jit(solution)/shard_map/ppermute | solution.py:537
  29.2 9.0 %collective-permute-start.9 = (bf16[256,128]{1,0:T(8,128)(2,1)S(1)}, bf16[256,128]{1,0:T(8,128)(2,1)S(1)}, u32[]{:S(2)}, u32[]{:S(2)}) collective-permute-start(bf16[256,128]{1,0:T(8,128)(2,1)S(1)} %get-tuple-element.42), channel_id=1, source_target_pairs={{0,24},{2,26},{4,28},{6,30},{8,16},{10,18},{12,20},{14,22},{16,8},... | collective-permute-start | bytes 196616 | tf_op jit(solution)/shard_map/ppermute | solution.py:537

commit v4 on v3

--- a/solution.py
+++ b/solution.py
@@ -393,6 +393,7 @@
 
     columns = columns_of(windows)
     width = len(columns)
+    whole = width == 4 * tiles
 
     def spread_window(turn):
         bands = []
@@ -419,48 +420,54 @@
                 sine = sines[child, column : column + 1, :]
                 real_sum = real_sum + (cosine * real - sine * imag)
                 imag_sum = imag_sum + (sine * real + cosine * imag)
-            at_row = 2 * turn + half
-            total[pl.ds(at_row, sources, stride=width), :] = real_sum
-            total[pl.ds(sources * width + at_row, sources, stride=width), :] = imag_sum
+            if whole:
+                total[pl.ds(column, sources, stride=width), :] = real_sum
+                total[pl.ds(sources * width + column, sources, stride=width), :] = imag_sum
+            else:
+                at_row = (2 * turn + half) * 2 * sources
+                out[at_row : at_row + sources, :] = real_sum.astype(out.dtype)
+                out[at_row + sources : at_row + 2 * sources, :] = imag_sum.astype(out.dtype)
 
     for turn in range(len(windows) + 1):
         if turn < len(windows):
             spread_window(turn)
         if turn:
             sum_window(turn - 1)
-    out[: 2 * sources * width, :] = total[: 2 * sources * width, :].astype(out.dtype)
+    if whole:
+        out[: 2 * sources * width, :] = total[: 2 * sources * width, :].astype(out.dtype)
     if out.shape[0] > 2 * sources * width:
         out[2 * sources * width :, :] = jnp.zeros((out.shape[0] - 2 * sources * width, LANES), out.dtype)
 
 
-def spans_of(columns):
-    spans, begin = [], 0
-    for i in range(1, len(columns) + 1):
-        if i == len(columns) or columns[i] != columns[i - 1] + 1:
-            spans.append((begin, columns[begin], i - begin))
-            begin = i
-    return spans
-
-
-def finish_ahead_kernel(own_step, early_step, columns, members, boxes, sources, rows, parent_of, own, early, center_cos, center_sin, parent_out, far_out, early_out):
+def place_columns(arrived, columns, sources, rows, cosines, sines, pattern, far):
+    for index, column in enumerate(columns):
+        real, imag = (
+            arrived[pl.ds((2 * index + half) * sources, sources), :].astype(jnp.float32) for half in range(2)
+        )
+        at = pl.ds(column, sources, stride=rows)
+        pattern[0, at, :] = real
+        pattern[1, at, :] = imag
+        cosine, sine = cosines[column : column + 1, :], sines[column : column + 1, :]
+        far[0, at, :] += cosine * real - sine * imag
+        far[1, at, :] += sine * real + cosine * imag
+
+
+def finish_ahead_kernel(
+    own_step, early_step, columns, members, boxes, sources, rows,
+    parent_of, own, early, center_cos, center_sin, parent_out, far_out, early_out,
+):
     name = parent_of[((lax.axis_index("wide") // members) ^ own_step) * members * boxes]
-    width = len(columns)
+    cosine, sine = center_cos[own_step], center_sin[own_step]
     for source in range(sources):
-        real_at, imag_at = (pl.ds((half * sources + source) * rows, rows) for half in range(2))
-        real, imag = own[real_at, :], own[imag_at, :]
-        cosine, sine = center_cos[own_step], center_sin[own_step]
-        parent_out[name, real_at, :] = real
-        parent_out[name, imag_at, :] = imag
-        far_out[real_at, :] = cosine * real - sine * imag
-        far_out[imag_at, :] = sine * real + cosine * imag
-        for begin, column, length in spans_of(columns):
-            real, imag = (early[pl.ds((half * sources + source) * width + begin, length), :].astype(jnp.float32) for half in range(2))
-            cosine, sine = (table[early_step, column : column + length, :] for table in (center_cos, center_sin))
-            real_at, imag_at = (pl.ds((half * sources + source) * rows + column, length) for half in range(2))
-            early_out[real_at, :] = real
-            early_out[imag_at, :] = imag
-            far_out[real_at, :] += cosine * real - sine * imag
-            far_out[imag_at, :] += sine * real + cosine * imag
+        at = pl.ds(source * rows, rows)
+        real, imag = (own[pl.ds((half * sources + source) * rows, rows), :] for half in range(2))
+        parent_out[name, 0, at, :] = real
+        parent_out[name, 1, at, :] = imag
+        far_out[0, at, :] = cosine * real - sine * imag
+        far_out[1, at, :] = sine * real + cosine * imag
+    place_columns(
+        early, columns, sources, rows, center_cos.at[early_step], center_sin.at[early_step], early_out, far_out
+    )
 
 
 def finish_kernel(steps, early_step, columns, members, boxes, sources, rows, parts, parent_of, *refs):
@@ -468,43 +475,42 @@
     late, early, center_cos, center_sin, far_in, _, parent_out, far_out, names, held, far_held, name_sem, sems = refs
     name_copy = pltpu.make_async_copy(parent_of, names, name_sem)
     name_copy.start()
-    width = len(columns)
     group_at = lax.axis_index("wide") // members
     copies = []
+
+    def send(source, target):
+        copies.append(pltpu.make_async_copy(source, target, sems.at[len(copies)]))
+        copies[-1].start()
+
+    last = len(steps)
+    held[last] = early[...]
+    far_held[...] = far_in[...]
+    place_columns(
+        late, columns, sources, rows, center_cos.at[early_step], center_sin.at[early_step], held.at[last], far_held
+    )
+    name_copy.wait()
+    places = [names[(group_at ^ step) * members * boxes] for step in (*steps, early_step)]
+    send(held.at[last], parent_out.at[places[last]])
     each = sources // parts
     for part in range(parts):
         for source in range(part * each, (part + 1) * each):
-            real_at, imag_at = (pl.ds((half * sources + source) * rows, rows) for half in range(2))
-            far_real, far_imag = far_in[real_at, :], far_in[imag_at, :]
+            at = pl.ds(source * rows, rows)
+            far_real, far_imag = far_held[0, at, :], far_held[1, at, :]
             for index, step in enumerate(steps):
-                real, imag = whole[index][real_at, :].astype(jnp.float32), whole[index][imag_at, :].astype(jnp.float32)
+                real, imag = (
+                    whole[index][pl.ds((half * sources + source) * rows, rows), :].astype(jnp.float32) for half in range(2)
+                )
                 cosine, sine = center_cos[step], center_sin[step]
-                held[index, real_at, :] = real
-                held[index, imag_at, :] = imag
+                held[index, 0, at, :] = real
+                held[index, 1, at, :] = imag
                 far_real = far_real + (cosine * real - sine * imag)
                 far_imag = far_imag + (sine * real + cosine * imag)
-            far_held[real_at, :] = far_real
-            far_held[imag_at, :] = far_imag
-            index = len(steps)
-            held[index, real_at, :] = early[real_at, :]
-            held[index, imag_at, :] = early[imag_at, :]
-            for begin, column, length in spans_of(columns):
-                real, imag = (late[pl.ds((half * sources + source) * width + begin, length), :].astype(jnp.float32) for half in range(2))
-                cosine, sine = (table[early_step, column : column + length, :] for table in (center_cos, center_sin))
-                real_at, imag_at = (pl.ds((half * sources + source) * rows + column, length) for half in range(2))
-                held[index, real_at, :] = real
-                held[index, imag_at, :] = imag
-                far_held[real_at, :] += cosine * real - sine * imag
-                far_held[imag_at, :] += sine * real + cosine * imag
-        if part == 0:
-            name_copy.wait()
-            places = [names[(group_at ^ step) * members * boxes] for step in (*steps, early_step)]
-        for half in range(2):
-            at = pl.ds((half * sources + part * each) * rows, each * rows)
-            moves = [(held.at[index, at], parent_out.at[place, at]) for index, place in enumerate(places)]
-            for source, target in moves + [(far_held.at[at], far_out.at[at])]:
-                copies.append(pltpu.make_async_copy(source, target, sems.at[len(copies)]))
-                copies[-1].start()
+            far_held[0, at, :] = far_real
+            far_held[1, at, :] = far_imag
+        at = pl.ds(part * each * rows, each * rows)
+        for index in range(last):
+            send(held.at[index, :, at], parent_out.at[places[index], :, at])
+        send(far_held.at[:, at], far_out.at[:, at])
     for copy in copies:
         copy.wait()
 
@@ -543,7 +549,7 @@
     wide_at = lax.axis_index("wide")
     heads = []
     for swap in range(2, members):
-        first = (((wide_at // members) ^ (groups - 1)) * members + ((wide_at % members) ^ swap)) * piece
+        first = (wide_at ^ ((groups - 1) * members + swap)) * piece
         heads.append(lax.dynamic_slice_in_dim(child_pattern, first, piece, 3))
     near = swap_with(child_pattern, 1)
     heads = [swap_with(head, swap + 2) for swap, head in enumerate(heads)]
@@ -656,7 +662,7 @@
     (arrived[0],) = sums_of(jobs, data, jnp.float32, 1)
     done = [(top, columns_of(inner), done[0]), (top, columns_of(outer), done[1])]
     held = arrived
-    whole = f32(2 * sources * out_rows, LANES)
+    whole = f32(2, sources * out_rows, LANES)
     (_, early_columns, early_array), (_, late_columns, late_array) = done
     parent_pattern, far_field, early_pattern = pl.pallas_call(
         functools.partial(finish_ahead_kernel, 0, top, early_columns, members, boxes, sources, out_rows),
@@ -680,7 +686,7 @@
             pltpu.VMEM((len(steps) + 1, *whole.shape), jnp.float32),
             pltpu.VMEM(whole.shape, jnp.float32),
             pltpu.SemaphoreType.DMA,
-            pltpu.SemaphoreType.DMA((2 * parts * (len(steps) + 2),)),
+            pltpu.SemaphoreType.DMA((1 + parts * (len(steps) + 1),)),
         ],
         compiler_params=limit,
         cost_estimate=cost(30),

time: 41.9 us -> 41.7 us (level)
  no operation moved by 1% of the time
where the time goes in v4:
time: 41.7 us; the launch traced here: 41.5 us
  starting transfers between devices  21.8 us (52%)
  Pallas kernels  12.5 us (30%)
  waiting for transfers between devices  4.88 us (12%)
  local copies, waits for them, and re-layouts  1.6 us (4%)
  between operations  0.76 us (2%)
    ppermute x10, starting transfers between devices, swap_with(): return lax.ppermute(array, 'wide', [(i, i ^ step) for i in range(n_wide)])  18.3 us
    pallas_call x4, Pallas kernels, sums_of(): pl.pallas_call(functools.partial(combine_kernel, jobs, members, boxes, so...  6.93 us
    ppermute x10, waiting for transfers between devices, swap_with(): return lax.ppermute(array, 'wide', [(i, i ^ step) for i in range(n_wide)])  4.87 us
    ppermute x2, starting transfers between devices, other_half(): return lax.ppermute(array, ('wide', 'narrow'), pairs)  3.48 us
    pallas_call x1, Pallas kernels, grouped(): pl.pallas_call(functools.partial(finish_kernel, steps, top, late_columns,...  1.97 us
    pallas_call x1, Pallas kernels, grouped(): pl.pallas_call(functools.partial(finish_ahead_kernel, 0, top, early_colum...  1.94 us
    dynamic_slice x1, local copies, waits for them, and re-layouts, grouped(): heads.append(lax.dynamic_slice_in_dim(child_pattern, first, piece, 3))  1.04 us
    pallas_call x1, Pallas kernels, grouped(): pl.pallas_call(functools.partial(prep_kernel, groups, members, boxes, pie...  0.96 us
  transfers between devices with their start and end apart: 12, of which 3 were waited for; matrix products, arithmetic and copies ran while one was open for 2% of the time, Pallas kernels for 25%

profile of v4, /device:TPU:0, one launch (start us, length us, event | category | flops | bytes accessed | tf_op | source)
XLA Modules:
  0.0 41.5 jit_solution(15553039174350772979)
XLA Ops:
  0.6 0.5 %collective-permute-start = (bf16[2,2,32,8192]{3,2,1,0:T(8,128)(2,1)}, bf16[2,2,32,8192]{3,2,1,0:T(8,128)(2,1)S(1)}, u32[]{:S(2)}, u32[]{:S(2)}) collective-permute-start(bf16[2,2,32,8192]{3,2,1,0:T(8,128)(2,1)} %refs_0_.6), channel_id=1, source_target_pairs={{0,2},{2,0},{4,6},{6,4},{8,10},{10,8},{12,14},{14,12},{16,18},{18,... | collective-permute-start | bytes 6291464 | tf_op jit(solution)/shard_map/ppermute | solution.py:543
  1.1 0.0 copy-start.3
  1.2 0.0 copy-start.4
  1.2 0.0 copy-start.5
  1.2 0.0 copy-start.6
  1.2 1.0 %constant_dynamic-slice_fusion = (bf16[2,2,32,512]{3,2,1,0:T(8,128)(2,1)S(1)}, bf16[2,2,32,512]{3,2,1,0:T(8,128)(2,1)S(1)}) fusion(bf16[2,2,32,8192]{3,2,1,0:T(8,128)(2,1)} %refs_0_.6, s32[]{:T(128)S(6)} %select_n.7, s32[]{:T(128)S(6)} %select_n.6), kind=kLoop, calls=%fused_computation | loop fusion | bytes 524296 | tf_op jit(solution)/shard_map/dynamic_slice | solution.py:553
  2.2 2.7 %collective-permute-start.5 = (bf16[2,2,32,512]{3,2,1,0:T(8,128)(2,1)S(1)}, bf16[2,2,32,512]{3,2,1,0:T(8,128)(2,1)S(1)}, u32[]{:S(2)}, u32[]{:S(2)}) collective-permute-start(bf16[2,2,32,512]{3,2,1,0:T(8,128)(2,1)S(1)} %get-tuple-element.56), channel_id=1, source_target_pairs={{0,6},{2,4},{4,2},{6,0},{8,14},{10,12},{12,10},{14,8},{16,22},{18,... | collective-permute-start | bytes 393224 | tf_op jit(solution)/shard_map/ppermute | solution.py:543
  4.9 0.0 collective-permute-start.4
  4.9 0.2 axes.1
  5.1 0.0 copy-start
  5.1 0.0 copy-done.3
  5.2 0.0 copy-done.4
  5.2 0.0 copy-done.5
  5.2 0.0 copy-done.6
  5.2 1.0 %prep.1 = (f32[4,8,16,128]{3,2,1,0:T(8,128)S(1)}, f32[4,8,16,128]{3,2,1,0:T(8,128)S(1)}, f32[4,16,128]{2,1,0:T(8,128)S(1)}, f32[4,16,128]{2,1,0:T(8,128)S(1)}, f32[4,16,128]{2,1,0:T(8,128)S(1)}) custom-call(s32[32]{0:T(128)S(1)} %copy-done.3, s32[32]{0:T(128)S(1)} %copy-done.6, f32[4,3]{1,0:T(4,128)S(1)} %copy-done.5, s32[512,128]{1,0:T(8,128)S(1)} %bitcast.3, ...), custom_call_target="tpu_custom_call" | custom-call | flops 1000000000 | bytes 3600001 | tf_op jit(solution)/shard_map/prep/pallas_call | solution.py:569
  6.2 0.0 copy-start.1
  6.2 0.0 copy-start.2
  6.2 0.0 collective-permute-done.near.refs_1_
  6.2 0.5 %copy-done = bf16[2,2,32,8192]{3,2,1,0:T(8,128)(2,1)S(1)} copy-done((bf16[2,2,32,8192]{3,2,1,0:T(8,128)(2,1)S(1)}, bf16[2,2,32,8192]{3,2,1,0:T(8,128)(2,1)}, u32[]{:S(2)}) %copy-start) | copy-done | bytes 2097176
  6.7 0.5 %pack.1 = (bf16[1088,128]{1,0:T(8,128)(2,1)S(1)}, bf16[1056,128]{1,0:T(8,128)(2,1)S(1)}, bf16[1056,128]{1,0:T(8,128)(2,1)S(1)}, bf16[32,128]{1,0:T(8,128)(2,1)S(1)}) custom-call(bf16[2,2,32,8192]{3,2,1,0:T(8,128)(2,1)S(1)} %copy-done, bf16[2,2,32,8192]{3,2,1,0:T(8,128)(2,1)S(1)} %collective-permute-done.near.refs_1_), custom_call_target="tpu_custom_call" | custom-call | flops 1000000000 | bytes 3600001 | tf_op jit(solution)/shard_map/pack/pallas_call | solution.py:588
  7.2 2.9 %collective-permute-start.3 = (bf16[32,128]{1,0:T(8,128)(2,1)S(1)}, bf16[32,128]{1,0:T(8,128)(2,1)S(1)}, u32[]{:S(2)}, u32[]{:S(2)}) collective-permute-start(bf16[32,128]{1,0:T(8,128)(2,1)S(1)} %get-tuple-element.30), channel_id=1, source_target_pairs={{0,5},{1,4},{2,7},{3,6},{4,1},{5,0},{6,3},{7,2},{8,13},{9,12},{10,... | collective-permute-start | bytes 24584 | tf_op jit(solution)/shard_map/ppermute | solution.py:559
  10.2 0.5 %collective-permute-start.2 = (bf16[32,128]{1,0:T(8,128)(2,1)S(1)}, bf16[32,128]{1,0:T(8,128)(2,1)S(1)}, u32[]{:S(2)}, u32[]{:S(2)}) collective-permute-start(bf16[32,128]{1,0:T(8,128)(2,1)S(1)} %get-tuple-element.30), channel_id=1, source_target_pairs={{0,1},{1,0},{2,3},{3,2},{4,5},{5,4},{6,7},{7,6},{8,9},{9,8},{10,11... | collective-permute-start | bytes 24584 | tf_op jit(solution)/shard_map/ppermute | solution.py:559
  10.7 0.1 collective-permute-start.1
  10.8 0.0 collective-permute-done.5.refs_6_.refs_3_
  10.8 1.2 %collective-permute-done.4.refs_5_.refs_2_ = bf16[2,2,32,512]{3,2,1,0:T(8,128)(2,1)S(1)} collective-permute-done((bf16[2,2,32,512]{3,2,1,0:T(8,128)(2,1)S(1)}, bf16[2,2,32,512]{3,2,1,0:T(8,128)(2,1)S(1)}, u32[]{:S(2)}, u32[]{:S(2)}) %collective-permute-start.4) | collective-permute-done | bytes 131104 | tf_op jit(solution)/shard_map/ppermute | solution.py:543
  11.9 0.0 copy-done.1
  11.9 0.0 copy-done.2
  11.9 1.1 %combine.5 = bf16[768,128]{1,0:T(8,128)(2,1)S(1)} custom-call(bf16[2,2,32,8192]{3,2,1,0:T(8,128)(2,1)S(1)} %copy-done, bf16[2,2,32,8192]{3,2,1,0:T(8,128)(2,1)S(1)} %collective-permute-done.near.refs_1_, bf16[2,2,32,512]{3,2,1,0:T(8,128)(2,1)S(1)} %collective-permute-done.4.refs_5_.refs_2_, ...), custom_call_target="tpu_custom_call" | custom-call | flops 5000000000 | bytes 18000000 | tf_op jit(solution)/shard_map/combine/pallas_call | solution.py:611
  13.0 3.7 %collective-permute-start.10 = (bf16[768,128]{1,0:T(8,128)(2,1)S(1)}, bf16[768,128]{1,0:T(8,128)(2,1)S(1)}, u32[]{:S(2)}, u32[]{:S(2)}) collective-permute-start(bf16[768,128]{1,0:T(8,128)(2,1)S(1)} %combine.5), channel_id=1, source_target_pairs={{0,24},{2,26},{4,28},{6,30},{8,16},{10,18},{12,20},{14,22},{16,8},... | collective-permute-start | bytes 589832 | tf_op jit(solution)/shard_map/ppermute | solution.py:543
  16.7 2.0 %collective-permute-start.7 = (bf16[1056,128]{1,0:T(8,128)(2,1)S(1)}, bf16[1056,128]{1,0:T(8,128)(2,1)S(1)}, u32[]{:S(2)}, u32[]{:S(2)}) collective-permute-start(bf16[1056,128]{1,0:T(8,128)(2,1)S(1)} %get-tuple-element.41), channel_id=1, source_target_pairs={{0,4},{2,6},{4,0},{6,2},{8,12},{10,14},{12,8},{14,10},{16,20},{18,... | collective-permute-start | bytes 811016 | tf_op jit(solution)/shard_map/ppermute | solution.py:543
  18.8 0.0 collective-permute-done.3.refs_4_
  18.8 0.0 collective-permute-done.2.refs_3_
  18.8 0.0 collective-permute-done.1.refs_2_
  18.8 2.2 %combine.4 = (bf16[1040,128]{1,0:T(8,128)(2,1)S(1)}, bf16[256,128]{1,0:T(8,128)(2,1)S(1)}) custom-call(bf16[2,2,32,8192]{3,2,1,0:T(8,128)(2,1)S(1)} %copy-done, bf16[2,2,32,8192]{3,2,1,0:T(8,128)(2,1)S(1)} %collective-permute-done.near.refs_1_, bf16[1088,128]{1,0:T(8,128)(2,1)S(1)} %collective-permute-done.1.refs_2_, ...), custom_call_target="tpu_custom_call" | custom-call | flops 30000001024 | bytes 108000000 | tf_op jit(solution)/shard_map/combine/pallas_call | solution.py:611
  21.0 4.2 %collective-permute-start.6 = (bf16[1040,128]{1,0:T(8,128)(2,1)S(1)}, bf16[1040,128]{1,0:T(8,128)(2,1)S(1)}, u32[]{:S(2)}, u32[]{:S(2)}) collective-permute-start(bf16[1040,128]{1,0:T(8,128)(2,1)S(1)} %get-tuple-element.39), channel_id=1, source_target_pairs={{0,16},{2,18},{4,20},{6,22},{8,24},{10,26},{12,28},{14,30},{16,0},... | collective-permute-start | bytes 798728 | tf_op jit(solution)/shard_map/ppermute | solution.py:543
  25.2 0.5 %collective-permute-start.11 = (bf16[1056,128]{1,0:T(8,128)(2,1)S(1)}, bf16[1056,128]{1,0:T(8,128)(2,1)S(1)}, u32[]{:S(2)}, u32[]{:S(2)}) collective-permute-start(bf16[1056,128]{1,0:T(8,128)(2,1)S(1)} %get-tuple-element.45), channel_id=1, source_target_pairs={{0,4},{2,6},{4,0},{6,2},{8,12},{10,14},{12,8},{14,10},{16,20},{18,... | collective-permute-start | bytes 811016 | tf_op jit(solution)/shard_map/ppermute | solution.py:543
  25.7 0.0 collective-permute-done.7.refs_2_
  25.7 1.8 %combine.6 = bf16[1024,128]{1,0:T(8,128)(2,1)S(1)} custom-call(bf16[2,2,32,8192]{3,2,1,0:T(8,128)(2,1)S(1)} %copy-done, bf16[2,2,32,8192]{3,2,1,0:T(8,128)(2,1)S(1)} %collective-permute-done.near.refs_1_, bf16[1056,128]{1,0:T(8,128)(2,1)S(1)} %collective-permute-done.7.refs_2_, bf16[32,128]{1,0:T(8,128)(2,1)S(1)} %collective-permute-done.2.refs_3_, ...), custom_call_target="tpu_custom_call" | custom-call | flops 2000000000 | bytes 7200001 | tf_op jit(solution)/shard_map/combine/pallas_call | solution.py:611
  27.5 1.6 %collective-permute-start.8 = (bf16[1024,128]{1,0:T(8,128)(2,1)S(1)}, bf16[1024,128]{1,0:T(8,128)(2,1)S(1)}, u32[]{:S(2)}, u32[]{:S(2)}) collective-permute-start(bf16[1024,128]{1,0:T(8,128)(2,1)S(1)} %combine.6), channel_id=1, source_target_pairs={{0,8},{2,10},{4,12},{6,14},{8,0},{10,2},{12,4},{14,6},{16,24},{18,... | collective-permute-start | bytes 786440 | tf_op jit(solution)/shard_map/ppermute | solution.py:543
  29.2 0.0 collective-permute-done.10.early
  29.2 2.9 %collective-permute-start.9 = (bf16[256,128]{1,0:T(8,128)(2,1)S(1)}, bf16[256,128]{1,0:T(8,128)(2,1)S(1)}, u32[]{:S(2)}, u32[]{:S(2)}) collective-permute-start(bf16[256,128]{1,0:T(8,128)(2,1)S(1)} %get-tuple-element.42), channel_id=1, source_target_pairs={{0,24},{2,26},{4,28},{6,30},{8,16},{10,18},{12,20},{14,22},{16,8},... | collective-permute-start | bytes 196616 | tf_op jit(solution)/shard_map/ppermute | solution.py:543
  32.1 0.0 collective-permute-done.11.refs_2_
  32.1 1.8 %combine.7.own = f32[1024,128]{1,0:T(8,128)S(1)} custom-call(bf16[2,2,32,8192]{3,2,1,0:T(8,128)(2,1)S(1)} %copy-done, bf16[2,2,32,8192]{3,2,1,0:T(8,128)(2,1)S(1)} %collective-permute-done.near.refs_1_, bf16[1056,128]{1,0:T(8,128)(2,1)S(1)} %collective-permute-done.11.refs_2_, bf16[32,128]{1,0:T(8,128)(2,1)S(1)} %collective-permute-done.2.refs_3_, ...), custom_call_target="tpu_custom_call" | custom-call | flops 1000000000 | bytes 3600001 | tf_op jit(solution)/shard_map/combine/pallas_call | solution.py:611
  33.9 1.9 %finish_ahead.1 = (f32[4,2,512,128]{3,2,1,0:T(8,128)}, f32[2,512,128]{2,1,0:T(8,128)S(1)}, f32[2,512,128]{2,1,0:T(8,128)S(1)}) custom-call(s32[32]{0:T(128)S(1)} %copy-done.3, f32[1024,128]{1,0:T(8,128)S(1)} %combine.7.own, bf16[768,128]{1,0:T(8,128)(2,1)S(1)} %collective-permute-done.10.early, f32[4,16,128]{2,1,0:T(8,128)S(1)} %get-tuple-element.47.center_cos.refs_4_, ...), custom_call_target="tpu_custom_call" | custom-call | bytes 1 | tf_op jit(solution)/shard_map/finish_ahead/pallas_call | solution.py:667
  35.9 2.3 %collective-permute-done.9.refs_2_ = bf16[256,128]{1,0:T(8,128)(2,1)S(1)} collective-permute-done((bf16[256,128]{1,0:T(8,128)(2,1)S(1)}, bf16[256,128]{1,0:T(8,128)(2,1)S(1)}, u32[]{:S(2)}, u32[]{:S(2)}) %collective-permute-start.9) | collective-permute-done | bytes 65568 | tf_op jit(solution)/shard_map/ppermute | solution.py:543
  38.1 1.4 %collective-permute-done.8.refs_1_ = bf16[1024,128]{1,0:T(8,128)(2,1)S(1)} collective-permute-done((bf16[1024,128]{1,0:T(8,128)(2,1)S(1)}, bf16[1024,128]{1,0:T(8,128)(2,1)S(1)}, u32[]{:S(2)}, u32[]{:S(2)}) %collective-permute-start.8) | collective-permute-done | bytes 262176 | tf_op jit(solution)/shard_map/ppermute | solution.py:543
  39.6 0.0 collective-permute-done.6.refs_0_
  39.6 2.0 %finish_last.1 = (f32[4,2,512,128]{3,2,1,0:T(8,128)}, f32[2,512,128]{2,1,0:T(8,128)}) custom-call(s32[32]{0:T(128)S(1)} %copy-done.3, bf16[1040,128]{1,0:T(8,128)(2,1)S(1)} %collective-permute-done.6.refs_0_, bf16[1024,128]{1,0:T(8,128)(2,1)S(1)} %collective-permute-done.8.refs_1_, ...), custom_call_target="tpu_custom_call", output_to_operand_aliasing={{0}: (8, {})} | custom-call | flops 30000001024 | bytes 108000000 | tf_op jit(solution)/shard_map/finish_last/pallas_call | solution.py:678
Async XLA Ops:
  0.6 5.6 %collective-permute-start = (bf16[2,2,32,8192]{3,2,1,0:T(8,128)(2,1)}, bf16[2,2,32,8192]{3,2,1,0:T(8,128)(2,1)S(1)}, u32[]{:S(2)}, u32[]{:S(2)}) collective-permute-start(bf16[2,2,32,8192]{3,2,1,0:T(8,128)(2,1)} %refs_0_.6), channel_id=1, source_target_pairs={{0,2},{2,0},{4,6},{6,4},{8,10},{10,8},{12,14},{14,12},{16,18},{18,... | collective-permute-start | bytes 6291464 | tf_op jit(solution)/shard_map/ppermute | solution.py:543
  1.1 4.0 %copy-start.3 = (s32[32]{0:T(128)S(1)}, s32[32]{0:T(128)}, u32[]{:S(2)}) copy-start(s32[32]{0:T(128)} %parent_of.5) | copy-start | bytes 388
  1.2 4.0 %copy-start.4 = (s32[65536]{0:T(1024)S(1)}, s32[65536]{0:T(1024)}, u32[]{:S(2)}) copy-start(s32[65536]{0:T(1024)} %param.17) | copy-start | bytes 786436
  1.2 4.0 %copy-start.5 = (f32[4,3]{1,0:T(4,128)S(1)}, f32[4,3]{1,0:T(4,128)}, u32[]{:S(2)}) copy-start(f32[4,3]{1,0:T(4,128)} %center.1) | copy-start | bytes 148
  1.2 4.0 %copy-start.6 = (s32[32]{0:T(128)S(1)}, s32[32]{0:T(128)}, u32[]{:S(2)}) copy-start(s32[32]{0:T(128)} %octant_of.1) | copy-start | bytes 388
  2.2 8.6 %collective-permute-start.5 = (bf16[2,2,32,512]{3,2,1,0:T(8,128)(2,1)S(1)}, bf16[2,2,32,512]{3,2,1,0:T(8,128)(2,1)S(1)}, u32[]{:S(2)}, u32[]{:S(2)}) collective-permute-start(bf16[2,2,32,512]{3,2,1,0:T(8,128)(2,1)S(1)} %get-tuple-element.56), channel_id=1, source_target_pairs={{0,6},{2,4},{4,2},{6,0},{8,14},{10,12},{12,10},{14,8},{16,22},{18,... | collective-permute-start | bytes 393224 | tf_op jit(solution)/shard_map/ppermute | solution.py:543
  4.9 7.0 %collective-permute-start.4 = (bf16[2,2,32,512]{3,2,1,0:T(8,128)(2,1)S(1)}, bf16[2,2,32,512]{3,2,1,0:T(8,128)(2,1)S(1)}, u32[]{:S(2)}, u32[]{:S(2)}) collective-permute-start(bf16[2,2,32,512]{3,2,1,0:T(8,128)(2,1)S(1)} %get-tuple-element.57), channel_id=1, source_target_pairs={{0,4},{2,6},{4,0},{6,2},{8,12},{10,14},{12,8},{14,10},{16,20},{18,... | collective-permute-start | bytes 393224 | tf_op jit(solution)/shard_map/ppermute | solution.py:543
  5.1 1.6 %copy-start = (bf16[2,2,32,8192]{3,2,1,0:T(8,128)(2,1)S(1)}, bf16[2,2,32,8192]{3,2,1,0:T(8,128)(2,1)}, u32[]{:S(2)}) copy-start(bf16[2,2,32,8192]{3,2,1,0:T(8,128)(2,1)} %refs_0_.6) | copy-start | bytes 6291460
  6.2 5.8 %copy-start.1 = (bf16[256,256]{1,0:T(8,128)(2,1)S(1)}, bf16[256,256]{1,0:T(8,128)(2,1)}, u32[]{:S(2)}) copy-start(bf16[256,256]{1,0:T(8,128)(2,1)} %constant.21.clone.refs_11_.refs_8_.refs_9_) | copy-start | bytes 393220
  6.2 5.8 %copy-start.2 = (bf16[256,256]{1,0:T(8,128)(2,1)S(1)}, bf16[256,256]{1,0:T(8,128)(2,1)}, u32[]{:S(2)}) copy-start(bf16[256,256]{1,0:T(8,128)(2,1)} %constant.20.clone.refs_10_.refs_7_.refs_8_) | copy-start | bytes 393220
  7.2 11.5 %collective-permute-start.3 = (bf16[32,128]{1,0:T(8,128)(2,1)S(1)}, bf16[32,128]{1,0:T(8,128)(2,1)S(1)}, u32[]{:S(2)}, u32[]{:S(2)}) collective-permute-start(bf16[32,128]{1,0:T(8,128)(2,1)S(1)} %get-tuple-element.30), channel_id=1, source_target_pairs={{0,5},{1,4},{2,7},{3,6},{4,1},{5,0},{6,3},{7,2},{8,13},{9,12},{10,... | collective-permute-start | bytes 24584 | tf_op jit(solution)/shard_map/ppermute | solution.py:559
  10.2 8.6 %collective-permute-start.2 = (bf16[32,128]{1,0:T(8,128)(2,1)S(1)}, bf16[32,128]{1,0:T(8,128)(2,1)S(1)}, u32[]{:S(2)}, u32[]{:S(2)}) collective-permute-start(bf16[32,128]{1,0:T(8,128)(2,1)S(1)} %get-tuple-element.30), channel_id=1, source_target_pairs={{0,1},{1,0},{2,3},{3,2},{4,5},{5,4},{6,7},{7,6},{8,9},{9,8},{10,11... | collective-permute-start | bytes 24584 | tf_op jit(solution)/shard_map/ppermute | solution.py:559
  10.7 8.0 %collective-permute-start.1 = (bf16[1088,128]{1,0:T(8,128)(2,1)S(1)}, bf16[1088,128]{1,0:T(8,128)(2,1)S(1)}, u32[]{:S(2)}, u32[]{:S(2)}) collective-permute-start(bf16[1088,128]{1,0:T(8,128)(2,1)S(1)} %get-tuple-element.29), channel_id=1, source_target_pairs={{0,4},{2,6},{4,0},{6,2},{8,12},{10,14},{12,8},{14,10},{16,20},{18,... | collective-permute-start | bytes 835592 | tf_op jit(solution)/shard_map/ppermute | solution.py:543
  13.0 16.2 %collective-permute-start.10 = (bf16[768,128]{1,0:T(8,128)(2,1)S(1)}, bf16[768,128]{1,0:T(8,128)(2,1)S(1)}, u32[]{:S(2)}, u32[]{:S(2)}) collective-permute-start(bf16[768,128]{1,0:T(8,128)(2,1)S(1)} %combine.5), channel_id=1, source_target_pairs={{0,24},{2,26},{4,28},{6,30},{8,16},{10,18},{12,20},{14,22},{16,8},... | collective-permute-start | bytes 589832 | tf_op jit(solution)/shard_map/ppermute | solution.py:543
  16.7 9.0 %collective-permute-start.7 = (bf16[1056,128]{1,0:T(8,128)(2,1)S(1)}, bf16[1056,128]{1,0:T(8,128)(2,1)S(1)}, u32[]{:S(2)}, u32[]{:S(2)}) collective-permute-start(bf16[1056,128]{1,0:T(8,128)(2,1)S(1)} %get-tuple-element.41), channel_id=1, source_target_pairs={{0,4},{2,6},{4,0},{6,2},{8,12},{10,14},{12,8},{14,10},{16,20},{18,... | collective-permute-start | bytes 811016 | tf_op jit(solution)/shard_map/ppermute | solution.py:543
  21.0 18.6 %collective-permute-start.6 = (bf16[1040,128]{1,0:T(8,128)(2,1)S(1)}, bf16[1040,128]{1,0:T(8,128)(2,1)S(1)}, u32[]{:S(2)}, u32[]{:S(2)}) collective-permute-start(bf16[1040,128]{1,0:T(8,128)(2,1)S(1)} %get-tuple-element.39), channel_id=1, source_target_pairs={{0,16},{2,18},{4,20},{6,22},{8,24},{10,26},{12,28},{14,30},{16,0},... | collective-permute-start | bytes 798728 | tf_op jit(solution)/shard_map/ppermute | solution.py:543
  25.2 6.9 %collective-permute-start.11 = (bf16[1056,128]{1,0:T(8,128)(2,1)S(1)}, bf16[1056,128]{1,0:T(8,128)(2,1)S(1)}, u32[]{:S(2)}, u32[]{:S(2)}) collective-permute-start(bf16[1056,128]{1,0:T(8,128)(2,1)S(1)} %get-tuple-element.45), channel_id=1, source_target_pairs={{0,4},{2,6},{4,0},{6,2},{8,12},{10,14},{12,8},{14,10},{16,20},{18,... | collective-permute-start | bytes 811016 | tf_op jit(solution)/shard_map/ppermute | solution.py:543
  27.5 12.0 %collective-permute-start.8 = (bf16[1024,128]{1,0:T(8,128)(2,1)S(1)}, bf16[1024,128]{1,0:T(8,128)(2,1)S(1)}, u32[]{:S(2)}, u32[]{:S(2)}) collective-permute-start(bf16[1024,128]{1,0:T(8,128)(2,1)S(1)} %combine.6), channel_id=1, source_target_pairs={{0,8},{2,10},{4,12},{6,14},{8,0},{10,2},{12,4},{14,6},{16,24},{18,... | collective-permute-start | bytes 786440 | tf_op jit(solution)/shard_map/ppermute | solution.py:543
  29.2 9.0 %collective-permute-start.9 = (bf16[256,128]{1,0:T(8,128)(2,1)S(1)}, bf16[256,128]{1,0:T(8,128)(2,1)S(1)}, u32[]{:S(2)}, u32[]{:S(2)}) collective-permute-start(bf16[256,128]{1,0:T(8,128)(2,1)S(1)} %get-tuple-element.42), channel_id=1, source_target_pairs={{0,24},{2,26},{4,28},{6,30},{8,16},{10,18},{12,20},{14,22},{16,8},... | collective-permute-start | bytes 196616 | tf_op jit(solution)/shard_map/ppermute | solution.py:543

commit v5 on v4

--- a/solution.py
+++ b/solution.py
@@ -184,6 +184,19 @@
     return np.concatenate([high, low], axis=1)
 
 
+def shift_of(step, groups):
+    half = groups // 2
+    return ([0] + [half, *(shift for shift in range(1, groups) if shift != half)][::-1])[step]
+
+
+def group_after(group, step, groups):
+    return (group + shift_of(step, groups)) & (groups - 1)
+
+
+def group_before(group, step, groups):
+    return (group + groups - shift_of(step, groups)) & (groups - 1)
+
+
 def rim_masks():
     slot = lax.broadcasted_iota(jnp.int32, (RIM, LANES), 0)
     lane = lax.broadcasted_iota(jnp.int32, (RIM, LANES), 1)
@@ -225,7 +238,7 @@
         for swap in range(2, members, 2):
             out, base = outs[(part - 1) * (members // 2 - 1) + swap // 2 - 1], 0
             target = member_at ^ swap
-            first = ((group_at ^ (groups - 1 - part)) * members + target) * piece
+            first = (group_after(group_at, groups - 1 - part, groups) * members + target) * piece
             for ref in (cells, near):
                 for index in range(tiles):
                     out[base : base + rows, :] = tile(ref, first + index * LANES)
@@ -233,7 +246,7 @@
                 out[base : base + RIM, :] = rim_at(ref, first).astype(jnp.bfloat16)
                 base += RIM
                 if part == 1:
-                    rim = rim_at(ref, ((group_at ^ (groups - 1)) * members + target) * piece)
+                    rim = rim_at(ref, (group_after(group_at, groups - 1, groups) * members + target) * piece)
                     out[base : base + RIM, :] = rim.astype(jnp.bfloat16)
                     base += RIM
 
@@ -258,7 +271,8 @@
     lane = lax.broadcasted_iota(jnp.int32, (rows, LANES), 1)
     cos_azimuth, sin_azimuth = turned((((row * LANES + lane) & 255).astype(jnp.float32) + 0.5) / 256.0)
     for step in range(groups):
-        first_row = lax.axis_index("narrow") * half_rows + ((group_at ^ step) * members + member_at) * rows
+        at = group_after(group_at, step, groups) * members + member_at
+        first_row = lax.axis_index("narrow") * half_rows + at * rows
         ring = ((first_row + row) * LANES + lane) >> 8
         dir_z, sin_polar = turned((ring.astype(jnp.float32) + 0.5) / (2 * (sample_count // 256)))
         for axis, direction in enumerate((sin_polar * cos_azimuth, sin_polar * sin_azimuth, dir_z)):
@@ -278,7 +292,9 @@
     row = lax.broadcasted_iota(jnp.int32, (rows, LANES), 0)
     lane = lax.broadcasted_iota(jnp.int32, (rows, LANES), 1)
     first_rows = [
-        pl.multiple_of(lax.axis_index("narrow") * half_rows + ((group_at ^ step) * members + member_at) * rows, 8)
+        pl.multiple_of(
+            lax.axis_index("narrow") * half_rows + (group_after(group_at, step, groups) * members + member_at) * rows, 8
+        )
         for step in range(groups)
     ]
     copies = [
@@ -288,7 +304,7 @@
         copy.start()
     scale = 1.0 / math.sqrt(center.shape[0])
     for step in range(groups):
-        parent = parent_of[(group_at ^ step) * members * boxes]
+        parent = parent_of[group_before(group_at, step, groups) * members * boxes]
         turns = sum(center[parent, axis] * center_dirs[axis] for axis in range(3))
         turn_cos, turn_sin = turned(turns)
         center_cos[step] = turn_cos * scale
@@ -337,7 +353,8 @@
     block = data[0].shape[3]
     wide_at = lax.axis_index("wide")
     last = lax.axis_size("wide") - 1
-    at = ((wide_at // members) ^ step) * members + wide_at % members
+    groups = lax.axis_size("wide") // members
+    at = group_after(wide_at // members, step, groups) * members + wide_at % members
     first = at * (tiles * LANES)
 
     def local(ref, lane):
@@ -434,9 +451,7 @@
         if turn:
             sum_window(turn - 1)
     if whole:
-        out[: 2 * sources * width, :] = total[: 2 * sources * width, :].astype(out.dtype)
-    if out.shape[0] > 2 * sources * width:
-        out[2 * sources * width :, :] = jnp.zeros((out.shape[0] - 2 * sources * width, LANES), out.dtype)
+        out[...] = total[...].astype(out.dtype)
 
 
 def place_columns(arrived, columns, sources, rows, cosines, sines, pattern, far):
@@ -452,19 +467,25 @@
         far[1, at, :] += sine * real + cosine * imag
 
 
-def finish_ahead_kernel(
-    own_step, early_step, columns, members, boxes, sources, rows,
-    parent_of, own, early, center_cos, center_sin, parent_out, far_out, early_out,
-):
-    name = parent_of[((lax.axis_index("wide") // members) ^ own_step) * members * boxes]
-    cosine, sine = center_cos[own_step], center_sin[own_step]
+def finish_ahead_kernel(steps, early_step, columns, members, boxes, sources, rows, parent_of, *refs):
+    whole, (early, center_cos, center_sin, parent_out, far_out, early_out) = refs[: len(steps)], refs[len(steps) :]
+    groups = lax.axis_size("wide") // members
+    group_at = lax.axis_index("wide") // members
+    names = [parent_of[group_before(group_at, step, groups) * members * boxes] for step in steps]
     for source in range(sources):
         at = pl.ds(source * rows, rows)
-        real, imag = (own[pl.ds((half * sources + source) * rows, rows), :] for half in range(2))
-        parent_out[name, 0, at, :] = real
-        parent_out[name, 1, at, :] = imag
-        far_out[0, at, :] = cosine * real - sine * imag
-        far_out[1, at, :] = sine * real + cosine * imag
+        far_real = far_imag = 0.0
+        for index, step in enumerate(steps):
+            real, imag = (
+                whole[index][pl.ds((half * sources + source) * rows, rows), :].astype(jnp.float32) for half in range(2)
+            )
+            cosine, sine = center_cos[step], center_sin[step]
+            parent_out[names[index], 0, at, :] = real
+            parent_out[names[index], 1, at, :] = imag
+            far_real = far_real + (cosine * real - sine * imag)
+            far_imag = far_imag + (sine * real + cosine * imag)
+        far_out[0, at, :] = far_real
+        far_out[1, at, :] = far_imag
     place_columns(
         early, columns, sources, rows, center_cos.at[early_step], center_sin.at[early_step], early_out, far_out
     )
@@ -489,7 +510,8 @@
         late, columns, sources, rows, center_cos.at[early_step], center_sin.at[early_step], held.at[last], far_held
     )
     name_copy.wait()
-    places = [names[(group_at ^ step) * members * boxes] for step in (*steps, early_step)]
+    groups = lax.axis_size("wide") // members
+    places = [names[group_before(group_at, step, groups) * members * boxes] for step in (*steps, early_step)]
     send(held.at[last], parent_out.at[places[last]])
     each = sources // parts
     for part in range(parts):
@@ -542,6 +564,10 @@
     def swap_with(array, step):
         return lax.ppermute(array, "wide", [(i, i ^ step) for i in range(n_wide)])
 
+    def move_by(array, step):
+        shift = shift_of(step, groups) * members
+        return lax.ppermute(array, "wide", [(i, (i + shift) % n_wide) for i in range(n_wide)])
+
     def tie(*arrays):
         return lax.optimization_barrier(arrays)
 
@@ -549,7 +575,7 @@
     wide_at = lax.axis_index("wide")
     heads = []
     for swap in range(2, members):
-        first = (wide_at ^ ((groups - 1) * members + swap)) * piece
+        first = (wide_at ^ (groups // 2 * members + swap)) * piece
         heads.append(lax.dynamic_slice_in_dim(child_pattern, first, piece, 3))
     near = swap_with(child_pattern, 1)
     heads = [swap_with(head, swap + 2) for swap, head in enumerate(heads)]
@@ -603,10 +629,7 @@
     top = groups - 1
 
     def sums_of(jobs, data, dtype, micros):
-        shapes = [
-            jax.ShapeDtypeStruct((2 * sources * len(columns_of(job[1])) + (RIM if job[0] == top - 1 else 0), LANES), dtype)
-            for job in jobs
-        ]
+        shapes = [jax.ShapeDtypeStruct((2 * sources * len(columns_of(job[1])), LANES), dtype) for job in jobs]
         inputs = [*data, cosines, sines, excess, bands[0], bands[1]]
         return pl.pallas_call(
             functools.partial(combine_kernel, jobs, members, boxes, sources, tiles, len(data)),
@@ -632,7 +655,7 @@
     early_sends = sends[pairs : 2 * pairs]
     *early_sends, total = tie(*early_sends, total)
     sends[pairs : 2 * pairs] = early_sends
-    done = [swap_with(total, top * members)]
+    done = [move_by(total, top)]
     arrived = {}
     for part in range(1, groups):
         step = top - part
@@ -642,9 +665,9 @@
             if part < groups - 1:
                 tied = tie(*sends[part * pairs : (part + 1) * pairs], *totals)
                 sends[part * pairs : (part + 1) * pairs], totals = tied[:pairs], list(tied[pairs:])
-            arrived[step + 1] = swap_with(totals[0], (step + 1) * members)
+            arrived[step + 1] = move_by(totals[0], step + 1)
             if part == 2:
-                done.append(swap_with(totals[1], top * members))
+                done.append(move_by(totals[1], top))
         got = [swap_with(array, 2 * pair + 2) for pair, array in enumerate(sent)]
         length = full + (RIM if part == 1 else 0)
         places = [(2 + member // 2, member % 2 * length) for member in range(far)]
@@ -664,16 +687,17 @@
     held = arrived
     whole = f32(2, sources * out_rows, LANES)
     (_, early_columns, early_array), (_, late_columns, late_array) = done
+    ahead = [0, *range(2, top)]
     parent_pattern, far_field, early_pattern = pl.pallas_call(
-        functools.partial(finish_ahead_kernel, 0, top, early_columns, members, boxes, sources, out_rows),
+        functools.partial(finish_ahead_kernel, ahead, top, early_columns, members, boxes, sources, out_rows),
         out_shape=[f32(parents, *whole.shape), whole, whole],
-        in_specs=[smem] + [vmem] * 4,
+        in_specs=[smem] + [vmem] * (len(ahead) + 3),
         out_specs=[vmem] * 3,
         compiler_params=limit,
         cost_estimate=cost(0),
         name="finish_ahead",
-    )(child_parent, held[0], early_array, center_cos, center_sin)
-    steps = sorted((step for step in held if step), reverse=True)
+    )(child_parent, *[held[step] for step in ahead], early_array, center_cos, center_sin)
+    steps = [1]
     parts = 4
     parent_pattern, far_field = pl.pallas_call(
         functools.partial(finish_kernel, steps, top, late_columns, members, boxes, sources, out_rows, parts),

time: 41.7 us -> 40.9 us (0.981)
  starting transfers between devices: 21.8 us -> 18.4 us
  waiting for transfers between devices: 4.88 us -> 7.31 us
    ppermute x10 -> x6, starting transfers between devices: 18.3 us -> 6.01 us  [swap_with(): return lax.ppermute(array, 'wide', [(i, i ^ step) for i in range(n_wide)])]
    ppermute x0 -> x4, starting transfers between devices: none -> 8.96 us  [move_by(): lax.ppermute(array, 'wide', [(i, (i + shift) % n_wide) for i in range(n_w...]
    ppermute x0 -> x4, waiting for transfers between devices: none -> 3.27 us  [move_by(): lax.ppermute(array, 'wide', [(i, (i + shift) % n_wide) for i in range(n_w...]
    ppermute x10 -> x6, waiting for transfers between devices: 4.87 us -> 4.03 us  [swap_with(): return lax.ppermute(array, 'wide', [(i, i ^ step) for i in range(n_wide)])]
  transfers between devices with their start and end apart: 12 -> 12, of which waited for: 3 -> 4; matrix products, arithmetic and copies ran while one was open for 2% -> 3% of each run, Pallas kernels for 25% -> 27%
where the time goes in v5:
time: 40.9 us; the launch traced here: 40.7 us
  starting transfers between devices  18.4 us (45%)
  Pallas kernels  12.6 us (31%)
  waiting for transfers between devices  7.31 us (18%)
  local copies, waits for them, and re-layouts  1.6 us (4%)
  between operations  0.77 us (2%)
    ppermute x4, starting transfers between devices, move_by(): lax.ppermute(array, 'wide', [(i, (i + shift) % n_wide) for i in range(n_w...  8.96 us
    pallas_call x4, Pallas kernels, sums_of(): pl.pallas_call(functools.partial(combine_kernel, jobs, members, boxes, so...  6.94 us
    ppermute x6, starting transfers between devices, swap_with(): return lax.ppermute(array, 'wide', [(i, i ^ step) for i in range(n_wide)])  6.01 us
    ppermute x6, waiting for transfers between devices, swap_with(): return lax.ppermute(array, 'wide', [(i, i ^ step) for i in range(n_wide)])  4.03 us
    ppermute x2, starting transfers between devices, other_half(): return lax.ppermute(array, ('wide', 'narrow'), pairs)  3.48 us
    ppermute x4, waiting for transfers between devices, move_by(): lax.ppermute(array, 'wide', [(i, (i + shift) % n_wide) for i in range(n_w...  3.27 us
    pallas_call x1, Pallas kernels, grouped(): pl.pallas_call(functools.partial(finish_ahead_kernel, ahead, top, early_c...  2.22 us
    pallas_call x1, Pallas kernels, grouped(): pl.pallas_call(functools.partial(finish_kernel, steps, top, late_columns,...  1.76 us
  transfers between devices with their start and end apart: 12, of which 4 were waited for; matrix products, arithmetic and copies ran while one was open for 3% of the time, Pallas kernels for 27%

profile of v5, /device:TPU:0, one launch (start us, length us, event | category | flops | bytes accessed | tf_op | source)
XLA Modules:
  0.0 40.7 jit_solution(1345362137456806955)
XLA Ops:
  0.6 0.5 %collective-permute-start = (bf16[2,2,32,8192]{3,2,1,0:T(8,128)(2,1)}, bf16[2,2,32,8192]{3,2,1,0:T(8,128)(2,1)S(1)}, u32[]{:S(2)}, u32[]{:S(2)}) collective-permute-start(bf16[2,2,32,8192]{3,2,1,0:T(8,128)(2,1)} %refs_0_.6), channel_id=1, source_target_pairs={{0,2},{2,0},{4,6},{6,4},{8,10},{10,8},{12,14},{14,12},{16,18},{18,... | collective-permute-start | bytes 6291464 | tf_op jit(solution)/shard_map/ppermute | solution.py:565
  1.1 0.0 copy-start.3
  1.2 0.0 copy-start.4
  1.2 0.0 copy-start.5
  1.2 0.0 copy-start.6
  1.2 1.0 %constant_dynamic-slice_fusion = (bf16[2,2,32,512]{3,2,1,0:T(8,128)(2,1)S(1)}, bf16[2,2,32,512]{3,2,1,0:T(8,128)(2,1)S(1)}) fusion(bf16[2,2,32,8192]{3,2,1,0:T(8,128)(2,1)} %refs_0_.6, s32[]{:T(128)S(6)} %select_n.7, s32[]{:T(128)S(6)} %select_n.6), kind=kLoop, calls=%fused_computation | loop fusion | bytes 524296 | tf_op jit(solution)/shard_map/dynamic_slice | solution.py:579
  2.2 2.7 %collective-permute-start.2 = (bf16[2,2,32,512]{3,2,1,0:T(8,128)(2,1)S(1)}, bf16[2,2,32,512]{3,2,1,0:T(8,128)(2,1)S(1)}, u32[]{:S(2)}, u32[]{:S(2)}) collective-permute-start(bf16[2,2,32,512]{3,2,1,0:T(8,128)(2,1)S(1)} %get-tuple-element.56), channel_id=1, source_target_pairs={{0,6},{2,4},{4,2},{6,0},{8,14},{10,12},{12,10},{14,8},{16,22},{18,... | collective-permute-start | bytes 393224 | tf_op jit(solution)/shard_map/ppermute | solution.py:565
  4.9 0.0 collective-permute-start.1
  4.9 0.2 axes.1
  5.1 0.0 copy-start
  5.1 0.0 copy-done.3
  5.2 0.0 copy-done.4
  5.2 0.0 copy-done.5
  5.2 0.0 copy-done.6
  5.2 1.0 %prep.1 = (f32[4,8,16,128]{3,2,1,0:T(8,128)S(1)}, f32[4,8,16,128]{3,2,1,0:T(8,128)S(1)}, f32[4,16,128]{2,1,0:T(8,128)S(1)}, f32[4,16,128]{2,1,0:T(8,128)S(1)}, f32[4,16,128]{2,1,0:T(8,128)S(1)}) custom-call(s32[32]{0:T(128)S(1)} %copy-done.3, s32[32]{0:T(128)S(1)} %copy-done.6, f32[4,3]{1,0:T(4,128)S(1)} %copy-done.5, s32[512,128]{1,0:T(8,128)S(1)} %bitcast.3, ...), custom_call_target="tpu_custom_call" | custom-call | flops 1000000000 | bytes 3600001 | tf_op jit(solution)/shard_map/prep/pallas_call | solution.py:595
  6.2 0.0 copy-start.1
  6.2 0.0 copy-start.2
  6.2 0.0 collective-permute-done.near.refs_1_
  6.2 0.5 %copy-done = bf16[2,2,32,8192]{3,2,1,0:T(8,128)(2,1)S(1)} copy-done((bf16[2,2,32,8192]{3,2,1,0:T(8,128)(2,1)S(1)}, bf16[2,2,32,8192]{3,2,1,0:T(8,128)(2,1)}, u32[]{:S(2)}) %copy-start) | copy-done | bytes 2097176
  6.7 0.5 %pack.1 = (bf16[1088,128]{1,0:T(8,128)(2,1)S(1)}, bf16[1056,128]{1,0:T(8,128)(2,1)S(1)}, bf16[1056,128]{1,0:T(8,128)(2,1)S(1)}, bf16[32,128]{1,0:T(8,128)(2,1)S(1)}) custom-call(bf16[2,2,32,8192]{3,2,1,0:T(8,128)(2,1)S(1)} %copy-done, bf16[2,2,32,8192]{3,2,1,0:T(8,128)(2,1)S(1)} %collective-permute-done.near.refs_1_), custom_call_target="tpu_custom_call" | custom-call | flops 1000000000 | bytes 3600001 | tf_op jit(solution)/shard_map/pack/pallas_call | solution.py:614
  7.2 2.9 %collective-permute-start.5 = (bf16[32,128]{1,0:T(8,128)(2,1)S(1)}, bf16[32,128]{1,0:T(8,128)(2,1)S(1)}, u32[]{:S(2)}, u32[]{:S(2)}) collective-permute-start(bf16[32,128]{1,0:T(8,128)(2,1)S(1)} %get-tuple-element.36), channel_id=1, source_target_pairs={{0,5},{1,4},{2,7},{3,6},{4,1},{5,0},{6,3},{7,2},{8,13},{9,12},{10,... | collective-permute-start | bytes 24584 | tf_op jit(solution)/shard_map/ppermute | solution.py:585
  10.2 0.5 %collective-permute-start.4 = (bf16[32,128]{1,0:T(8,128)(2,1)S(1)}, bf16[32,128]{1,0:T(8,128)(2,1)S(1)}, u32[]{:S(2)}, u32[]{:S(2)}) collective-permute-start(bf16[32,128]{1,0:T(8,128)(2,1)S(1)} %get-tuple-element.36), channel_id=1, source_target_pairs={{0,1},{1,0},{2,3},{3,2},{4,5},{5,4},{6,7},{7,6},{8,9},{9,8},{10,11... | collective-permute-start | bytes 24584 | tf_op jit(solution)/shard_map/ppermute | solution.py:585
  10.7 0.1 collective-permute-start.7
  10.8 0.0 collective-permute-done.2.refs_3_.refs_6_
  10.8 1.2 %collective-permute-done.1.refs_2_.refs_5_ = bf16[2,2,32,512]{3,2,1,0:T(8,128)(2,1)S(1)} collective-permute-done((bf16[2,2,32,512]{3,2,1,0:T(8,128)(2,1)S(1)}, bf16[2,2,32,512]{3,2,1,0:T(8,128)(2,1)S(1)}, u32[]{:S(2)}, u32[]{:S(2)}) %collective-permute-start.1) | collective-permute-done | bytes 131104 | tf_op jit(solution)/shard_map/ppermute | solution.py:565
  11.9 0.0 copy-done.1
  11.9 0.0 copy-done.2
  11.9 1.1 %combine.4 = bf16[768,128]{1,0:T(8,128)(2,1)S(1)} custom-call(bf16[2,2,32,8192]{3,2,1,0:T(8,128)(2,1)S(1)} %copy-done, bf16[2,2,32,8192]{3,2,1,0:T(8,128)(2,1)S(1)} %collective-permute-done.near.refs_1_, bf16[2,2,32,512]{3,2,1,0:T(8,128)(2,1)S(1)} %collective-permute-done.1.refs_2_.refs_5_, ...), custom_call_target="tpu_custom_call" | custom-call | flops 5000000000 | bytes 18000000 | tf_op jit(solution)/shard_map/combine/pallas_call | solution.py:634
  13.0 2.7 %collective-permute-start.9 = (bf16[768,128]{1,0:T(8,128)(2,1)S(1)}, bf16[768,128]{1,0:T(8,128)(2,1)S(1)}, u32[]{:S(2)}, u32[]{:S(2)}) collective-permute-start(bf16[768,128]{1,0:T(8,128)(2,1)S(1)} %combine.4), channel_id=1, source_target_pairs={{0,16},{2,18},{4,20},{6,22},{8,24},{10,26},{12,28},{14,30},{16,0},... | collective-permute-start | bytes 589832 | tf_op jit(solution)/shard_map/ppermute | solution.py:569
  15.7 2.0 %collective-permute-start.3 = (bf16[1056,128]{1,0:T(8,128)(2,1)S(1)}, bf16[1056,128]{1,0:T(8,128)(2,1)S(1)}, u32[]{:S(2)}, u32[]{:S(2)}) collective-permute-start(bf16[1056,128]{1,0:T(8,128)(2,1)S(1)} %get-tuple-element.35), channel_id=1, source_target_pairs={{0,4},{2,6},{4,0},{6,2},{8,12},{10,14},{12,8},{14,10},{16,20},{18,... | collective-permute-start | bytes 811016 | tf_op jit(solution)/shard_map/ppermute | solution.py:565
  17.8 0.0 collective-permute-done.5.refs_4_
  17.8 0.0 collective-permute-done.4.refs_3_
  17.8 1.6 %collective-permute-done.7.refs_2_ = bf16[1088,128]{1,0:T(8,128)(2,1)S(1)} collective-permute-done((bf16[1088,128]{1,0:T(8,128)(2,1)S(1)}, bf16[1088,128]{1,0:T(8,128)(2,1)S(1)}, u32[]{:S(2)}, u32[]{:S(2)}) %collective-permute-start.7) | collective-permute-done | bytes 278560 | tf_op jit(solution)/shard_map/ppermute | solution.py:565
  19.4 2.2 %combine.6 = (bf16[1024,128]{1,0:T(8,128)(2,1)S(1)}, bf16[256,128]{1,0:T(8,128)(2,1)S(1)}) custom-call(bf16[2,2,32,8192]{3,2,1,0:T(8,128)(2,1)S(1)} %copy-done, bf16[2,2,32,8192]{3,2,1,0:T(8,128)(2,1)S(1)} %collective-permute-done.near.refs_1_, bf16[1088,128]{1,0:T(8,128)(2,1)S(1)} %collective-permute-done.7.refs_2_, ...), custom_call_target="tpu_custom_call" | custom-call | flops 30000001024 | bytes 108000000 | tf_op jit(solution)/shard_map/combine/pallas_call | solution.py:634
  21.6 1.6 %collective-permute-start.11 = (bf16[1024,128]{1,0:T(8,128)(2,1)S(1)}, bf16[1024,128]{1,0:T(8,128)(2,1)S(1)}, u32[]{:S(2)}, u32[]{:S(2)}) collective-permute-start(bf16[1024,128]{1,0:T(8,128)(2,1)S(1)} %get-tuple-element.45), channel_id=1, source_target_pairs={{0,8},{2,10},{4,12},{6,14},{8,16},{10,18},{12,20},{14,22},{16,24},... | collective-permute-start | bytes 786440 | tf_op jit(solution)/shard_map/ppermute | solution.py:569
  23.2 0.7 %collective-permute-start.10 = (bf16[1056,128]{1,0:T(8,128)(2,1)S(1)}, bf16[1056,128]{1,0:T(8,128)(2,1)S(1)}, u32[]{:S(2)}, u32[]{:S(2)}) collective-permute-start(bf16[1056,128]{1,0:T(8,128)(2,1)S(1)} %get-tuple-element.44), channel_id=1, source_target_pairs={{0,4},{2,6},{4,0},{6,2},{8,12},{10,14},{12,8},{14,10},{16,20},{18,... | collective-permute-start | bytes 811016 | tf_op jit(solution)/shard_map/ppermute | solution.py:565
  23.9 1.3 %collective-permute-done.3.refs_2_ = bf16[1056,128]{1,0:T(8,128)(2,1)S(1)} collective-permute-done((bf16[1056,128]{1,0:T(8,128)(2,1)S(1)}, bf16[1056,128]{1,0:T(8,128)(2,1)S(1)}, u32[]{:S(2)}, u32[]{:S(2)}) %collective-permute-start.3) | collective-permute-done | bytes 270368 | tf_op jit(solution)/shard_map/ppermute | solution.py:565
  25.1 1.8 %combine.5 = bf16[1024,128]{1,0:T(8,128)(2,1)S(1)} custom-call(bf16[2,2,32,8192]{3,2,1,0:T(8,128)(2,1)S(1)} %copy-done, bf16[2,2,32,8192]{3,2,1,0:T(8,128)(2,1)S(1)} %collective-permute-done.near.refs_1_, bf16[1056,128]{1,0:T(8,128)(2,1)S(1)} %collective-permute-done.3.refs_2_, bf16[32,128]{1,0:T(8,128)(2,1)S(1)} %collective-permute-done.4.refs_3_, ...), custom_call_target="tpu_custom_call" | custom-call | flops 2000000000 | bytes 7200001 | tf_op jit(solution)/shard_map/combine/pallas_call | solution.py:634
  27.0 4.6 %collective-permute-start.6 = (bf16[1024,128]{1,0:T(8,128)(2,1)S(1)}, bf16[1024,128]{1,0:T(8,128)(2,1)S(1)}, u32[]{:S(2)}, u32[]{:S(2)}) collective-permute-start(bf16[1024,128]{1,0:T(8,128)(2,1)S(1)} %combine.5), channel_id=1, source_target_pairs={{0,24},{2,26},{4,28},{6,30},{8,0},{10,2},{12,4},{14,6},{16,8},{18,... | collective-permute-start | bytes 786440 | tf_op jit(solution)/shard_map/ppermute | solution.py:569
  31.6 0.0 collective-permute-done.9.refs_2_
  31.6 0.0 collective-permute-start.8
  31.6 0.0 collective-permute-done.10.refs_2_
  31.6 1.8 %combine.7.refs_0_ = f32[1024,128]{1,0:T(8,128)S(1)} custom-call(bf16[2,2,32,8192]{3,2,1,0:T(8,128)(2,1)S(1)} %copy-done, bf16[2,2,32,8192]{3,2,1,0:T(8,128)(2,1)S(1)} %collective-permute-done.near.refs_1_, bf16[1056,128]{1,0:T(8,128)(2,1)S(1)} %collective-permute-done.10.refs_2_, bf16[32,128]{1,0:T(8,128)(2,1)S(1)} %collective-permute-done.4.refs_3_, ...), custom_call_target="tpu_custom_call" | custom-call | flops 1000000000 | bytes 3600001 | tf_op jit(solution)/shard_map/combine/pallas_call | solution.py:634
  33.5 0.0 collective-permute-done.11.refs_1_
  33.5 2.2 %finish_ahead.1 = (f32[4,2,512,128]{3,2,1,0:T(8,128)}, f32[2,512,128]{2,1,0:T(8,128)S(1)}, f32[2,512,128]{2,1,0:T(8,128)S(1)}) custom-call(s32[32]{0:T(128)S(1)} %copy-done.3, f32[1024,128]{1,0:T(8,128)S(1)} %combine.7.refs_0_, bf16[1024,128]{1,0:T(8,128)(2,1)S(1)} %collective-permute-done.11.refs_1_, bf16[768,128]{1,0:T(8,128)(2,1)S(1)} %collective-permute-done.9.refs_2_, ...), custom_call_target="tpu_custom_call" | custom-call | bytes 1 | tf_op jit(solution)/shard_map/finish_ahead/pallas_call | solution.py:691
  35.7 3.3 %collective-permute-done.8.refs_1_ = bf16[256,128]{1,0:T(8,128)(2,1)S(1)} collective-permute-done((bf16[256,128]{1,0:T(8,128)(2,1)S(1)}, bf16[256,128]{1,0:T(8,128)(2,1)S(1)}, u32[]{:S(2)}, u32[]{:S(2)}) %collective-permute-start.8) | collective-permute-done | bytes 65568 | tf_op jit(solution)/shard_map/ppermute | solution.py:569
  39.0 0.0 collective-permute-done.6.refs_0_
  39.0 1.8 %finish_last.1 = (f32[4,2,512,128]{3,2,1,0:T(8,128)}, f32[2,512,128]{2,1,0:T(8,128)}) custom-call(s32[32]{0:T(128)S(1)} %copy-done.3, bf16[1024,128]{1,0:T(8,128)(2,1)S(1)} %collective-permute-done.6.refs_0_, bf16[256,128]{1,0:T(8,128)(2,1)S(1)} %collective-permute-done.8.refs_1_, ...), custom_call_target="tpu_custom_call", output_to_operand_aliasing={{0}: (7, {})} | custom-call | flops 30000001024 | bytes 108000000 | tf_op jit(solution)/shard_map/finish_last/pallas_call | solution.py:702
Async XLA Ops:
  0.6 5.6 %collective-permute-start = (bf16[2,2,32,8192]{3,2,1,0:T(8,128)(2,1)}, bf16[2,2,32,8192]{3,2,1,0:T(8,128)(2,1)S(1)}, u32[]{:S(2)}, u32[]{:S(2)}) collective-permute-start(bf16[2,2,32,8192]{3,2,1,0:T(8,128)(2,1)} %refs_0_.6), channel_id=1, source_target_pairs={{0,2},{2,0},{4,6},{6,4},{8,10},{10,8},{12,14},{14,12},{16,18},{18,... | collective-permute-start | bytes 6291464 | tf_op jit(solution)/shard_map/ppermute | solution.py:565
  1.1 4.0 %copy-start.3 = (s32[32]{0:T(128)S(1)}, s32[32]{0:T(128)}, u32[]{:S(2)}) copy-start(s32[32]{0:T(128)} %parent_of.5) | copy-start | bytes 388
  1.2 4.0 %copy-start.4 = (s32[65536]{0:T(1024)S(1)}, s32[65536]{0:T(1024)}, u32[]{:S(2)}) copy-start(s32[65536]{0:T(1024)} %param.17) | copy-start | bytes 786436
  1.2 4.0 %copy-start.5 = (f32[4,3]{1,0:T(4,128)S(1)}, f32[4,3]{1,0:T(4,128)}, u32[]{:S(2)}) copy-start(f32[4,3]{1,0:T(4,128)} %center.1) | copy-start | bytes 148
  1.2 4.0 %copy-start.6 = (s32[32]{0:T(128)S(1)}, s32[32]{0:T(128)}, u32[]{:S(2)}) copy-start(s32[32]{0:T(128)} %octant_of.1) | copy-start | bytes 388
  2.2 8.6 %collective-permute-start.2 = (bf16[2,2,32,512]{3,2,1,0:T(8,128)(2,1)S(1)}, bf16[2,2,32,512]{3,2,1,0:T(8,128)(2,1)S(1)}, u32[]{:S(2)}, u32[]{:S(2)}) collective-permute-start(bf16[2,2,32,512]{3,2,1,0:T(8,128)(2,1)S(1)} %get-tuple-element.56), channel_id=1, source_target_pairs={{0,6},{2,4},{4,2},{6,0},{8,14},{10,12},{12,10},{14,8},{16,22},{18,... | collective-permute-start | bytes 393224 | tf_op jit(solution)/shard_map/ppermute | solution.py:565
  4.9 7.0 %collective-permute-start.1 = (bf16[2,2,32,512]{3,2,1,0:T(8,128)(2,1)S(1)}, bf16[2,2,32,512]{3,2,1,0:T(8,128)(2,1)S(1)}, u32[]{:S(2)}, u32[]{:S(2)}) collective-permute-start(bf16[2,2,32,512]{3,2,1,0:T(8,128)(2,1)S(1)} %get-tuple-element.57), channel_id=1, source_target_pairs={{0,4},{2,6},{4,0},{6,2},{8,12},{10,14},{12,8},{14,10},{16,20},{18,... | collective-permute-start | bytes 393224 | tf_op jit(solution)/shard_map/ppermute | solution.py:565
  5.1 1.6 %copy-start = (bf16[2,2,32,8192]{3,2,1,0:T(8,128)(2,1)S(1)}, bf16[2,2,32,8192]{3,2,1,0:T(8,128)(2,1)}, u32[]{:S(2)}) copy-start(bf16[2,2,32,8192]{3,2,1,0:T(8,128)(2,1)} %refs_0_.6) | copy-start | bytes 6291460
  6.2 5.8 %copy-start.1 = (bf16[256,256]{1,0:T(8,128)(2,1)S(1)}, bf16[256,256]{1,0:T(8,128)(2,1)}, u32[]{:S(2)}) copy-start(bf16[256,256]{1,0:T(8,128)(2,1)} %constant.21.clone.refs_8_.refs_9_.refs_11_) | copy-start | bytes 393220
  6.2 5.8 %copy-start.2 = (bf16[256,256]{1,0:T(8,128)(2,1)S(1)}, bf16[256,256]{1,0:T(8,128)(2,1)}, u32[]{:S(2)}) copy-start(bf16[256,256]{1,0:T(8,128)(2,1)} %constant.20.clone.refs_7_.refs_8_.refs_10_) | copy-start | bytes 393220
  7.2 10.5 %collective-permute-start.5 = (bf16[32,128]{1,0:T(8,128)(2,1)S(1)}, bf16[32,128]{1,0:T(8,128)(2,1)S(1)}, u32[]{:S(2)}, u32[]{:S(2)}) collective-permute-start(bf16[32,128]{1,0:T(8,128)(2,1)S(1)} %get-tuple-element.36), channel_id=1, source_target_pairs={{0,5},{1,4},{2,7},{3,6},{4,1},{5,0},{6,3},{7,2},{8,13},{9,12},{10,... | collective-permute-start | bytes 24584 | tf_op jit(solution)/shard_map/ppermute | solution.py:585
  10.2 7.6 %collective-permute-start.4 = (bf16[32,128]{1,0:T(8,128)(2,1)S(1)}, bf16[32,128]{1,0:T(8,128)(2,1)S(1)}, u32[]{:S(2)}, u32[]{:S(2)}) collective-permute-start(bf16[32,128]{1,0:T(8,128)(2,1)S(1)} %get-tuple-element.36), channel_id=1, source_target_pairs={{0,1},{1,0},{2,3},{3,2},{4,5},{5,4},{6,7},{7,6},{8,9},{9,8},{10,11... | collective-permute-start | bytes 24584 | tf_op jit(solution)/shard_map/ppermute | solution.py:585
  10.7 8.6 %collective-permute-start.7 = (bf16[1088,128]{1,0:T(8,128)(2,1)S(1)}, bf16[1088,128]{1,0:T(8,128)(2,1)S(1)}, u32[]{:S(2)}, u32[]{:S(2)}) collective-permute-start(bf16[1088,128]{1,0:T(8,128)(2,1)S(1)} %get-tuple-element.38), channel_id=1, source_target_pairs={{0,4},{2,6},{4,0},{6,2},{8,12},{10,14},{12,8},{14,10},{16,20},{18,... | collective-permute-start | bytes 835592 | tf_op jit(solution)/shard_map/ppermute | solution.py:565
  13.0 18.6 %collective-permute-start.9 = (bf16[768,128]{1,0:T(8,128)(2,1)S(1)}, bf16[768,128]{1,0:T(8,128)(2,1)S(1)}, u32[]{:S(2)}, u32[]{:S(2)}) collective-permute-start(bf16[768,128]{1,0:T(8,128)(2,1)S(1)} %combine.4), channel_id=1, source_target_pairs={{0,16},{2,18},{4,20},{6,22},{8,24},{10,26},{12,28},{14,30},{16,0},... | collective-permute-start | bytes 589832 | tf_op jit(solution)/shard_map/ppermute | solution.py:569
  15.7 9.4 %collective-permute-start.3 = (bf16[1056,128]{1,0:T(8,128)(2,1)S(1)}, bf16[1056,128]{1,0:T(8,128)(2,1)S(1)}, u32[]{:S(2)}, u32[]{:S(2)}) collective-permute-start(bf16[1056,128]{1,0:T(8,128)(2,1)S(1)} %get-tuple-element.35), channel_id=1, source_target_pairs={{0,4},{2,6},{4,0},{6,2},{8,12},{10,14},{12,8},{14,10},{16,20},{18,... | collective-permute-start | bytes 811016 | tf_op jit(solution)/shard_map/ppermute | solution.py:565
  21.6 11.9 %collective-permute-start.11 = (bf16[1024,128]{1,0:T(8,128)(2,1)S(1)}, bf16[1024,128]{1,0:T(8,128)(2,1)S(1)}, u32[]{:S(2)}, u32[]{:S(2)}) collective-permute-start(bf16[1024,128]{1,0:T(8,128)(2,1)S(1)} %get-tuple-element.45), channel_id=1, source_target_pairs={{0,8},{2,10},{4,12},{6,14},{8,16},{10,18},{12,20},{14,22},{16,24},... | collective-permute-start | bytes 786440 | tf_op jit(solution)/shard_map/ppermute | solution.py:569
  23.2 8.4 %collective-permute-start.10 = (bf16[1056,128]{1,0:T(8,128)(2,1)S(1)}, bf16[1056,128]{1,0:T(8,128)(2,1)S(1)}, u32[]{:S(2)}, u32[]{:S(2)}) collective-permute-start(bf16[1056,128]{1,0:T(8,128)(2,1)S(1)} %get-tuple-element.44), channel_id=1, source_target_pairs={{0,4},{2,6},{4,0},{6,2},{8,12},{10,14},{12,8},{14,10},{16,20},{18,... | collective-permute-start | bytes 811016 | tf_op jit(solution)/shard_map/ppermute | solution.py:565
  27.0 12.0 %collective-permute-start.6 = (bf16[1024,128]{1,0:T(8,128)(2,1)S(1)}, bf16[1024,128]{1,0:T(8,128)(2,1)S(1)}, u32[]{:S(2)}, u32[]{:S(2)}) collective-permute-start(bf16[1024,128]{1,0:T(8,128)(2,1)S(1)} %combine.5), channel_id=1, source_target_pairs={{0,24},{2,26},{4,28},{6,30},{8,0},{10,2},{12,4},{14,6},{16,8},{18,... | collective-permute-start | bytes 786440 | tf_op jit(solution)/shard_map/ppermute | solution.py:569
  31.6 7.3 %collective-permute-start.8 = (bf16[256,128]{1,0:T(8,128)(2,1)S(1)}, bf16[256,128]{1,0:T(8,128)(2,1)S(1)}, u32[]{:S(2)}, u32[]{:S(2)}) collective-permute-start(bf16[256,128]{1,0:T(8,128)(2,1)S(1)} %get-tuple-element.41), channel_id=1, source_target_pairs={{0,16},{2,18},{4,20},{6,22},{8,24},{10,26},{12,28},{14,30},{16,0},... | collective-permute-start | bytes 196616 | tf_op jit(solution)/shard_map/ppermute | solution.py:569

commit v6 on v5

--- a/solution.py
+++ b/solution.py
@@ -491,9 +491,45 @@
     )
 
 
-def finish_kernel(steps, early_step, columns, members, boxes, sources, rows, parts, parent_of, *refs):
+def join_kernel(steps, early_step, columns, members, boxes, sources, rows, parent_of, *refs):
     whole, refs = refs[: len(steps)], refs[len(steps) :]
-    late, early, center_cos, center_sin, far_in, _, parent_out, far_out, names, held, far_held, name_sem, sems = refs
+    late, early, center_cos, center_sin, far_in, _, parent_out, far_out, names, patterns, name_sem, sems = refs
+    name_copy = pltpu.make_async_copy(parent_of, names, name_sem)
+    name_copy.start()
+    last = len(steps)
+    patterns[last] = early[...]
+    for source in range(sources):
+        at = pl.ds(source * rows, rows)
+        far_real, far_imag = far_in[0, at, :], far_in[1, at, :]
+        for index, step in enumerate(steps):
+            real, imag = (
+                whole[index][pl.ds((half * sources + source) * rows, rows), :].astype(jnp.float32) for half in range(2)
+            )
+            cosine, sine = center_cos[step], center_sin[step]
+            patterns[index, 0, at, :] = real
+            patterns[index, 1, at, :] = imag
+            far_real = far_real + (cosine * real - sine * imag)
+            far_imag = far_imag + (sine * real + cosine * imag)
+        far_out[0, at, :] = far_real
+        far_out[1, at, :] = far_imag
+    place_columns(
+        late, columns, sources, rows, center_cos.at[early_step], center_sin.at[early_step], patterns.at[last], far_out
+    )
+    name_copy.wait()
+    groups = lax.axis_size("wide") // members
+    group_at = lax.axis_index("wide") // members
+    copies = []
+    for index, step in enumerate((*steps, early_step)):
+        name = names[group_before(group_at, step, groups) * members * boxes]
+        copies.append(pltpu.make_async_copy(patterns.at[index], parent_out.at[name], sems.at[index]))
+        copies[-1].start()
+    for copy in copies:
+        copy.wait()
+
+
+def finish_kernel(steps, members, boxes, sources, rows, parts, parent_of, *refs):
+    whole, refs = refs[: len(steps)], refs[len(steps) :]
+    center_cos, center_sin, far_in, _, parent_out, far_out, names, held, far_held, name_sem, sems = refs
     name_copy = pltpu.make_async_copy(parent_of, names, name_sem)
     name_copy.start()
     group_at = lax.axis_index("wide") // members
@@ -504,20 +540,14 @@
         copies[-1].start()
 
     last = len(steps)
-    held[last] = early[...]
-    far_held[...] = far_in[...]
-    place_columns(
-        late, columns, sources, rows, center_cos.at[early_step], center_sin.at[early_step], held.at[last], far_held
-    )
     name_copy.wait()
     groups = lax.axis_size("wide") // members
-    places = [names[group_before(group_at, step, groups) * members * boxes] for step in (*steps, early_step)]
-    send(held.at[last], parent_out.at[places[last]])
+    places = [names[group_before(group_at, step, groups) * members * boxes] for step in steps]
     each = sources // parts
     for part in range(parts):
         for source in range(part * each, (part + 1) * each):
             at = pl.ds(source * rows, rows)
-            far_real, far_imag = far_held[0, at, :], far_held[1, at, :]
+            far_real, far_imag = far_in[0, at, :], far_in[1, at, :]
             for index, step in enumerate(steps):
                 real, imag = (
                     whole[index][pl.ds((half * sources + source) * rows, rows), :].astype(jnp.float32) for half in range(2)
@@ -682,12 +712,12 @@
             jobs.append((top, outer, outer_places, list(zip(rims, edge_at))))
             data = data + heads
     data[0], done[0] = tie(data[0], done[0])
-    (arrived[0],) = sums_of(jobs, data, jnp.float32, 1)
+    (arrived[0],) = sums_of(jobs, data, jnp.float32, 0)
     done = [(top, columns_of(inner), done[0]), (top, columns_of(outer), done[1])]
     held = arrived
     whole = f32(2, sources * out_rows, LANES)
     (_, early_columns, early_array), (_, late_columns, late_array) = done
-    ahead = [0, *range(2, top)]
+    ahead = [0]
     parent_pattern, far_field, early_pattern = pl.pallas_call(
         functools.partial(finish_ahead_kernel, ahead, top, early_columns, members, boxes, sources, out_rows),
         out_shape=[f32(parents, *whole.shape), whole, whole],
@@ -697,25 +727,45 @@
         cost_estimate=cost(0),
         name="finish_ahead",
     )(child_parent, *[held[step] for step in ahead], early_array, center_cos, center_sin)
+    between = list(range(2, top))
+    parent_pattern, far_field = pl.pallas_call(
+        functools.partial(join_kernel, between, top, late_columns, members, boxes, sources, out_rows),
+        out_shape=[f32(parents, *whole.shape), whole],
+        in_specs=[hbm] + [vmem] * (len(between) + 5) + [hbm],
+        out_specs=[hbm, vmem],
+        input_output_aliases={len(between) + 6: 0},
+        scratch_shapes=[
+            pltpu.SMEM(child_parent.shape, jnp.int32),
+            pltpu.VMEM((len(between) + 1, *whole.shape), jnp.float32),
+            pltpu.SemaphoreType.DMA,
+            pltpu.SemaphoreType.DMA((len(between) + 1,)),
+        ],
+        compiler_params=limit,
+        cost_estimate=cost(5),
+        name="join",
+    )(
+        child_parent, *[held[step] for step in between], late_array, early_pattern, center_cos, center_sin, far_field,
+        parent_pattern,
+    )
     steps = [1]
     parts = 4
     parent_pattern, far_field = pl.pallas_call(
-        functools.partial(finish_kernel, steps, top, late_columns, members, boxes, sources, out_rows, parts),
+        functools.partial(finish_kernel, steps, members, boxes, sources, out_rows, parts),
         out_shape=[f32(parents, *whole.shape), whole],
-        in_specs=[hbm] + [vmem] * (len(steps) + 5) + [hbm],
+        in_specs=[hbm] + [vmem] * (len(steps) + 3) + [hbm],
         out_specs=[hbm, hbm],
-        input_output_aliases={len(steps) + 6: 0},
+        input_output_aliases={len(steps) + 4: 0},
         scratch_shapes=[
             pltpu.SMEM(child_parent.shape, jnp.int32),
-            pltpu.VMEM((len(steps) + 1, *whole.shape), jnp.float32),
+            pltpu.VMEM((len(steps), *whole.shape), jnp.float32),
             pltpu.VMEM(whole.shape, jnp.float32),
             pltpu.SemaphoreType.DMA,
-            pltpu.SemaphoreType.DMA((1 + parts * (len(steps) + 1),)),
+            pltpu.SemaphoreType.DMA((parts * (len(steps) + 1),)),
         ],
         compiler_params=limit,
         cost_estimate=cost(30),
         name="finish_last",
-    )(child_parent, *[held[step] for step in steps], late_array, early_pattern, center_cos, center_sin, far_field, parent_pattern)
+    )(child_parent, *[held[step] for step in steps], center_cos, center_sin, far_field, parent_pattern)
     return (
         parent_pattern.reshape(parents, 2, sources, 1, 4 * piece),
         far_field.reshape(2, sources, 1, 4 * piece),

time: 40.9 us -> 40.4 us (0.988)
  waiting for transfers between devices: 7.31 us -> 5.35 us
  Pallas kernels: 12.6 us -> 13.7 us
    pallas_call x1 -> x2, Pallas kernels: 1.76 us -> 3.13 us  [the longest x1 1.58 us: grouped(): pl.pallas_call(functools.partial(finish_kernel, steps, members, boxes, so...]
    ppermute x6, waiting for transfers between devices: 4.03 us -> 2.75 us  [swap_with(): return lax.ppermute(array, 'wide', [(i, i ^ step) for i in range(n_wide)])]
    ppermute x4, waiting for transfers between devices: 3.27 us -> 2.59 us  [move_by(): lax.ppermute(array, 'wide', [(i, (i + shift) % n_wide) for i in range(n_w...]
  transfers between devices with their start and end apart: 12 -> 12, of which waited for: 4 -> 4; matrix products, arithmetic and copies ran while one was open for 3% -> 3% of each run, Pallas kernels for 27% -> 30%
where the time goes in v6:
time: 40.4 us; the launch traced here: 40.2 us
  starting transfers between devices  18.8 us (47%)
  Pallas kernels  13.7 us (34%)
  waiting for transfers between devices  5.35 us (13%)
  local copies, waits for them, and re-layouts  1.6 us (4%)
  between operations  0.76 us (2%)
    ppermute x4, starting transfers between devices, move_by(): lax.ppermute(array, 'wide', [(i, (i + shift) % n_wide) for i in range(n_w...  9.28 us
    pallas_call x4, Pallas kernels, sums_of(): pl.pallas_call(functools.partial(combine_kernel, jobs, members, boxes, so...  6.92 us
    ppermute x6, starting transfers between devices, swap_with(): return lax.ppermute(array, 'wide', [(i, i ^ step) for i in range(n_wide)])  6.07 us
    ppermute x2, starting transfers between devices, other_half(): return lax.ppermute(array, ('wide', 'narrow'), pairs)  3.48 us
    ppermute x6, waiting for transfers between devices, swap_with(): return lax.ppermute(array, 'wide', [(i, i ^ step) for i in range(n_wide)])  2.75 us
    ppermute x4, waiting for transfers between devices, move_by(): lax.ppermute(array, 'wide', [(i, (i + shift) % n_wide) for i in range(n_w...  2.59 us
    pallas_call x1, Pallas kernels, grouped(): pl.pallas_call(functools.partial(finish_ahead_kernel, ahead, top, early_c...  1.95 us
    pallas_call x1, Pallas kernels, grouped(): pl.pallas_call(functools.partial(finish_kernel, steps, members, boxes, so...  1.58 us
  transfers between devices with their start and end apart: 12, of which 4 were waited for; matrix products, arithmetic and copies ran while one was open for 3% of the time, Pallas kernels for 30%

profile of v6, /device:TPU:0, one launch (start us, length us, event | category | flops | bytes accessed | tf_op | source)
XLA Modules:
  0.0 40.2 jit_solution(5996707060582988289)
XLA Ops:
  0.6 0.5 %collective-permute-start = (bf16[2,2,32,8192]{3,2,1,0:T(8,128)(2,1)}, bf16[2,2,32,8192]{3,2,1,0:T(8,128)(2,1)S(1)}, u32[]{:S(2)}, u32[]{:S(2)}) collective-permute-start(bf16[2,2,32,8192]{3,2,1,0:T(8,128)(2,1)} %refs_0_.6), channel_id=1, source_target_pairs={{0,2},{2,0},{4,6},{6,4},{8,10},{10,8},{12,14},{14,12},{16,18},{18,... | collective-permute-start | bytes 6291464 | tf_op jit(solution)/shard_map/ppermute | solution.py:595
  1.1 0.0 copy-start.3
  1.2 0.0 copy-start.4
  1.2 0.0 copy-start.5
  1.2 1.0 %constant_dynamic-slice_fusion = (bf16[2,2,32,512]{3,2,1,0:T(8,128)(2,1)S(1)}, bf16[2,2,32,512]{3,2,1,0:T(8,128)(2,1)S(1)}) fusion(bf16[2,2,32,8192]{3,2,1,0:T(8,128)(2,1)} %refs_0_.6, s32[]{:T(128)S(6)} %select_n.7, s32[]{:T(128)S(6)} %select_n.6), kind=kLoop, calls=%fused_computation | loop fusion | bytes 524296 | tf_op jit(solution)/shard_map/dynamic_slice | solution.py:609
  2.2 2.7 %collective-permute-start.2 = (bf16[2,2,32,512]{3,2,1,0:T(8,128)(2,1)S(1)}, bf16[2,2,32,512]{3,2,1,0:T(8,128)(2,1)S(1)}, u32[]{:S(2)}, u32[]{:S(2)}) collective-permute-start(bf16[2,2,32,512]{3,2,1,0:T(8,128)(2,1)S(1)} %get-tuple-element.60), channel_id=1, source_target_pairs={{0,6},{2,4},{4,2},{6,0},{8,14},{10,12},{12,10},{14,8},{16,22},{18,... | collective-permute-start | bytes 393224 | tf_op jit(solution)/shard_map/ppermute | solution.py:595
  4.9 0.0 collective-permute-start.1
  4.9 0.2 axes.1
  5.1 0.0 copy-start
  5.1 0.0 copy-done.3
  5.2 0.0 copy-done.4
  5.2 0.0 copy-done.5
  5.2 0.0 copy-done.6
  5.2 1.0 %prep.1 = (f32[4,8,16,128]{3,2,1,0:T(8,128)S(1)}, f32[4,8,16,128]{3,2,1,0:T(8,128)S(1)}, f32[4,16,128]{2,1,0:T(8,128)S(1)}, f32[4,16,128]{2,1,0:T(8,128)S(1)}, f32[4,16,128]{2,1,0:T(8,128)S(1)}) custom-call(s32[32]{0:T(128)S(1)} %copy-done.3, s32[32]{0:T(128)S(1)} %copy-done.6, f32[4,3]{1,0:T(4,128)S(1)} %copy-done.5, s32[512,128]{1,0:T(8,128)S(1)} %bitcast.3, ...), custom_call_target="tpu_custom_call" | custom-call | flops 1000000000 | bytes 3600001 | tf_op jit(solution)/shard_map/prep/pallas_call | solution.py:625
  6.2 0.0 copy-start.1
  6.2 0.0 copy-start.2
  6.2 0.0 collective-permute-done.near.refs_1_
  6.2 0.5 %copy-done = bf16[2,2,32,8192]{3,2,1,0:T(8,128)(2,1)S(1)} copy-done((bf16[2,2,32,8192]{3,2,1,0:T(8,128)(2,1)S(1)}, bf16[2,2,32,8192]{3,2,1,0:T(8,128)(2,1)}, u32[]{:S(2)}) %copy-start) | copy-done | bytes 2097176
  6.7 0.5 %pack.1 = (bf16[1088,128]{1,0:T(8,128)(2,1)S(1)}, bf16[1056,128]{1,0:T(8,128)(2,1)S(1)}, bf16[1056,128]{1,0:T(8,128)(2,1)S(1)}, bf16[32,128]{1,0:T(8,128)(2,1)S(1)}) custom-call(bf16[2,2,32,8192]{3,2,1,0:T(8,128)(2,1)S(1)} %copy-done, bf16[2,2,32,8192]{3,2,1,0:T(8,128)(2,1)S(1)} %collective-permute-done.near.refs_1_), custom_call_target="tpu_custom_call" | custom-call | flops 1000000000 | bytes 3600001 | tf_op jit(solution)/shard_map/pack/pallas_call | solution.py:644
  7.2 2.9 %collective-permute-start.5 = (bf16[32,128]{1,0:T(8,128)(2,1)S(1)}, bf16[32,128]{1,0:T(8,128)(2,1)S(1)}, u32[]{:S(2)}, u32[]{:S(2)}) collective-permute-start(bf16[32,128]{1,0:T(8,128)(2,1)S(1)} %get-tuple-element.38), channel_id=1, source_target_pairs={{0,5},{1,4},{2,7},{3,6},{4,1},{5,0},{6,3},{7,2},{8,13},{9,12},{10,... | collective-permute-start | bytes 24584 | tf_op jit(solution)/shard_map/ppermute | solution.py:615
  10.2 0.5 %collective-permute-start.4 = (bf16[32,128]{1,0:T(8,128)(2,1)S(1)}, bf16[32,128]{1,0:T(8,128)(2,1)S(1)}, u32[]{:S(2)}, u32[]{:S(2)}) collective-permute-start(bf16[32,128]{1,0:T(8,128)(2,1)S(1)} %get-tuple-element.38), channel_id=1, source_target_pairs={{0,1},{1,0},{2,3},{3,2},{4,5},{5,4},{6,7},{7,6},{8,9},{9,8},{10,11... | collective-permute-start | bytes 24584 | tf_op jit(solution)/shard_map/ppermute | solution.py:615
  10.7 0.1 collective-permute-start.7
  10.8 0.0 collective-permute-done.2.refs_3_.refs_6_
  10.8 1.2 %collective-permute-done.1.refs_2_.refs_5_ = bf16[2,2,32,512]{3,2,1,0:T(8,128)(2,1)S(1)} collective-permute-done((bf16[2,2,32,512]{3,2,1,0:T(8,128)(2,1)S(1)}, bf16[2,2,32,512]{3,2,1,0:T(8,128)(2,1)S(1)}, u32[]{:S(2)}, u32[]{:S(2)}) %collective-permute-start.1) | collective-permute-done | bytes 131104 | tf_op jit(solution)/shard_map/ppermute | solution.py:595
  11.9 0.0 copy-done.1
  11.9 0.0 copy-done.2
  11.9 1.0 %combine.4 = bf16[768,128]{1,0:T(8,128)(2,1)S(1)} custom-call(bf16[2,2,32,8192]{3,2,1,0:T(8,128)(2,1)S(1)} %copy-done, bf16[2,2,32,8192]{3,2,1,0:T(8,128)(2,1)S(1)} %collective-permute-done.near.refs_1_, bf16[2,2,32,512]{3,2,1,0:T(8,128)(2,1)S(1)} %collective-permute-done.1.refs_2_.refs_5_, ...), custom_call_target="tpu_custom_call" | custom-call | flops 5000000000 | bytes 18000000 | tf_op jit(solution)/shard_map/combine/pallas_call | solution.py:664
  13.0 2.7 %collective-permute-start.10 = (bf16[768,128]{1,0:T(8,128)(2,1)S(1)}, bf16[768,128]{1,0:T(8,128)(2,1)S(1)}, u32[]{:S(2)}, u32[]{:S(2)}) collective-permute-start(bf16[768,128]{1,0:T(8,128)(2,1)S(1)} %combine.4), channel_id=1, source_target_pairs={{0,16},{2,18},{4,20},{6,22},{8,24},{10,26},{12,28},{14,30},{16,0},... | collective-permute-start | bytes 589832 | tf_op jit(solution)/shard_map/ppermute | solution.py:599
  15.7 2.0 %collective-permute-start.3 = (bf16[1056,128]{1,0:T(8,128)(2,1)S(1)}, bf16[1056,128]{1,0:T(8,128)(2,1)S(1)}, u32[]{:S(2)}, u32[]{:S(2)}) collective-permute-start(bf16[1056,128]{1,0:T(8,128)(2,1)S(1)} %get-tuple-element.37), channel_id=1, source_target_pairs={{0,4},{2,6},{4,0},{6,2},{8,12},{10,14},{12,8},{14,10},{16,20},{18,... | collective-permute-start | bytes 811016 | tf_op jit(solution)/shard_map/ppermute | solution.py:595
  17.8 0.0 collective-permute-done.5.refs_4_
  17.8 0.0 collective-permute-done.4.refs_3_
  17.8 1.6 %collective-permute-done.7.refs_2_ = bf16[1088,128]{1,0:T(8,128)(2,1)S(1)} collective-permute-done((bf16[1088,128]{1,0:T(8,128)(2,1)S(1)}, bf16[1088,128]{1,0:T(8,128)(2,1)S(1)}, u32[]{:S(2)}, u32[]{:S(2)}) %collective-permute-start.7) | collective-permute-done | bytes 278560 | tf_op jit(solution)/shard_map/ppermute | solution.py:595
  19.4 2.2 %combine.6 = (bf16[1024,128]{1,0:T(8,128)(2,1)S(1)}, bf16[256,128]{1,0:T(8,128)(2,1)S(1)}) custom-call(bf16[2,2,32,8192]{3,2,1,0:T(8,128)(2,1)S(1)} %copy-done, bf16[2,2,32,8192]{3,2,1,0:T(8,128)(2,1)S(1)} %collective-permute-done.near.refs_1_, bf16[1088,128]{1,0:T(8,128)(2,1)S(1)} %collective-permute-done.7.refs_2_, ...), custom_call_target="tpu_custom_call" | custom-call | flops 30000001024 | bytes 108000000 | tf_op jit(solution)/shard_map/combine/pallas_call | solution.py:664
  21.6 0.7 %collective-permute-start.11 = (bf16[1056,128]{1,0:T(8,128)(2,1)S(1)}, bf16[1056,128]{1,0:T(8,128)(2,1)S(1)}, u32[]{:S(2)}, u32[]{:S(2)}) collective-permute-start(bf16[1056,128]{1,0:T(8,128)(2,1)S(1)} %get-tuple-element.49), channel_id=1, source_target_pairs={{0,4},{2,6},{4,0},{6,2},{8,12},{10,14},{12,8},{14,10},{16,20},{18,... | collective-permute-start | bytes 811016 | tf_op jit(solution)/shard_map/ppermute | solution.py:595
  22.3 1.6 %collective-permute-start.8 = (bf16[1024,128]{1,0:T(8,128)(2,1)S(1)}, bf16[1024,128]{1,0:T(8,128)(2,1)S(1)}, u32[]{:S(2)}, u32[]{:S(2)}) collective-permute-start(bf16[1024,128]{1,0:T(8,128)(2,1)S(1)} %get-tuple-element.45), channel_id=1, source_target_pairs={{0,8},{2,10},{4,12},{6,14},{8,16},{10,18},{12,20},{14,22},{16,24},... | collective-permute-start | bytes 786440 | tf_op jit(solution)/shard_map/ppermute | solution.py:599
  23.9 0.9 %collective-permute-done.10.refs_1_ = bf16[768,128]{1,0:T(8,128)(2,1)S(1)} collective-permute-done((bf16[768,128]{1,0:T(8,128)(2,1)S(1)}, bf16[768,128]{1,0:T(8,128)(2,1)S(1)}, u32[]{:S(2)}, u32[]{:S(2)}) %collective-permute-start.10) | collective-permute-done | bytes 196640 | tf_op jit(solution)/shard_map/ppermute | solution.py:599
  24.8 2.5 %collective-permute-start.9 = (bf16[256,128]{1,0:T(8,128)(2,1)S(1)}, bf16[256,128]{1,0:T(8,128)(2,1)S(1)}, u32[]{:S(2)}, u32[]{:S(2)}) collective-permute-start(bf16[256,128]{1,0:T(8,128)(2,1)S(1)} %get-tuple-element.46), channel_id=1, source_target_pairs={{0,16},{2,18},{4,20},{6,22},{8,24},{10,26},{12,28},{14,30},{16,0},... | collective-permute-start | bytes 196616 | tf_op jit(solution)/shard_map/ppermute | solution.py:599
  27.3 0.0 collective-permute-done.3.refs_2_
  27.3 1.8 %combine.5 = bf16[1024,128]{1,0:T(8,128)(2,1)S(1)} custom-call(bf16[2,2,32,8192]{3,2,1,0:T(8,128)(2,1)S(1)} %copy-done, bf16[2,2,32,8192]{3,2,1,0:T(8,128)(2,1)S(1)} %collective-permute-done.near.refs_1_, bf16[1056,128]{1,0:T(8,128)(2,1)S(1)} %collective-permute-done.3.refs_2_, bf16[32,128]{1,0:T(8,128)(2,1)S(1)} %collective-permute-done.4.refs_3_, ...), custom_call_target="tpu_custom_call" | custom-call | flops 2000000000 | bytes 7200001 | tf_op jit(solution)/shard_map/combine/pallas_call | solution.py:664
  29.1 2.5 %collective-permute-start.6 = (bf16[1024,128]{1,0:T(8,128)(2,1)S(1)}, bf16[1024,128]{1,0:T(8,128)(2,1)S(1)}, u32[]{:S(2)}, u32[]{:S(2)}) collective-permute-start(bf16[1024,128]{1,0:T(8,128)(2,1)S(1)} %combine.5), channel_id=1, source_target_pairs={{0,24},{2,26},{4,28},{6,30},{8,0},{10,2},{12,4},{14,6},{16,8},{18,... | collective-permute-start | bytes 786440 | tf_op jit(solution)/shard_map/ppermute | solution.py:599
  31.6 0.0 collective-permute-done.11.refs_2_
  31.6 1.8 %combine.7.refs_0_ = f32[1024,128]{1,0:T(8,128)S(1)} custom-call(bf16[2,2,32,8192]{3,2,1,0:T(8,128)(2,1)S(1)} %copy-done, bf16[2,2,32,8192]{3,2,1,0:T(8,128)(2,1)S(1)} %collective-permute-done.near.refs_1_, bf16[1056,128]{1,0:T(8,128)(2,1)S(1)} %collective-permute-done.11.refs_2_, bf16[32,128]{1,0:T(8,128)(2,1)S(1)} %collective-permute-done.4.refs_3_, ...), custom_call_target="tpu_custom_call" | custom-call | bytes 1 | tf_op jit(solution)/shard_map/combine/pallas_call | solution.py:664
  33.4 1.9 %finish_ahead.1 = (f32[4,2,512,128]{3,2,1,0:T(8,128)}, f32[2,512,128]{2,1,0:T(8,128)S(1)}, f32[2,512,128]{2,1,0:T(8,128)S(1)}) custom-call(s32[32]{0:T(128)S(1)} %copy-done.3, f32[1024,128]{1,0:T(8,128)S(1)} %combine.7.refs_0_, bf16[768,128]{1,0:T(8,128)(2,1)S(1)} %collective-permute-done.10.refs_1_, ...), custom_call_target="tpu_custom_call" | custom-call | bytes 1 | tf_op jit(solution)/shard_map/finish_ahead/pallas_call | solution.py:721
  35.4 0.0 collective-permute-done.9.refs_1_
  35.4 0.0 collective-permute-done.8.refs_0_
  35.4 1.6 %join.1 = (f32[4,2,512,128]{3,2,1,0:T(8,128)}, f32[2,512,128]{2,1,0:T(8,128)S(1)}) custom-call(s32[32]{0:T(128)S(1)} %copy-done.3, bf16[1024,128]{1,0:T(8,128)(2,1)S(1)} %collective-permute-done.8.refs_0_, bf16[256,128]{1,0:T(8,128)(2,1)S(1)} %collective-permute-done.9.refs_1_, ...), custom_call_target="tpu_custom_call", output_to_operand_aliasing={{0}: (7, {})} | custom-call | flops 5000000000 | bytes 18000000 | tf_op jit(solution)/shard_map/join/pallas_call | solution.py:731
  37.0 1.7 %collective-permute-done.6.refs_0_ = bf16[1024,128]{1,0:T(8,128)(2,1)S(1)} collective-permute-done((bf16[1024,128]{1,0:T(8,128)(2,1)S(1)}, bf16[1024,128]{1,0:T(8,128)(2,1)S(1)}, u32[]{:S(2)}, u32[]{:S(2)}) %collective-permute-start.6) | collective-permute-done | bytes 262176 | tf_op jit(solution)/shard_map/ppermute | solution.py:599
  38.6 1.6 %finish_last.1 = (f32[4,2,512,128]{3,2,1,0:T(8,128)}, f32[2,512,128]{2,1,0:T(8,128)}) custom-call(s32[32]{0:T(128)S(1)} %copy-done.3, bf16[1024,128]{1,0:T(8,128)(2,1)S(1)} %collective-permute-done.6.refs_0_, f32[4,16,128]{2,1,0:T(8,128)S(1)} %get-tuple-element.39.refs_2_.refs_3_.refs_1_, ...), custom_call_target="tpu_custom_call", output_to_operand_aliasing={{0}: (5, {})} | custom-call | flops 30000001024 | bytes 108000000 | tf_op jit(solution)/shard_map/finish_last/pallas_call | solution.py:752
  (1 shorter events, 0.0 us)
Async XLA Ops:
  0.6 5.6 %collective-permute-start = (bf16[2,2,32,8192]{3,2,1,0:T(8,128)(2,1)}, bf16[2,2,32,8192]{3,2,1,0:T(8,128)(2,1)S(1)}, u32[]{:S(2)}, u32[]{:S(2)}) collective-permute-start(bf16[2,2,32,8192]{3,2,1,0:T(8,128)(2,1)} %refs_0_.6), channel_id=1, source_target_pairs={{0,2},{2,0},{4,6},{6,4},{8,10},{10,8},{12,14},{14,12},{16,18},{18,... | collective-permute-start | bytes 6291464 | tf_op jit(solution)/shard_map/ppermute | solution.py:595
  1.1 4.0 %copy-start.3 = (s32[32]{0:T(128)S(1)}, s32[32]{0:T(128)}, u32[]{:S(2)}) copy-start(s32[32]{0:T(128)} %parent_of.7) | copy-start | bytes 388
  1.2 4.0 %copy-start.4 = (s32[65536]{0:T(1024)S(1)}, s32[65536]{0:T(1024)}, u32[]{:S(2)}) copy-start(s32[65536]{0:T(1024)} %param.17) | copy-start | bytes 786436
  1.2 4.0 %copy-start.5 = (f32[4,3]{1,0:T(4,128)S(1)}, f32[4,3]{1,0:T(4,128)}, u32[]{:S(2)}) copy-start(f32[4,3]{1,0:T(4,128)} %center.1) | copy-start | bytes 148
  1.2 4.0 %copy-start.6 = (s32[32]{0:T(128)S(1)}, s32[32]{0:T(128)}, u32[]{:S(2)}) copy-start(s32[32]{0:T(128)} %octant_of.1) | copy-start | bytes 388
  2.2 8.6 %collective-permute-start.2 = (bf16[2,2,32,512]{3,2,1,0:T(8,128)(2,1)S(1)}, bf16[2,2,32,512]{3,2,1,0:T(8,128)(2,1)S(1)}, u32[]{:S(2)}, u32[]{:S(2)}) collective-permute-start(bf16[2,2,32,512]{3,2,1,0:T(8,128)(2,1)S(1)} %get-tuple-element.60), channel_id=1, source_target_pairs={{0,6},{2,4},{4,2},{6,0},{8,14},{10,12},{12,10},{14,8},{16,22},{18,... | collective-permute-start | bytes 393224 | tf_op jit(solution)/shard_map/ppermute | solution.py:595
  4.9 7.0 %collective-permute-start.1 = (bf16[2,2,32,512]{3,2,1,0:T(8,128)(2,1)S(1)}, bf16[2,2,32,512]{3,2,1,0:T(8,128)(2,1)S(1)}, u32[]{:S(2)}, u32[]{:S(2)}) collective-permute-start(bf16[2,2,32,512]{3,2,1,0:T(8,128)(2,1)S(1)} %get-tuple-element.61), channel_id=1, source_target_pairs={{0,4},{2,6},{4,0},{6,2},{8,12},{10,14},{12,8},{14,10},{16,20},{18,... | collective-permute-start | bytes 393224 | tf_op jit(solution)/shard_map/ppermute | solution.py:595
  5.1 1.6 %copy-start = (bf16[2,2,32,8192]{3,2,1,0:T(8,128)(2,1)S(1)}, bf16[2,2,32,8192]{3,2,1,0:T(8,128)(2,1)}, u32[]{:S(2)}) copy-start(bf16[2,2,32,8192]{3,2,1,0:T(8,128)(2,1)} %refs_0_.6) | copy-start | bytes 6291460
  6.2 5.8 %copy-start.1 = (bf16[256,256]{1,0:T(8,128)(2,1)S(1)}, bf16[256,256]{1,0:T(8,128)(2,1)}, u32[]{:S(2)}) copy-start(bf16[256,256]{1,0:T(8,128)(2,1)} %constant.21.clone.refs_8_.refs_9_.refs_11_) | copy-start | bytes 393220
  6.2 5.8 %copy-start.2 = (bf16[256,256]{1,0:T(8,128)(2,1)S(1)}, bf16[256,256]{1,0:T(8,128)(2,1)}, u32[]{:S(2)}) copy-start(bf16[256,256]{1,0:T(8,128)(2,1)} %constant.20.clone.refs_7_.refs_8_.refs_10_) | copy-start | bytes 393220
  7.2 10.5 %collective-permute-start.5 = (bf16[32,128]{1,0:T(8,128)(2,1)S(1)}, bf16[32,128]{1,0:T(8,128)(2,1)S(1)}, u32[]{:S(2)}, u32[]{:S(2)}) collective-permute-start(bf16[32,128]{1,0:T(8,128)(2,1)S(1)} %get-tuple-element.38), channel_id=1, source_target_pairs={{0,5},{1,4},{2,7},{3,6},{4,1},{5,0},{6,3},{7,2},{8,13},{9,12},{10,... | collective-permute-start | bytes 24584 | tf_op jit(solution)/shard_map/ppermute | solution.py:615
  10.2 7.6 %collective-permute-start.4 = (bf16[32,128]{1,0:T(8,128)(2,1)S(1)}, bf16[32,128]{1,0:T(8,128)(2,1)S(1)}, u32[]{:S(2)}, u32[]{:S(2)}) collective-permute-start(bf16[32,128]{1,0:T(8,128)(2,1)S(1)} %get-tuple-element.38), channel_id=1, source_target_pairs={{0,1},{1,0},{2,3},{3,2},{4,5},{5,4},{6,7},{7,6},{8,9},{9,8},{10,11... | collective-permute-start | bytes 24584 | tf_op jit(solution)/shard_map/ppermute | solution.py:615
  10.7 8.6 %collective-permute-start.7 = (bf16[1088,128]{1,0:T(8,128)(2,1)S(1)}, bf16[1088,128]{1,0:T(8,128)(2,1)S(1)}, u32[]{:S(2)}, u32[]{:S(2)}) collective-permute-start(bf16[1088,128]{1,0:T(8,128)(2,1)S(1)} %get-tuple-element.42), channel_id=1, source_target_pairs={{0,4},{2,6},{4,0},{6,2},{8,12},{10,14},{12,8},{14,10},{16,20},{18,... | collective-permute-start | bytes 835592 | tf_op jit(solution)/shard_map/ppermute | solution.py:595
  13.0 11.8 %collective-permute-start.10 = (bf16[768,128]{1,0:T(8,128)(2,1)S(1)}, bf16[768,128]{1,0:T(8,128)(2,1)S(1)}, u32[]{:S(2)}, u32[]{:S(2)}) collective-permute-start(bf16[768,128]{1,0:T(8,128)(2,1)S(1)} %combine.4), channel_id=1, source_target_pairs={{0,16},{2,18},{4,20},{6,22},{8,24},{10,26},{12,28},{14,30},{16,0},... | collective-permute-start | bytes 589832 | tf_op jit(solution)/shard_map/ppermute | solution.py:599
  15.7 11.6 %collective-permute-start.3 = (bf16[1056,128]{1,0:T(8,128)(2,1)S(1)}, bf16[1056,128]{1,0:T(8,128)(2,1)S(1)}, u32[]{:S(2)}, u32[]{:S(2)}) collective-permute-start(bf16[1056,128]{1,0:T(8,128)(2,1)S(1)} %get-tuple-element.37), channel_id=1, source_target_pairs={{0,4},{2,6},{4,0},{6,2},{8,12},{10,14},{12,8},{14,10},{16,20},{18,... | collective-permute-start | bytes 811016 | tf_op jit(solution)/shard_map/ppermute | solution.py:595
  21.6 10.0 %collective-permute-start.11 = (bf16[1056,128]{1,0:T(8,128)(2,1)S(1)}, bf16[1056,128]{1,0:T(8,128)(2,1)S(1)}, u32[]{:S(2)}, u32[]{:S(2)}) collective-permute-start(bf16[1056,128]{1,0:T(8,128)(2,1)S(1)} %get-tuple-element.49), channel_id=1, source_target_pairs={{0,4},{2,6},{4,0},{6,2},{8,12},{10,14},{12,8},{14,10},{16,20},{18,... | collective-permute-start | bytes 811016 | tf_op jit(solution)/shard_map/ppermute | solution.py:595
  22.3 13.1 %collective-permute-start.8 = (bf16[1024,128]{1,0:T(8,128)(2,1)S(1)}, bf16[1024,128]{1,0:T(8,128)(2,1)S(1)}, u32[]{:S(2)}, u32[]{:S(2)}) collective-permute-start(bf16[1024,128]{1,0:T(8,128)(2,1)S(1)} %get-tuple-element.45), channel_id=1, source_target_pairs={{0,8},{2,10},{4,12},{6,14},{8,16},{10,18},{12,20},{14,22},{16,24},... | collective-permute-start | bytes 786440 | tf_op jit(solution)/shard_map/ppermute | solution.py:599
  24.8 10.6 %collective-permute-start.9 = (bf16[256,128]{1,0:T(8,128)(2,1)S(1)}, bf16[256,128]{1,0:T(8,128)(2,1)S(1)}, u32[]{:S(2)}, u32[]{:S(2)}) collective-permute-start(bf16[256,128]{1,0:T(8,128)(2,1)S(1)} %get-tuple-element.46), channel_id=1, source_target_pairs={{0,16},{2,18},{4,20},{6,22},{8,24},{10,26},{12,28},{14,30},{16,0},... | collective-permute-start | bytes 196616 | tf_op jit(solution)/shard_map/ppermute | solution.py:599
  29.1 9.5 %collective-permute-start.6 = (bf16[1024,128]{1,0:T(8,128)(2,1)S(1)}, bf16[1024,128]{1,0:T(8,128)(2,1)S(1)}, u32[]{:S(2)}, u32[]{:S(2)}) collective-permute-start(bf16[1024,128]{1,0:T(8,128)(2,1)S(1)} %combine.5), channel_id=1, source_target_pairs={{0,24},{2,26},{4,28},{6,30},{8,0},{10,2},{12,4},{14,6},{16,8},{18,... | collective-permute-start | bytes 786440 | tf_op jit(solution)/shard_map/ppermute | solution.py:599

commit v7 on v6

--- a/solution.py
+++ b/solution.py
@@ -497,32 +497,34 @@
     name_copy = pltpu.make_async_copy(parent_of, names, name_sem)
     name_copy.start()
     last = len(steps)
+    groups = lax.axis_size("wide") // members
+    group_at = lax.axis_index("wide") // members
+    copies = []
+
+    def send(index, step):
+        name = names[group_before(group_at, step, groups) * members * boxes]
+        copies.append(pltpu.make_async_copy(patterns.at[index], parent_out.at[name], sems.at[index]))
+        copies[-1].start()
+
     patterns[last] = early[...]
-    for source in range(sources):
-        at = pl.ds(source * rows, rows)
-        far_real, far_imag = far_in[0, at, :], far_in[1, at, :]
-        for index, step in enumerate(steps):
+    far_out[...] = far_in[...]
+    place_columns(
+        late, columns, sources, rows, center_cos.at[early_step], center_sin.at[early_step], patterns.at[last], far_out
+    )
+    name_copy.wait()
+    send(last, early_step)
+    for index, step in enumerate(steps):
+        cosine, sine = center_cos[step], center_sin[step]
+        for source in range(sources):
+            at = pl.ds(source * rows, rows)
             real, imag = (
                 whole[index][pl.ds((half * sources + source) * rows, rows), :].astype(jnp.float32) for half in range(2)
             )
-            cosine, sine = center_cos[step], center_sin[step]
             patterns[index, 0, at, :] = real
             patterns[index, 1, at, :] = imag
-            far_real = far_real + (cosine * real - sine * imag)
-            far_imag = far_imag + (sine * real + cosine * imag)
-        far_out[0, at, :] = far_real
-        far_out[1, at, :] = far_imag
-    place_columns(
-        late, columns, sources, rows, center_cos.at[early_step], center_sin.at[early_step], patterns.at[last], far_out
-    )
-    name_copy.wait()
-    groups = lax.axis_size("wide") // members
-    group_at = lax.axis_index("wide") // members
-    copies = []
-    for index, step in enumerate((*steps, early_step)):
-        name = names[group_before(group_at, step, groups) * members * boxes]
-        copies.append(pltpu.make_async_copy(patterns.at[index], parent_out.at[name], sems.at[index]))
-        copies[-1].start()
+            far_out[0, at, :] += cosine * real - sine * imag
+            far_out[1, at, :] += sine * real + cosine * imag
+        send(index, step)
     for copy in copies:
         copy.wait()
 

time: 40.4 us -> 40.4 us (level)
  no operation moved by 1% of the time
where the time goes in v7:
time: 40.4 us; the launch traced here: 40.2 us
  starting transfers between devices  18.8 us (47%)
  Pallas kernels  13.7 us (34%)
  waiting for transfers between devices  5.37 us (13%)
  local copies, waits for them, and re-layouts  1.6 us (4%)
  between operations  0.76 us (2%)
    ppermute x4, starting transfers between devices, move_by(): lax.ppermute(array, 'wide', [(i, (i + shift) % n_wide) for i in range(n_w...  9.28 us
    pallas_call x4, Pallas kernels, sums_of(): pl.pallas_call(functools.partial(combine_kernel, jobs, members, boxes, so...  6.92 us
    ppermute x6, starting transfers between devices, swap_with(): return lax.ppermute(array, 'wide', [(i, i ^ step) for i in range(n_wide)])  6.07 us
    ppermute x2, starting transfers between devices, other_half(): return lax.ppermute(array, ('wide', 'narrow'), pairs)  3.48 us
    ppermute x6, waiting for transfers between devices, swap_with(): return lax.ppermute(array, 'wide', [(i, i ^ step) for i in range(n_wide)])  2.75 us
    ppermute x4, waiting for transfers between devices, move_by(): lax.ppermute(array, 'wide', [(i, (i + shift) % n_wide) for i in range(n_w...  2.61 us
    pallas_call x1, Pallas kernels, grouped(): pl.pallas_call(functools.partial(finish_ahead_kernel, ahead, top, early_c...  1.95 us
    pallas_call x1, Pallas kernels, grouped(): pl.pallas_call(functools.partial(finish_kernel, steps, members, boxes, so...  1.58 us
  transfers between devices with their start and end apart: 12, of which 4 were waited for; matrix products, arithmetic and copies ran while one was open for 3% of the time, Pallas kernels for 30%

profile of v7, /device:TPU:0, one launch (start us, length us, event | category | flops | bytes accessed | tf_op | source)
XLA Modules:
  0.0 40.2 jit_solution(6118306255487076208)
XLA Ops:
  0.6 0.5 %collective-permute-start = (bf16[2,2,32,8192]{3,2,1,0:T(8,128)(2,1)}, bf16[2,2,32,8192]{3,2,1,0:T(8,128)(2,1)S(1)}, u32[]{:S(2)}, u32[]{:S(2)}) collective-permute-start(bf16[2,2,32,8192]{3,2,1,0:T(8,128)(2,1)} %refs_0_.6), channel_id=1, source_target_pairs={{0,2},{2,0},{4,6},{6,4},{8,10},{10,8},{12,14},{14,12},{16,18},{18,... | collective-permute-start | bytes 6291464 | tf_op jit(solution)/shard_map/ppermute | solution.py:597
  1.1 0.0 copy-start.3
  1.2 0.0 copy-start.4
  1.2 0.0 copy-start.5
  1.2 1.0 %constant_dynamic-slice_fusion = (bf16[2,2,32,512]{3,2,1,0:T(8,128)(2,1)S(1)}, bf16[2,2,32,512]{3,2,1,0:T(8,128)(2,1)S(1)}) fusion(bf16[2,2,32,8192]{3,2,1,0:T(8,128)(2,1)} %refs_0_.6, s32[]{:T(128)S(6)} %select_n.7, s32[]{:T(128)S(6)} %select_n.6), kind=kLoop, calls=%fused_computation | loop fusion | bytes 524296 | tf_op jit(solution)/shard_map/dynamic_slice | solution.py:611
  2.2 2.7 %collective-permute-start.2 = (bf16[2,2,32,512]{3,2,1,0:T(8,128)(2,1)S(1)}, bf16[2,2,32,512]{3,2,1,0:T(8,128)(2,1)S(1)}, u32[]{:S(2)}, u32[]{:S(2)}) collective-permute-start(bf16[2,2,32,512]{3,2,1,0:T(8,128)(2,1)S(1)} %get-tuple-element.60), channel_id=1, source_target_pairs={{0,6},{2,4},{4,2},{6,0},{8,14},{10,12},{12,10},{14,8},{16,22},{18,... | collective-permute-start | bytes 393224 | tf_op jit(solution)/shard_map/ppermute | solution.py:597
  4.9 0.0 collective-permute-start.1
  4.9 0.2 axes.1
  5.1 0.0 copy-start
  5.1 0.0 copy-done.3
  5.2 0.0 copy-done.4
  5.2 0.0 copy-done.5
  5.2 0.0 copy-done.6
  5.2 1.0 %prep.1 = (f32[4,8,16,128]{3,2,1,0:T(8,128)S(1)}, f32[4,8,16,128]{3,2,1,0:T(8,128)S(1)}, f32[4,16,128]{2,1,0:T(8,128)S(1)}, f32[4,16,128]{2,1,0:T(8,128)S(1)}, f32[4,16,128]{2,1,0:T(8,128)S(1)}) custom-call(s32[32]{0:T(128)S(1)} %copy-done.3, s32[32]{0:T(128)S(1)} %copy-done.6, f32[4,3]{1,0:T(4,128)S(1)} %copy-done.5, s32[512,128]{1,0:T(8,128)S(1)} %bitcast.3, ...), custom_call_target="tpu_custom_call" | custom-call | flops 1000000000 | bytes 3600001 | tf_op jit(solution)/shard_map/prep/pallas_call | solution.py:627
  6.2 0.0 copy-start.1
  6.2 0.0 copy-start.2
  6.2 0.0 collective-permute-done.near.refs_1_
  6.2 0.5 %copy-done = bf16[2,2,32,8192]{3,2,1,0:T(8,128)(2,1)S(1)} copy-done((bf16[2,2,32,8192]{3,2,1,0:T(8,128)(2,1)S(1)}, bf16[2,2,32,8192]{3,2,1,0:T(8,128)(2,1)}, u32[]{:S(2)}) %copy-start) | copy-done | bytes 2097176
  6.7 0.5 %pack.1 = (bf16[1088,128]{1,0:T(8,128)(2,1)S(1)}, bf16[1056,128]{1,0:T(8,128)(2,1)S(1)}, bf16[1056,128]{1,0:T(8,128)(2,1)S(1)}, bf16[32,128]{1,0:T(8,128)(2,1)S(1)}) custom-call(bf16[2,2,32,8192]{3,2,1,0:T(8,128)(2,1)S(1)} %copy-done, bf16[2,2,32,8192]{3,2,1,0:T(8,128)(2,1)S(1)} %collective-permute-done.near.refs_1_), custom_call_target="tpu_custom_call" | custom-call | flops 1000000000 | bytes 3600001 | tf_op jit(solution)/shard_map/pack/pallas_call | solution.py:646
  7.2 2.9 %collective-permute-start.5 = (bf16[32,128]{1,0:T(8,128)(2,1)S(1)}, bf16[32,128]{1,0:T(8,128)(2,1)S(1)}, u32[]{:S(2)}, u32[]{:S(2)}) collective-permute-start(bf16[32,128]{1,0:T(8,128)(2,1)S(1)} %get-tuple-element.38), channel_id=1, source_target_pairs={{0,5},{1,4},{2,7},{3,6},{4,1},{5,0},{6,3},{7,2},{8,13},{9,12},{10,... | collective-permute-start | bytes 24584 | tf_op jit(solution)/shard_map/ppermute | solution.py:617
  10.2 0.5 %collective-permute-start.4 = (bf16[32,128]{1,0:T(8,128)(2,1)S(1)}, bf16[32,128]{1,0:T(8,128)(2,1)S(1)}, u32[]{:S(2)}, u32[]{:S(2)}) collective-permute-start(bf16[32,128]{1,0:T(8,128)(2,1)S(1)} %get-tuple-element.38), channel_id=1, source_target_pairs={{0,1},{1,0},{2,3},{3,2},{4,5},{5,4},{6,7},{7,6},{8,9},{9,8},{10,11... | collective-permute-start | bytes 24584 | tf_op jit(solution)/shard_map/ppermute | solution.py:617
  10.7 0.1 collective-permute-start.7
  10.8 0.0 collective-permute-done.2.refs_3_.refs_6_
  10.8 1.2 %collective-permute-done.1.refs_2_.refs_5_ = bf16[2,2,32,512]{3,2,1,0:T(8,128)(2,1)S(1)} collective-permute-done((bf16[2,2,32,512]{3,2,1,0:T(8,128)(2,1)S(1)}, bf16[2,2,32,512]{3,2,1,0:T(8,128)(2,1)S(1)}, u32[]{:S(2)}, u32[]{:S(2)}) %collective-permute-start.1) | collective-permute-done | bytes 131104 | tf_op jit(solution)/shard_map/ppermute | solution.py:597
  11.9 0.0 copy-done.1
  11.9 0.0 copy-done.2
  11.9 1.0 %combine.4 = bf16[768,128]{1,0:T(8,128)(2,1)S(1)} custom-call(bf16[2,2,32,8192]{3,2,1,0:T(8,128)(2,1)S(1)} %copy-done, bf16[2,2,32,8192]{3,2,1,0:T(8,128)(2,1)S(1)} %collective-permute-done.near.refs_1_, bf16[2,2,32,512]{3,2,1,0:T(8,128)(2,1)S(1)} %collective-permute-done.1.refs_2_.refs_5_, ...), custom_call_target="tpu_custom_call" | custom-call | flops 5000000000 | bytes 18000000 | tf_op jit(solution)/shard_map/combine/pallas_call | solution.py:666
  13.0 2.7 %collective-permute-start.10 = (bf16[768,128]{1,0:T(8,128)(2,1)S(1)}, bf16[768,128]{1,0:T(8,128)(2,1)S(1)}, u32[]{:S(2)}, u32[]{:S(2)}) collective-permute-start(bf16[768,128]{1,0:T(8,128)(2,1)S(1)} %combine.4), channel_id=1, source_target_pairs={{0,16},{2,18},{4,20},{6,22},{8,24},{10,26},{12,28},{14,30},{16,0},... | collective-permute-start | bytes 589832 | tf_op jit(solution)/shard_map/ppermute | solution.py:601
  15.7 2.0 %collective-permute-start.3 = (bf16[1056,128]{1,0:T(8,128)(2,1)S(1)}, bf16[1056,128]{1,0:T(8,128)(2,1)S(1)}, u32[]{:S(2)}, u32[]{:S(2)}) collective-permute-start(bf16[1056,128]{1,0:T(8,128)(2,1)S(1)} %get-tuple-element.37), channel_id=1, source_target_pairs={{0,4},{2,6},{4,0},{6,2},{8,12},{10,14},{12,8},{14,10},{16,20},{18,... | collective-permute-start | bytes 811016 | tf_op jit(solution)/shard_map/ppermute | solution.py:597
  17.8 0.0 collective-permute-done.5.refs_4_
  17.8 0.0 collective-permute-done.4.refs_3_
  17.8 1.6 %collective-permute-done.7.refs_2_ = bf16[1088,128]{1,0:T(8,128)(2,1)S(1)} collective-permute-done((bf16[1088,128]{1,0:T(8,128)(2,1)S(1)}, bf16[1088,128]{1,0:T(8,128)(2,1)S(1)}, u32[]{:S(2)}, u32[]{:S(2)}) %collective-permute-start.7) | collective-permute-done | bytes 278560 | tf_op jit(solution)/shard_map/ppermute | solution.py:597
  19.4 2.2 %combine.6 = (bf16[1024,128]{1,0:T(8,128)(2,1)S(1)}, bf16[256,128]{1,0:T(8,128)(2,1)S(1)}) custom-call(bf16[2,2,32,8192]{3,2,1,0:T(8,128)(2,1)S(1)} %copy-done, bf16[2,2,32,8192]{3,2,1,0:T(8,128)(2,1)S(1)} %collective-permute-done.near.refs_1_, bf16[1088,128]{1,0:T(8,128)(2,1)S(1)} %collective-permute-done.7.refs_2_, ...), custom_call_target="tpu_custom_call" | custom-call | flops 30000001024 | bytes 108000000 | tf_op jit(solution)/shard_map/combine/pallas_call | solution.py:666
  21.6 0.7 %collective-permute-start.11 = (bf16[1056,128]{1,0:T(8,128)(2,1)S(1)}, bf16[1056,128]{1,0:T(8,128)(2,1)S(1)}, u32[]{:S(2)}, u32[]{:S(2)}) collective-permute-start(bf16[1056,128]{1,0:T(8,128)(2,1)S(1)} %get-tuple-element.49), channel_id=1, source_target_pairs={{0,4},{2,6},{4,0},{6,2},{8,12},{10,14},{12,8},{14,10},{16,20},{18,... | collective-permute-start | bytes 811016 | tf_op jit(solution)/shard_map/ppermute | solution.py:597
  22.3 1.6 %collective-permute-start.8 = (bf16[1024,128]{1,0:T(8,128)(2,1)S(1)}, bf16[1024,128]{1,0:T(8,128)(2,1)S(1)}, u32[]{:S(2)}, u32[]{:S(2)}) collective-permute-start(bf16[1024,128]{1,0:T(8,128)(2,1)S(1)} %get-tuple-element.45), channel_id=1, source_target_pairs={{0,8},{2,10},{4,12},{6,14},{8,16},{10,18},{12,20},{14,22},{16,24},... | collective-permute-start | bytes 786440 | tf_op jit(solution)/shard_map/ppermute | solution.py:601
  23.9 0.9 %collective-permute-done.10.refs_1_ = bf16[768,128]{1,0:T(8,128)(2,1)S(1)} collective-permute-done((bf16[768,128]{1,0:T(8,128)(2,1)S(1)}, bf16[768,128]{1,0:T(8,128)(2,1)S(1)}, u32[]{:S(2)}, u32[]{:S(2)}) %collective-permute-start.10) | collective-permute-done | bytes 196640 | tf_op jit(solution)/shard_map/ppermute | solution.py:601
  24.8 2.5 %collective-permute-start.9 = (bf16[256,128]{1,0:T(8,128)(2,1)S(1)}, bf16[256,128]{1,0:T(8,128)(2,1)S(1)}, u32[]{:S(2)}, u32[]{:S(2)}) collective-permute-start(bf16[256,128]{1,0:T(8,128)(2,1)S(1)} %get-tuple-element.46), channel_id=1, source_target_pairs={{0,16},{2,18},{4,20},{6,22},{8,24},{10,26},{12,28},{14,30},{16,0},... | collective-permute-start | bytes 196616 | tf_op jit(solution)/shard_map/ppermute | solution.py:601
  27.3 0.0 collective-permute-done.3.refs_2_
  27.3 1.8 %combine.5 = bf16[1024,128]{1,0:T(8,128)(2,1)S(1)} custom-call(bf16[2,2,32,8192]{3,2,1,0:T(8,128)(2,1)S(1)} %copy-done, bf16[2,2,32,8192]{3,2,1,0:T(8,128)(2,1)S(1)} %collective-permute-done.near.refs_1_, bf16[1056,128]{1,0:T(8,128)(2,1)S(1)} %collective-permute-done.3.refs_2_, bf16[32,128]{1,0:T(8,128)(2,1)S(1)} %collective-permute-done.4.refs_3_, ...), custom_call_target="tpu_custom_call" | custom-call | flops 2000000000 | bytes 7200001 | tf_op jit(solution)/shard_map/combine/pallas_call | solution.py:666
  29.1 2.5 %collective-permute-start.6 = (bf16[1024,128]{1,0:T(8,128)(2,1)S(1)}, bf16[1024,128]{1,0:T(8,128)(2,1)S(1)}, u32[]{:S(2)}, u32[]{:S(2)}) collective-permute-start(bf16[1024,128]{1,0:T(8,128)(2,1)S(1)} %combine.5), channel_id=1, source_target_pairs={{0,24},{2,26},{4,28},{6,30},{8,0},{10,2},{12,4},{14,6},{16,8},{18,... | collective-permute-start | bytes 786440 | tf_op jit(solution)/shard_map/ppermute | solution.py:601
  31.6 0.0 collective-permute-done.11.refs_2_
  31.6 1.8 %combine.7.refs_0_ = f32[1024,128]{1,0:T(8,128)S(1)} custom-call(bf16[2,2,32,8192]{3,2,1,0:T(8,128)(2,1)S(1)} %copy-done, bf16[2,2,32,8192]{3,2,1,0:T(8,128)(2,1)S(1)} %collective-permute-done.near.refs_1_, bf16[1056,128]{1,0:T(8,128)(2,1)S(1)} %collective-permute-done.11.refs_2_, bf16[32,128]{1,0:T(8,128)(2,1)S(1)} %collective-permute-done.4.refs_3_, ...), custom_call_target="tpu_custom_call" | custom-call | bytes 1 | tf_op jit(solution)/shard_map/combine/pallas_call | solution.py:666
  33.4 1.9 %finish_ahead.1 = (f32[4,2,512,128]{3,2,1,0:T(8,128)}, f32[2,512,128]{2,1,0:T(8,128)S(1)}, f32[2,512,128]{2,1,0:T(8,128)S(1)}) custom-call(s32[32]{0:T(128)S(1)} %copy-done.3, f32[1024,128]{1,0:T(8,128)S(1)} %combine.7.refs_0_, bf16[768,128]{1,0:T(8,128)(2,1)S(1)} %collective-permute-done.10.refs_1_, ...), custom_call_target="tpu_custom_call" | custom-call | bytes 1 | tf_op jit(solution)/shard_map/finish_ahead/pallas_call | solution.py:723
  35.4 0.0 collective-permute-done.9.refs_1_
  35.4 0.0 collective-permute-done.8.refs_0_
  35.4 1.5 %join.1 = (f32[4,2,512,128]{3,2,1,0:T(8,128)}, f32[2,512,128]{2,1,0:T(8,128)S(1)}) custom-call(s32[32]{0:T(128)S(1)} %copy-done.3, bf16[1024,128]{1,0:T(8,128)(2,1)S(1)} %collective-permute-done.8.refs_0_, bf16[256,128]{1,0:T(8,128)(2,1)S(1)} %collective-permute-done.9.refs_1_, ...), custom_call_target="tpu_custom_call", output_to_operand_aliasing={{0}: (7, {})} | custom-call | flops 5000000000 | bytes 18000000 | tf_op jit(solution)/shard_map/join/pallas_call | solution.py:733
  36.9 1.7 %collective-permute-done.6.refs_0_ = bf16[1024,128]{1,0:T(8,128)(2,1)S(1)} collective-permute-done((bf16[1024,128]{1,0:T(8,128)(2,1)S(1)}, bf16[1024,128]{1,0:T(8,128)(2,1)S(1)}, u32[]{:S(2)}, u32[]{:S(2)}) %collective-permute-start.6) | collective-permute-done | bytes 262176 | tf_op jit(solution)/shard_map/ppermute | solution.py:601
  38.6 1.6 %finish_last.1 = (f32[4,2,512,128]{3,2,1,0:T(8,128)}, f32[2,512,128]{2,1,0:T(8,128)}) custom-call(s32[32]{0:T(128)S(1)} %copy-done.3, bf16[1024,128]{1,0:T(8,128)(2,1)S(1)} %collective-permute-done.6.refs_0_, f32[4,16,128]{2,1,0:T(8,128)S(1)} %get-tuple-element.39.refs_2_.refs_3_.refs_1_, ...), custom_call_target="tpu_custom_call", output_to_operand_aliasing={{0}: (5, {})} | custom-call | flops 30000001024 | bytes 108000000 | tf_op jit(solution)/shard_map/finish_last/pallas_call | solution.py:754
  (1 shorter events, 0.0 us)
Async XLA Ops:
  0.6 5.6 %collective-permute-start = (bf16[2,2,32,8192]{3,2,1,0:T(8,128)(2,1)}, bf16[2,2,32,8192]{3,2,1,0:T(8,128)(2,1)S(1)}, u32[]{:S(2)}, u32[]{:S(2)}) collective-permute-start(bf16[2,2,32,8192]{3,2,1,0:T(8,128)(2,1)} %refs_0_.6), channel_id=1, source_target_pairs={{0,2},{2,0},{4,6},{6,4},{8,10},{10,8},{12,14},{14,12},{16,18},{18,... | collective-permute-start | bytes 6291464 | tf_op jit(solution)/shard_map/ppermute | solution.py:597
  1.1 4.0 %copy-start.3 = (s32[32]{0:T(128)S(1)}, s32[32]{0:T(128)}, u32[]{:S(2)}) copy-start(s32[32]{0:T(128)} %parent_of.7) | copy-start | bytes 388
  1.2 4.0 %copy-start.4 = (s32[65536]{0:T(1024)S(1)}, s32[65536]{0:T(1024)}, u32[]{:S(2)}) copy-start(s32[65536]{0:T(1024)} %param.17) | copy-start | bytes 786436
  1.2 4.0 %copy-start.5 = (f32[4,3]{1,0:T(4,128)S(1)}, f32[4,3]{1,0:T(4,128)}, u32[]{:S(2)}) copy-start(f32[4,3]{1,0:T(4,128)} %center.1) | copy-start | bytes 148
  1.2 4.0 %copy-start.6 = (s32[32]{0:T(128)S(1)}, s32[32]{0:T(128)}, u32[]{:S(2)}) copy-start(s32[32]{0:T(128)} %octant_of.1) | copy-start | bytes 388
  2.2 8.6 %collective-permute-start.2 = (bf16[2,2,32,512]{3,2,1,0:T(8,128)(2,1)S(1)}, bf16[2,2,32,512]{3,2,1,0:T(8,128)(2,1)S(1)}, u32[]{:S(2)}, u32[]{:S(2)}) collective-permute-start(bf16[2,2,32,512]{3,2,1,0:T(8,128)(2,1)S(1)} %get-tuple-element.60), channel_id=1, source_target_pairs={{0,6},{2,4},{4,2},{6,0},{8,14},{10,12},{12,10},{14,8},{16,22},{18,... | collective-permute-start | bytes 393224 | tf_op jit(solution)/shard_map/ppermute | solution.py:597
  4.9 7.0 %collective-permute-start.1 = (bf16[2,2,32,512]{3,2,1,0:T(8,128)(2,1)S(1)}, bf16[2,2,32,512]{3,2,1,0:T(8,128)(2,1)S(1)}, u32[]{:S(2)}, u32[]{:S(2)}) collective-permute-start(bf16[2,2,32,512]{3,2,1,0:T(8,128)(2,1)S(1)} %get-tuple-element.61), channel_id=1, source_target_pairs={{0,4},{2,6},{4,0},{6,2},{8,12},{10,14},{12,8},{14,10},{16,20},{18,... | collective-permute-start | bytes 393224 | tf_op jit(solution)/shard_map/ppermute | solution.py:597
  5.1 1.6 %copy-start = (bf16[2,2,32,8192]{3,2,1,0:T(8,128)(2,1)S(1)}, bf16[2,2,32,8192]{3,2,1,0:T(8,128)(2,1)}, u32[]{:S(2)}) copy-start(bf16[2,2,32,8192]{3,2,1,0:T(8,128)(2,1)} %refs_0_.6) | copy-start | bytes 6291460
  6.2 5.8 %copy-start.1 = (bf16[256,256]{1,0:T(8,128)(2,1)S(1)}, bf16[256,256]{1,0:T(8,128)(2,1)}, u32[]{:S(2)}) copy-start(bf16[256,256]{1,0:T(8,128)(2,1)} %constant.21.clone.refs_8_.refs_9_.refs_11_) | copy-start | bytes 393220
  6.2 5.8 %copy-start.2 = (bf16[256,256]{1,0:T(8,128)(2,1)S(1)}, bf16[256,256]{1,0:T(8,128)(2,1)}, u32[]{:S(2)}) copy-start(bf16[256,256]{1,0:T(8,128)(2,1)} %constant.20.clone.refs_7_.refs_8_.refs_10_) | copy-start | bytes 393220
  7.2 10.5 %collective-permute-start.5 = (bf16[32,128]{1,0:T(8,128)(2,1)S(1)}, bf16[32,128]{1,0:T(8,128)(2,1)S(1)}, u32[]{:S(2)}, u32[]{:S(2)}) collective-permute-start(bf16[32,128]{1,0:T(8,128)(2,1)S(1)} %get-tuple-element.38), channel_id=1, source_target_pairs={{0,5},{1,4},{2,7},{3,6},{4,1},{5,0},{6,3},{7,2},{8,13},{9,12},{10,... | collective-permute-start | bytes 24584 | tf_op jit(solution)/shard_map/ppermute | solution.py:617
  10.2 7.6 %collective-permute-start.4 = (bf16[32,128]{1,0:T(8,128)(2,1)S(1)}, bf16[32,128]{1,0:T(8,128)(2,1)S(1)}, u32[]{:S(2)}, u32[]{:S(2)}) collective-permute-start(bf16[32,128]{1,0:T(8,128)(2,1)S(1)} %get-tuple-element.38), channel_id=1, source_target_pairs={{0,1},{1,0},{2,3},{3,2},{4,5},{5,4},{6,7},{7,6},{8,9},{9,8},{10,11... | collective-permute-start | bytes 24584 | tf_op jit(solution)/shard_map/ppermute | solution.py:617
  10.7 8.6 %collective-permute-start.7 = (bf16[1088,128]{1,0:T(8,128)(2,1)S(1)}, bf16[1088,128]{1,0:T(8,128)(2,1)S(1)}, u32[]{:S(2)}, u32[]{:S(2)}) collective-permute-start(bf16[1088,128]{1,0:T(8,128)(2,1)S(1)} %get-tuple-element.42), channel_id=1, source_target_pairs={{0,4},{2,6},{4,0},{6,2},{8,12},{10,14},{12,8},{14,10},{16,20},{18,... | collective-permute-start | bytes 835592 | tf_op jit(solution)/shard_map/ppermute | solution.py:597
  13.0 11.8 %collective-permute-start.10 = (bf16[768,128]{1,0:T(8,128)(2,1)S(1)}, bf16[768,128]{1,0:T(8,128)(2,1)S(1)}, u32[]{:S(2)}, u32[]{:S(2)}) collective-permute-start(bf16[768,128]{1,0:T(8,128)(2,1)S(1)} %combine.4), channel_id=1, source_target_pairs={{0,16},{2,18},{4,20},{6,22},{8,24},{10,26},{12,28},{14,30},{16,0},... | collective-permute-start | bytes 589832 | tf_op jit(solution)/shard_map/ppermute | solution.py:601
  15.7 11.6 %collective-permute-start.3 = (bf16[1056,128]{1,0:T(8,128)(2,1)S(1)}, bf16[1056,128]{1,0:T(8,128)(2,1)S(1)}, u32[]{:S(2)}, u32[]{:S(2)}) collective-permute-start(bf16[1056,128]{1,0:T(8,128)(2,1)S(1)} %get-tuple-element.37), channel_id=1, source_target_pairs={{0,4},{2,6},{4,0},{6,2},{8,12},{10,14},{12,8},{14,10},{16,20},{18,... | collective-permute-start | bytes 811016 | tf_op jit(solution)/shard_map/ppermute | solution.py:597
  21.6 10.0 %collective-permute-start.11 = (bf16[1056,128]{1,0:T(8,128)(2,1)S(1)}, bf16[1056,128]{1,0:T(8,128)(2,1)S(1)}, u32[]{:S(2)}, u32[]{:S(2)}) collective-permute-start(bf16[1056,128]{1,0:T(8,128)(2,1)S(1)} %get-tuple-element.49), channel_id=1, source_target_pairs={{0,4},{2,6},{4,0},{6,2},{8,12},{10,14},{12,8},{14,10},{16,20},{18,... | collective-permute-start | bytes 811016 | tf_op jit(solution)/shard_map/ppermute | solution.py:597
  22.3 13.1 %collective-permute-start.8 = (bf16[1024,128]{1,0:T(8,128)(2,1)S(1)}, bf16[1024,128]{1,0:T(8,128)(2,1)S(1)}, u32[]{:S(2)}, u32[]{:S(2)}) collective-permute-start(bf16[1024,128]{1,0:T(8,128)(2,1)S(1)} %get-tuple-element.45), channel_id=1, source_target_pairs={{0,8},{2,10},{4,12},{6,14},{8,16},{10,18},{12,20},{14,22},{16,24},... | collective-permute-start | bytes 786440 | tf_op jit(solution)/shard_map/ppermute | solution.py:601
  24.8 10.6 %collective-permute-start.9 = (bf16[256,128]{1,0:T(8,128)(2,1)S(1)}, bf16[256,128]{1,0:T(8,128)(2,1)S(1)}, u32[]{:S(2)}, u32[]{:S(2)}) collective-permute-start(bf16[256,128]{1,0:T(8,128)(2,1)S(1)} %get-tuple-element.46), channel_id=1, source_target_pairs={{0,16},{2,18},{4,20},{6,22},{8,24},{10,26},{12,28},{14,30},{16,0},... | collective-permute-start | bytes 196616 | tf_op jit(solution)/shard_map/ppermute | solution.py:601
  29.1 9.5 %collective-permute-start.6 = (bf16[1024,128]{1,0:T(8,128)(2,1)S(1)}, bf16[1024,128]{1,0:T(8,128)(2,1)S(1)}, u32[]{:S(2)}, u32[]{:S(2)}) collective-permute-start(bf16[1024,128]{1,0:T(8,128)(2,1)S(1)} %combine.5), channel_id=1, source_target_pairs={{0,24},{2,26},{4,28},{6,30},{8,0},{10,2},{12,4},{14,6},{16,8},{18,... | collective-permute-start | bytes 786440 | tf_op jit(solution)/shard_map/ppermute | solution.py:601

commit v8 on v7

--- a/solution.py
+++ b/solution.py
@@ -750,7 +750,7 @@
         parent_pattern,
     )
     steps = [1]
-    parts = 4
+    parts = 2
     parent_pattern, far_field = pl.pallas_call(
         functools.partial(finish_kernel, steps, members, boxes, sources, out_rows, parts),
         out_shape=[f32(parents, *whole.shape), whole],

time: 40.4 us -> 40.4 us (level)
  no operation moved by 1% of the time
where the time goes in v8:
time: 40.4 us; the launch traced here: 40.2 us
  starting transfers between devices  18.8 us (47%)
  Pallas kernels  13.7 us (34%)
  waiting for transfers between devices  5.37 us (13%)
  local copies, waits for them, and re-layouts  1.6 us (4%)
  between operations  0.76 us (2%)
    ppermute x4, starting transfers between devices, move_by(): lax.ppermute(array, 'wide', [(i, (i + shift) % n_wide) for i in range(n_w...  9.28 us
    pallas_call x4, Pallas kernels, sums_of(): pl.pallas_call(functools.partial(combine_kernel, jobs, members, boxes, so...  6.92 us
    ppermute x6, starting transfers between devices, swap_with(): return lax.ppermute(array, 'wide', [(i, i ^ step) for i in range(n_wide)])  6.07 us
    ppermute x2, starting transfers between devices, other_half(): return lax.ppermute(array, ('wide', 'narrow'), pairs)  3.48 us
    ppermute x6, waiting for transfers between devices, swap_with(): return lax.ppermute(array, 'wide', [(i, i ^ step) for i in range(n_wide)])  2.75 us
    ppermute x4, waiting for transfers between devices, move_by(): lax.ppermute(array, 'wide', [(i, (i + shift) % n_wide) for i in range(n_w...  2.61 us
    pallas_call x1, Pallas kernels, grouped(): pl.pallas_call(functools.partial(finish_ahead_kernel, ahead, top, early_c...  1.95 us
    pallas_call x1, Pallas kernels, grouped(): pl.pallas_call(functools.partial(finish_kernel, steps, members, boxes, so...  1.57 us
  transfers between devices with their start and end apart: 12, of which 4 were waited for; matrix products, arithmetic and copies ran while one was open for 3% of the time, Pallas kernels for 30%

profile of v8, /device:TPU:0, one launch (start us, length us, event | category | flops | bytes accessed | tf_op | source)
XLA Modules:
  0.0 40.2 jit_solution(7676676253698994894)
XLA Ops:
  0.6 0.5 %collective-permute-start = (bf16[2,2,32,8192]{3,2,1,0:T(8,128)(2,1)}, bf16[2,2,32,8192]{3,2,1,0:T(8,128)(2,1)S(1)}, u32[]{:S(2)}, u32[]{:S(2)}) collective-permute-start(bf16[2,2,32,8192]{3,2,1,0:T(8,128)(2,1)} %refs_0_.6), channel_id=1, source_target_pairs={{0,2},{2,0},{4,6},{6,4},{8,10},{10,8},{12,14},{14,12},{16,18},{18,... | collective-permute-start | bytes 6291464 | tf_op jit(solution)/shard_map/ppermute | solution.py:597
  1.1 0.0 copy-start.3
  1.2 0.0 copy-start.4
  1.2 0.0 copy-start.5
  1.2 1.0 %constant_dynamic-slice_fusion = (bf16[2,2,32,512]{3,2,1,0:T(8,128)(2,1)S(1)}, bf16[2,2,32,512]{3,2,1,0:T(8,128)(2,1)S(1)}) fusion(bf16[2,2,32,8192]{3,2,1,0:T(8,128)(2,1)} %refs_0_.6, s32[]{:T(128)S(6)} %select_n.7, s32[]{:T(128)S(6)} %select_n.6), kind=kLoop, calls=%fused_computation | loop fusion | bytes 524296 | tf_op jit(solution)/shard_map/dynamic_slice | solution.py:611
  2.2 2.7 %collective-permute-start.2 = (bf16[2,2,32,512]{3,2,1,0:T(8,128)(2,1)S(1)}, bf16[2,2,32,512]{3,2,1,0:T(8,128)(2,1)S(1)}, u32[]{:S(2)}, u32[]{:S(2)}) collective-permute-start(bf16[2,2,32,512]{3,2,1,0:T(8,128)(2,1)S(1)} %get-tuple-element.60), channel_id=1, source_target_pairs={{0,6},{2,4},{4,2},{6,0},{8,14},{10,12},{12,10},{14,8},{16,22},{18,... | collective-permute-start | bytes 393224 | tf_op jit(solution)/shard_map/ppermute | solution.py:597
  4.9 0.0 collective-permute-start.1
  4.9 0.2 axes.1
  5.1 0.0 copy-start
  5.1 0.0 copy-done.3
  5.2 0.0 copy-done.4
  5.2 0.0 copy-done.5
  5.2 0.0 copy-done.6
  5.2 1.0 %prep.1 = (f32[4,8,16,128]{3,2,1,0:T(8,128)S(1)}, f32[4,8,16,128]{3,2,1,0:T(8,128)S(1)}, f32[4,16,128]{2,1,0:T(8,128)S(1)}, f32[4,16,128]{2,1,0:T(8,128)S(1)}, f32[4,16,128]{2,1,0:T(8,128)S(1)}) custom-call(s32[32]{0:T(128)S(1)} %copy-done.3, s32[32]{0:T(128)S(1)} %copy-done.6, f32[4,3]{1,0:T(4,128)S(1)} %copy-done.5, s32[512,128]{1,0:T(8,128)S(1)} %bitcast.3, ...), custom_call_target="tpu_custom_call" | custom-call | flops 1000000000 | bytes 3600001 | tf_op jit(solution)/shard_map/prep/pallas_call | solution.py:627
  6.2 0.0 copy-start.1
  6.2 0.0 copy-start.2
  6.2 0.0 collective-permute-done.near.refs_1_
  6.2 0.5 %copy-done = bf16[2,2,32,8192]{3,2,1,0:T(8,128)(2,1)S(1)} copy-done((bf16[2,2,32,8192]{3,2,1,0:T(8,128)(2,1)S(1)}, bf16[2,2,32,8192]{3,2,1,0:T(8,128)(2,1)}, u32[]{:S(2)}) %copy-start) | copy-done | bytes 2097176
  6.7 0.5 %pack.1 = (bf16[1088,128]{1,0:T(8,128)(2,1)S(1)}, bf16[1056,128]{1,0:T(8,128)(2,1)S(1)}, bf16[1056,128]{1,0:T(8,128)(2,1)S(1)}, bf16[32,128]{1,0:T(8,128)(2,1)S(1)}) custom-call(bf16[2,2,32,8192]{3,2,1,0:T(8,128)(2,1)S(1)} %copy-done, bf16[2,2,32,8192]{3,2,1,0:T(8,128)(2,1)S(1)} %collective-permute-done.near.refs_1_), custom_call_target="tpu_custom_call" | custom-call | flops 1000000000 | bytes 3600001 | tf_op jit(solution)/shard_map/pack/pallas_call | solution.py:646
  7.2 2.9 %collective-permute-start.5 = (bf16[32,128]{1,0:T(8,128)(2,1)S(1)}, bf16[32,128]{1,0:T(8,128)(2,1)S(1)}, u32[]{:S(2)}, u32[]{:S(2)}) collective-permute-start(bf16[32,128]{1,0:T(8,128)(2,1)S(1)} %get-tuple-element.38), channel_id=1, source_target_pairs={{0,5},{1,4},{2,7},{3,6},{4,1},{5,0},{6,3},{7,2},{8,13},{9,12},{10,... | collective-permute-start | bytes 24584 | tf_op jit(solution)/shard_map/ppermute | solution.py:617
  10.2 0.5 %collective-permute-start.4 = (bf16[32,128]{1,0:T(8,128)(2,1)S(1)}, bf16[32,128]{1,0:T(8,128)(2,1)S(1)}, u32[]{:S(2)}, u32[]{:S(2)}) collective-permute-start(bf16[32,128]{1,0:T(8,128)(2,1)S(1)} %get-tuple-element.38), channel_id=1, source_target_pairs={{0,1},{1,0},{2,3},{3,2},{4,5},{5,4},{6,7},{7,6},{8,9},{9,8},{10,11... | collective-permute-start | bytes 24584 | tf_op jit(solution)/shard_map/ppermute | solution.py:617
  10.7 0.1 collective-permute-start.7
  10.8 0.0 collective-permute-done.2.refs_3_.refs_6_
  10.8 1.2 %collective-permute-done.1.refs_2_.refs_5_ = bf16[2,2,32,512]{3,2,1,0:T(8,128)(2,1)S(1)} collective-permute-done((bf16[2,2,32,512]{3,2,1,0:T(8,128)(2,1)S(1)}, bf16[2,2,32,512]{3,2,1,0:T(8,128)(2,1)S(1)}, u32[]{:S(2)}, u32[]{:S(2)}) %collective-permute-start.1) | collective-permute-done | bytes 131104 | tf_op jit(solution)/shard_map/ppermute | solution.py:597
  11.9 0.0 copy-done.1
  11.9 0.0 copy-done.2
  11.9 1.0 %combine.4 = bf16[768,128]{1,0:T(8,128)(2,1)S(1)} custom-call(bf16[2,2,32,8192]{3,2,1,0:T(8,128)(2,1)S(1)} %copy-done, bf16[2,2,32,8192]{3,2,1,0:T(8,128)(2,1)S(1)} %collective-permute-done.near.refs_1_, bf16[2,2,32,512]{3,2,1,0:T(8,128)(2,1)S(1)} %collective-permute-done.1.refs_2_.refs_5_, ...), custom_call_target="tpu_custom_call" | custom-call | flops 5000000000 | bytes 18000000 | tf_op jit(solution)/shard_map/combine/pallas_call | solution.py:666
  13.0 2.7 %collective-permute-start.10 = (bf16[768,128]{1,0:T(8,128)(2,1)S(1)}, bf16[768,128]{1,0:T(8,128)(2,1)S(1)}, u32[]{:S(2)}, u32[]{:S(2)}) collective-permute-start(bf16[768,128]{1,0:T(8,128)(2,1)S(1)} %combine.4), channel_id=1, source_target_pairs={{0,16},{2,18},{4,20},{6,22},{8,24},{10,26},{12,28},{14,30},{16,0},... | collective-permute-start | bytes 589832 | tf_op jit(solution)/shard_map/ppermute | solution.py:601
  15.7 2.0 %collective-permute-start.3 = (bf16[1056,128]{1,0:T(8,128)(2,1)S(1)}, bf16[1056,128]{1,0:T(8,128)(2,1)S(1)}, u32[]{:S(2)}, u32[]{:S(2)}) collective-permute-start(bf16[1056,128]{1,0:T(8,128)(2,1)S(1)} %get-tuple-element.37), channel_id=1, source_target_pairs={{0,4},{2,6},{4,0},{6,2},{8,12},{10,14},{12,8},{14,10},{16,20},{18,... | collective-permute-start | bytes 811016 | tf_op jit(solution)/shard_map/ppermute | solution.py:597
  17.8 0.0 collective-permute-done.5.refs_4_
  17.8 0.0 collective-permute-done.4.refs_3_
  17.8 1.6 %collective-permute-done.7.refs_2_ = bf16[1088,128]{1,0:T(8,128)(2,1)S(1)} collective-permute-done((bf16[1088,128]{1,0:T(8,128)(2,1)S(1)}, bf16[1088,128]{1,0:T(8,128)(2,1)S(1)}, u32[]{:S(2)}, u32[]{:S(2)}) %collective-permute-start.7) | collective-permute-done | bytes 278560 | tf_op jit(solution)/shard_map/ppermute | solution.py:597
  19.4 2.2 %combine.6 = (bf16[1024,128]{1,0:T(8,128)(2,1)S(1)}, bf16[256,128]{1,0:T(8,128)(2,1)S(1)}) custom-call(bf16[2,2,32,8192]{3,2,1,0:T(8,128)(2,1)S(1)} %copy-done, bf16[2,2,32,8192]{3,2,1,0:T(8,128)(2,1)S(1)} %collective-permute-done.near.refs_1_, bf16[1088,128]{1,0:T(8,128)(2,1)S(1)} %collective-permute-done.7.refs_2_, ...), custom_call_target="tpu_custom_call" | custom-call | flops 30000001024 | bytes 108000000 | tf_op jit(solution)/shard_map/combine/pallas_call | solution.py:666
  21.6 0.7 %collective-permute-start.11 = (bf16[1056,128]{1,0:T(8,128)(2,1)S(1)}, bf16[1056,128]{1,0:T(8,128)(2,1)S(1)}, u32[]{:S(2)}, u32[]{:S(2)}) collective-permute-start(bf16[1056,128]{1,0:T(8,128)(2,1)S(1)} %get-tuple-element.49), channel_id=1, source_target_pairs={{0,4},{2,6},{4,0},{6,2},{8,12},{10,14},{12,8},{14,10},{16,20},{18,... | collective-permute-start | bytes 811016 | tf_op jit(solution)/shard_map/ppermute | solution.py:597
  22.3 1.6 %collective-permute-start.8 = (bf16[1024,128]{1,0:T(8,128)(2,1)S(1)}, bf16[1024,128]{1,0:T(8,128)(2,1)S(1)}, u32[]{:S(2)}, u32[]{:S(2)}) collective-permute-start(bf16[1024,128]{1,0:T(8,128)(2,1)S(1)} %get-tuple-element.45), channel_id=1, source_target_pairs={{0,8},{2,10},{4,12},{6,14},{8,16},{10,18},{12,20},{14,22},{16,24},... | collective-permute-start | bytes 786440 | tf_op jit(solution)/shard_map/ppermute | solution.py:601
  23.9 0.9 %collective-permute-done.10.refs_1_ = bf16[768,128]{1,0:T(8,128)(2,1)S(1)} collective-permute-done((bf16[768,128]{1,0:T(8,128)(2,1)S(1)}, bf16[768,128]{1,0:T(8,128)(2,1)S(1)}, u32[]{:S(2)}, u32[]{:S(2)}) %collective-permute-start.10) | collective-permute-done | bytes 196640 | tf_op jit(solution)/shard_map/ppermute | solution.py:601
  24.8 2.5 %collective-permute-start.9 = (bf16[256,128]{1,0:T(8,128)(2,1)S(1)}, bf16[256,128]{1,0:T(8,128)(2,1)S(1)}, u32[]{:S(2)}, u32[]{:S(2)}) collective-permute-start(bf16[256,128]{1,0:T(8,128)(2,1)S(1)} %get-tuple-element.46), channel_id=1, source_target_pairs={{0,16},{2,18},{4,20},{6,22},{8,24},{10,26},{12,28},{14,30},{16,0},... | collective-permute-start | bytes 196616 | tf_op jit(solution)/shard_map/ppermute | solution.py:601
  27.3 0.0 collective-permute-done.3.refs_2_
  27.3 1.8 %combine.5 = bf16[1024,128]{1,0:T(8,128)(2,1)S(1)} custom-call(bf16[2,2,32,8192]{3,2,1,0:T(8,128)(2,1)S(1)} %copy-done, bf16[2,2,32,8192]{3,2,1,0:T(8,128)(2,1)S(1)} %collective-permute-done.near.refs_1_, bf16[1056,128]{1,0:T(8,128)(2,1)S(1)} %collective-permute-done.3.refs_2_, bf16[32,128]{1,0:T(8,128)(2,1)S(1)} %collective-permute-done.4.refs_3_, ...), custom_call_target="tpu_custom_call" | custom-call | flops 2000000000 | bytes 7200001 | tf_op jit(solution)/shard_map/combine/pallas_call | solution.py:666
  29.1 2.5 %collective-permute-start.6 = (bf16[1024,128]{1,0:T(8,128)(2,1)S(1)}, bf16[1024,128]{1,0:T(8,128)(2,1)S(1)}, u32[]{:S(2)}, u32[]{:S(2)}) collective-permute-start(bf16[1024,128]{1,0:T(8,128)(2,1)S(1)} %combine.5), channel_id=1, source_target_pairs={{0,24},{2,26},{4,28},{6,30},{8,0},{10,2},{12,4},{14,6},{16,8},{18,... | collective-permute-start | bytes 786440 | tf_op jit(solution)/shard_map/ppermute | solution.py:601
  31.6 0.0 collective-permute-done.11.refs_2_
  31.6 1.8 %combine.7.refs_0_ = f32[1024,128]{1,0:T(8,128)S(1)} custom-call(bf16[2,2,32,8192]{3,2,1,0:T(8,128)(2,1)S(1)} %copy-done, bf16[2,2,32,8192]{3,2,1,0:T(8,128)(2,1)S(1)} %collective-permute-done.near.refs_1_, bf16[1056,128]{1,0:T(8,128)(2,1)S(1)} %collective-permute-done.11.refs_2_, bf16[32,128]{1,0:T(8,128)(2,1)S(1)} %collective-permute-done.4.refs_3_, ...), custom_call_target="tpu_custom_call" | custom-call | bytes 1 | tf_op jit(solution)/shard_map/combine/pallas_call | solution.py:666
  33.4 1.9 %finish_ahead.1 = (f32[4,2,512,128]{3,2,1,0:T(8,128)}, f32[2,512,128]{2,1,0:T(8,128)S(1)}, f32[2,512,128]{2,1,0:T(8,128)S(1)}) custom-call(s32[32]{0:T(128)S(1)} %copy-done.3, f32[1024,128]{1,0:T(8,128)S(1)} %combine.7.refs_0_, bf16[768,128]{1,0:T(8,128)(2,1)S(1)} %collective-permute-done.10.refs_1_, ...), custom_call_target="tpu_custom_call" | custom-call | bytes 1 | tf_op jit(solution)/shard_map/finish_ahead/pallas_call | solution.py:723
  35.4 0.0 collective-permute-done.9.refs_1_
  35.4 0.0 collective-permute-done.8.refs_0_
  35.4 1.5 %join.1 = (f32[4,2,512,128]{3,2,1,0:T(8,128)}, f32[2,512,128]{2,1,0:T(8,128)S(1)}) custom-call(s32[32]{0:T(128)S(1)} %copy-done.3, bf16[1024,128]{1,0:T(8,128)(2,1)S(1)} %collective-permute-done.8.refs_0_, bf16[256,128]{1,0:T(8,128)(2,1)S(1)} %collective-permute-done.9.refs_1_, ...), custom_call_target="tpu_custom_call", output_to_operand_aliasing={{0}: (7, {})} | custom-call | flops 5000000000 | bytes 18000000 | tf_op jit(solution)/shard_map/join/pallas_call | solution.py:733
  36.9 1.7 %collective-permute-done.6.refs_0_ = bf16[1024,128]{1,0:T(8,128)(2,1)S(1)} collective-permute-done((bf16[1024,128]{1,0:T(8,128)(2,1)S(1)}, bf16[1024,128]{1,0:T(8,128)(2,1)S(1)}, u32[]{:S(2)}, u32[]{:S(2)}) %collective-permute-start.6) | collective-permute-done | bytes 262176 | tf_op jit(solution)/shard_map/ppermute | solution.py:601
  38.6 1.6 %finish_last.1 = (f32[4,2,512,128]{3,2,1,0:T(8,128)}, f32[2,512,128]{2,1,0:T(8,128)}) custom-call(s32[32]{0:T(128)S(1)} %copy-done.3, bf16[1024,128]{1,0:T(8,128)(2,1)S(1)} %collective-permute-done.6.refs_0_, f32[4,16,128]{2,1,0:T(8,128)S(1)} %get-tuple-element.39.refs_2_.refs_3_.refs_1_, ...), custom_call_target="tpu_custom_call", output_to_operand_aliasing={{0}: (5, {})} | custom-call | flops 30000001024 | bytes 108000000 | tf_op jit(solution)/shard_map/finish_last/pallas_call | solution.py:754
  (1 shorter events, 0.0 us)
Async XLA Ops:
  0.6 5.6 %collective-permute-start = (bf16[2,2,32,8192]{3,2,1,0:T(8,128)(2,1)}, bf16[2,2,32,8192]{3,2,1,0:T(8,128)(2,1)S(1)}, u32[]{:S(2)}, u32[]{:S(2)}) collective-permute-start(bf16[2,2,32,8192]{3,2,1,0:T(8,128)(2,1)} %refs_0_.6), channel_id=1, source_target_pairs={{0,2},{2,0},{4,6},{6,4},{8,10},{10,8},{12,14},{14,12},{16,18},{18,... | collective-permute-start | bytes 6291464 | tf_op jit(solution)/shard_map/ppermute | solution.py:597
  1.1 4.0 %copy-start.3 = (s32[32]{0:T(128)S(1)}, s32[32]{0:T(128)}, u32[]{:S(2)}) copy-start(s32[32]{0:T(128)} %parent_of.7) | copy-start | bytes 388
  1.2 4.0 %copy-start.4 = (s32[65536]{0:T(1024)S(1)}, s32[65536]{0:T(1024)}, u32[]{:S(2)}) copy-start(s32[65536]{0:T(1024)} %param.17) | copy-start | bytes 786436
  1.2 4.0 %copy-start.5 = (f32[4,3]{1,0:T(4,128)S(1)}, f32[4,3]{1,0:T(4,128)}, u32[]{:S(2)}) copy-start(f32[4,3]{1,0:T(4,128)} %center.1) | copy-start | bytes 148
  1.2 4.0 %copy-start.6 = (s32[32]{0:T(128)S(1)}, s32[32]{0:T(128)}, u32[]{:S(2)}) copy-start(s32[32]{0:T(128)} %octant_of.1) | copy-start | bytes 388
  2.2 8.6 %collective-permute-start.2 = (bf16[2,2,32,512]{3,2,1,0:T(8,128)(2,1)S(1)}, bf16[2,2,32,512]{3,2,1,0:T(8,128)(2,1)S(1)}, u32[]{:S(2)}, u32[]{:S(2)}) collective-permute-start(bf16[2,2,32,512]{3,2,1,0:T(8,128)(2,1)S(1)} %get-tuple-element.60), channel_id=1, source_target_pairs={{0,6},{2,4},{4,2},{6,0},{8,14},{10,12},{12,10},{14,8},{16,22},{18,... | collective-permute-start | bytes 393224 | tf_op jit(solution)/shard_map/ppermute | solution.py:597
  4.9 7.0 %collective-permute-start.1 = (bf16[2,2,32,512]{3,2,1,0:T(8,128)(2,1)S(1)}, bf16[2,2,32,512]{3,2,1,0:T(8,128)(2,1)S(1)}, u32[]{:S(2)}, u32[]{:S(2)}) collective-permute-start(bf16[2,2,32,512]{3,2,1,0:T(8,128)(2,1)S(1)} %get-tuple-element.61), channel_id=1, source_target_pairs={{0,4},{2,6},{4,0},{6,2},{8,12},{10,14},{12,8},{14,10},{16,20},{18,... | collective-permute-start | bytes 393224 | tf_op jit(solution)/shard_map/ppermute | solution.py:597
  5.1 1.6 %copy-start = (bf16[2,2,32,8192]{3,2,1,0:T(8,128)(2,1)S(1)}, bf16[2,2,32,8192]{3,2,1,0:T(8,128)(2,1)}, u32[]{:S(2)}) copy-start(bf16[2,2,32,8192]{3,2,1,0:T(8,128)(2,1)} %refs_0_.6) | copy-start | bytes 6291460
  6.2 5.8 %copy-start.1 = (bf16[256,256]{1,0:T(8,128)(2,1)S(1)}, bf16[256,256]{1,0:T(8,128)(2,1)}, u32[]{:S(2)}) copy-start(bf16[256,256]{1,0:T(8,128)(2,1)} %constant.21.clone.refs_8_.refs_9_.refs_11_) | copy-start | bytes 393220
  6.2 5.8 %copy-start.2 = (bf16[256,256]{1,0:T(8,128)(2,1)S(1)}, bf16[256,256]{1,0:T(8,128)(2,1)}, u32[]{:S(2)}) copy-start(bf16[256,256]{1,0:T(8,128)(2,1)} %constant.20.clone.refs_7_.refs_8_.refs_10_) | copy-start | bytes 393220
  7.2 10.5 %collective-permute-start.5 = (bf16[32,128]{1,0:T(8,128)(2,1)S(1)}, bf16[32,128]{1,0:T(8,128)(2,1)S(1)}, u32[]{:S(2)}, u32[]{:S(2)}) collective-permute-start(bf16[32,128]{1,0:T(8,128)(2,1)S(1)} %get-tuple-element.38), channel_id=1, source_target_pairs={{0,5},{1,4},{2,7},{3,6},{4,1},{5,0},{6,3},{7,2},{8,13},{9,12},{10,... | collective-permute-start | bytes 24584 | tf_op jit(solution)/shard_map/ppermute | solution.py:617
  10.2 7.6 %collective-permute-start.4 = (bf16[32,128]{1,0:T(8,128)(2,1)S(1)}, bf16[32,128]{1,0:T(8,128)(2,1)S(1)}, u32[]{:S(2)}, u32[]{:S(2)}) collective-permute-start(bf16[32,128]{1,0:T(8,128)(2,1)S(1)} %get-tuple-element.38), channel_id=1, source_target_pairs={{0,1},{1,0},{2,3},{3,2},{4,5},{5,4},{6,7},{7,6},{8,9},{9,8},{10,11... | collective-permute-start | bytes 24584 | tf_op jit(solution)/shard_map/ppermute | solution.py:617
  10.7 8.6 %collective-permute-start.7 = (bf16[1088,128]{1,0:T(8,128)(2,1)S(1)}, bf16[1088,128]{1,0:T(8,128)(2,1)S(1)}, u32[]{:S(2)}, u32[]{:S(2)}) collective-permute-start(bf16[1088,128]{1,0:T(8,128)(2,1)S(1)} %get-tuple-element.42), channel_id=1, source_target_pairs={{0,4},{2,6},{4,0},{6,2},{8,12},{10,14},{12,8},{14,10},{16,20},{18,... | collective-permute-start | bytes 835592 | tf_op jit(solution)/shard_map/ppermute | solution.py:597
  13.0 11.8 %collective-permute-start.10 = (bf16[768,128]{1,0:T(8,128)(2,1)S(1)}, bf16[768,128]{1,0:T(8,128)(2,1)S(1)}, u32[]{:S(2)}, u32[]{:S(2)}) collective-permute-start(bf16[768,128]{1,0:T(8,128)(2,1)S(1)} %combine.4), channel_id=1, source_target_pairs={{0,16},{2,18},{4,20},{6,22},{8,24},{10,26},{12,28},{14,30},{16,0},... | collective-permute-start | bytes 589832 | tf_op jit(solution)/shard_map/ppermute | solution.py:601
  15.7 11.6 %collective-permute-start.3 = (bf16[1056,128]{1,0:T(8,128)(2,1)S(1)}, bf16[1056,128]{1,0:T(8,128)(2,1)S(1)}, u32[]{:S(2)}, u32[]{:S(2)}) collective-permute-start(bf16[1056,128]{1,0:T(8,128)(2,1)S(1)} %get-tuple-element.37), channel_id=1, source_target_pairs={{0,4},{2,6},{4,0},{6,2},{8,12},{10,14},{12,8},{14,10},{16,20},{18,... | collective-permute-start | bytes 811016 | tf_op jit(solution)/shard_map/ppermute | solution.py:597
  21.6 10.0 %collective-permute-start.11 = (bf16[1056,128]{1,0:T(8,128)(2,1)S(1)}, bf16[1056,128]{1,0:T(8,128)(2,1)S(1)}, u32[]{:S(2)}, u32[]{:S(2)}) collective-permute-start(bf16[1056,128]{1,0:T(8,128)(2,1)S(1)} %get-tuple-element.49), channel_id=1, source_target_pairs={{0,4},{2,6},{4,0},{6,2},{8,12},{10,14},{12,8},{14,10},{16,20},{18,... | collective-permute-start | bytes 811016 | tf_op jit(solution)/shard_map/ppermute | solution.py:597
  22.3 13.1 %collective-permute-start.8 = (bf16[1024,128]{1,0:T(8,128)(2,1)S(1)}, bf16[1024,128]{1,0:T(8,128)(2,1)S(1)}, u32[]{:S(2)}, u32[]{:S(2)}) collective-permute-start(bf16[1024,128]{1,0:T(8,128)(2,1)S(1)} %get-tuple-element.45), channel_id=1, source_target_pairs={{0,8},{2,10},{4,12},{6,14},{8,16},{10,18},{12,20},{14,22},{16,24},... | collective-permute-start | bytes 786440 | tf_op jit(solution)/shard_map/ppermute | solution.py:601
  24.8 10.6 %collective-permute-start.9 = (bf16[256,128]{1,0:T(8,128)(2,1)S(1)}, bf16[256,128]{1,0:T(8,128)(2,1)S(1)}, u32[]{:S(2)}, u32[]{:S(2)}) collective-permute-start(bf16[256,128]{1,0:T(8,128)(2,1)S(1)} %get-tuple-element.46), channel_id=1, source_target_pairs={{0,16},{2,18},{4,20},{6,22},{8,24},{10,26},{12,28},{14,30},{16,0},... | collective-permute-start | bytes 196616 | tf_op jit(solution)/shard_map/ppermute | solution.py:601
  29.1 9.5 %collective-permute-start.6 = (bf16[1024,128]{1,0:T(8,128)(2,1)S(1)}, bf16[1024,128]{1,0:T(8,128)(2,1)S(1)}, u32[]{:S(2)}, u32[]{:S(2)}) collective-permute-start(bf16[1024,128]{1,0:T(8,128)(2,1)S(1)} %combine.5), channel_id=1, source_target_pairs={{0,24},{2,26},{4,28},{6,30},{8,0},{10,2},{12,4},{14,6},{16,8},{18,... | collective-permute-start | bytes 786440 | tf_op jit(solution)/shard_map/ppermute | solution.py:601
